TPU v7x, 512 devices: a whole 4x4x16 slice. The times are simulated.
512 devices in a mesh: dp: 4 (over y), ctx: 4 (over x), expert: 32 (over z, core).
Axes of the slice: x: 4, y: 4, z: 16, core: 2. Of those that a mesh axis runs over, the one named last changes fastest.
Arguments:
- query_rows: bfloat16 [4, 4, 32, 256, 2048], P('dp', 'ctx', 'expert'), may hold values from -7 to 7
- key_rows: bfloat16 [4, 4, 32, 256, 256], P('dp', 'ctx', 'expert'), may hold values from -7 to 7
- value_rows: bfloat16 [4, 4, 32, 256, 256], P('dp', 'ctx', 'expert'), may hold values from -6 to 6
- output_grad: bfloat16 [4, 4, 32, 256, 2048], P('dp', 'ctx', 'expert'), may hold values from -6 to 6
- sink_logits: float32 [32], replicated, may hold values from -1 to 2
- parent_branch: int32 [4, 4, 32], P('dp', 'ctx', 'expert'), may hold values from 0 to 31, as said below
- segment_length: int32 [4, 4, 32], P('dp', 'ctx', 'expert'), may hold values from 128 to 256
Outputs:
- query_grad: bfloat16 [4, 4, 32, 256, 2048], P('dp', 'ctx', 'expert')
- key_grad: bfloat16 [4, 4, 32, 256, 256], P('dp', 'ctx', 'expert')
- value_grad: bfloat16 [4, 4, 32, 256, 256], P('dp', 'ctx', 'expert')
- sink_grad: float32 [32], replicated
Inputs may be any that keep to these rules, and one draw needn't show every extreme that they name: parent_branch[t, l, b] lies in b - 1 .. b + 1; entries of level 0 are not read.
All inputs are finite; a program needn't handle non-finite values.
Results may differ from a plain program's by a relative error of at most 0.0034.
The roundings to bfloat16 on the way count: a program that leaves them out, or rounds other values in their place, can miss the bound.
Values may be sent and summed in bfloat16 or wider, within the bound.
No kernel may reach another device: no remote copies, remote signals or barrier semaphores. Data moves between devices by JAX's collectives and lax.ppermute only.
A program may use at most 64 MiB of HBM per device.

v0:
```python
import jax
import jax.numpy as jnp
from jax import lax
from jax.sharding import PartitionSpec as P

HQ = 32
HK = 4
HD = 64
WIN = 128


def passed_along(shard, axis, by):
    peers = lax.axis_size(axis)
    pairs = [(i, i + by) for i in range(peers) if 0 <= i + by < peers]
    return lax.ppermute(shard, axis, pairs)


def padded(cells, sides, width):
    for axis, dim in sides:
        count = lax.axis_size(axis)
        ends = count - 1
        head = lax.slice_in_dim(cells, 0, width, axis=dim)
        tail = lax.slice_in_dim(cells, cells.shape[dim] - width, cells.shape[dim], axis=dim)
        cells = jnp.concatenate(
            [
                lax.ppermute(tail, axis, [(i, (i + 1) % count) for i in range(ends)]),
                cells,
                lax.ppermute(head, axis, [((i + 1) % count, i) for i in range(ends)]),
            ],
            axis=dim,
        )
    return cells


def attend_backward(
    query_rows,
    key_rows,
    value_rows,
    output_grad,
    tail_keys,
    tail_values,
    live_count,
    has_parent,
    sink_logits,
):
    tokens = query_rows.shape[0]
    tail_len = tail_keys.shape[0]
    group_size = HQ // HK
    score_scale = HD ** (-0.5)
    row_index = jnp.arange(tokens, dtype=jnp.int32)[:, None]
    col_index = jnp.arange(tail_len + tokens, dtype=jnp.int32)[None, :]
    own_col = col_index - tail_len
    in_tail = (col_index < tail_len) & (col_index >= row_index) & has_parent
    in_own = (col_index >= tail_len) & (own_col <= row_index) & (own_col > row_index - WIN)
    visible = (in_tail | in_own) & (row_index < live_count)
    all_keys = jnp.concatenate([tail_keys, key_rows], axis=0)
    all_values = jnp.concatenate([tail_values, value_rows], axis=0)
    query_parts, key_parts, value_parts, sink_parts = ([], [], [], [])
    for head_group in range(HK):
        first_col = head_group * group_size * HD
        last_col = first_col + group_size * HD
        grouped_q = query_rows[:, first_col:last_col].reshape(tokens, group_size, HD)
        grouped_d = output_grad[:, first_col:last_col].reshape(tokens, group_size, HD)
        group_keys = all_keys[:, head_group * HD : (head_group + 1) * HD]
        group_values = all_values[:, head_group * HD : (head_group + 1) * HD]
        group_sinks = sink_logits[head_group * group_size : (head_group + 1) * group_size]
        scores = (
            jnp.einsum("ihd,jd->hij", grouped_q, group_keys, preferred_element_type=jnp.float32)
            * score_scale
        )
        scores = jnp.where(visible[None], scores, -1e30)
        row_max = jnp.maximum(jnp.max(scores, axis=2), group_sinks[:, None])
        weights = jnp.exp(scores - row_max[:, :, None])
        sink_weight = jnp.exp(group_sinks[:, None] - row_max)
        denominator = jnp.sum(weights, axis=2) + sink_weight
        probabilities = weights / denominator[:, :, None]
        sink_prob = sink_weight / denominator
        probs_low = probabilities.astype(jnp.bfloat16)
        outputs = jnp.einsum(
            "hij,jd->hid", probs_low, group_values, preferred_element_type=jnp.float32
        )
        row_delta = jnp.sum(outputs * jnp.swapaxes(grouped_d, 0, 1).astype(jnp.float32), axis=2)
        dot_grad = jnp.einsum(
            "ihd,jd->hij", grouped_d, group_values, preferred_element_type=jnp.float32
        )
        score_grad = (probabilities * (dot_grad - row_delta[:, :, None])).astype(jnp.bfloat16)
        query_parts.append(
            (
                jnp.einsum(
                    "hij,jd->ihd", score_grad, group_keys, preferred_element_type=jnp.float32
                )
                * score_scale
            ).reshape(tokens, group_size * HD)
        )
        key_parts.append(
            jnp.einsum("hij,ihd->jd", score_grad, grouped_q, preferred_element_type=jnp.float32)
            * score_scale
        )
        value_parts.append(
            jnp.einsum("hij,ihd->jd", probs_low, grouped_d, preferred_element_type=jnp.float32)
        )
        sink_parts.append(-jnp.sum(sink_prob * row_delta, axis=1))
    query_grad = jnp.concatenate(query_parts, axis=1).astype(jnp.bfloat16)
    return (
        query_grad,
        jnp.concatenate(key_parts, axis=1),
        jnp.concatenate(value_parts, axis=1),
        jnp.concatenate(sink_parts, axis=0),
    )


def shards(
    query_rows, key_rows, value_rows, output_grad, sink_logits, parent_branch, segment_length
):
    tail_len = WIN - 1
    own_queries = query_rows[0, 0, 0]
    own_keys = key_rows[0, 0, 0]
    own_values = value_rows[0, 0, 0]
    own_grad = output_grad[0, 0, 0]
    live_count = segment_length[0, 0, 0]
    parent = parent_branch[0, 0, 0]
    branch = lax.axis_index("expert")
    level = lax.axis_index("ctx")
    tail_start = live_count - tail_len
    own_tail = jnp.stack(
        [
            lax.dynamic_slice_in_dim(own_keys, tail_start, tail_len, 0),
            lax.dynamic_slice_in_dim(own_values, tail_start, tail_len, 0),
        ]
    )
    shifted = passed_along(own_tail, "ctx", 1)
    neighbours = padded(shifted[None], (("expert", 0),), 1)
    slot_index = parent - branch + 1
    parent_tail = lax.dynamic_index_in_dim(neighbours, slot_index, 0, keepdims=False)
    has_parent = level > 0
    query_grad, key_all, value_all, sink_terms = attend_backward(
        own_queries,
        own_keys,
        own_values,
        own_grad,
        parent_tail[0],
        parent_tail[1],
        live_count,
        has_parent,
        sink_logits,
    )
    tail_grads = jnp.stack([key_all[:tail_len], value_all[:tail_len]]).astype(jnp.bfloat16)
    slot_mask = (jnp.arange(3, dtype=jnp.int32) == slot_index) & has_parent
    slot_flags = slot_mask.astype(jnp.bfloat16)
    raised, raised_flags = passed_along((tail_grads, slot_flags), "ctx", -1)
    spread, spread_flags = (
        padded(raised[None], (("expert", 0),), 1),
        padded(raised_flags[None], (("expert", 0),), 1),
    )
    places = jnp.arange(3, dtype=jnp.int32)
    pick_table = (places[None, :] == (2 - places)[:, None]).astype(jnp.float32)
    weights = jnp.sum(spread_flags.astype(jnp.float32) * pick_table, axis=1)
    incoming = (
        weights[0] * spread[0].astype(jnp.float32)
        + weights[1] * spread[1].astype(jnp.float32)
        + weights[2] * spread[2].astype(jnp.float32)
    )
    own_rows = jnp.stack([key_all[tail_len:], value_all[tail_len:]])
    placed = lax.dynamic_update_slice_in_dim(jnp.zeros_like(own_rows), incoming, tail_start, 1)
    total_rows = (own_rows + placed).astype(jnp.bfloat16)
    sink_grad = lax.psum(sink_terms, ("dp", "ctx", "expert"))
    return (
        query_grad[None, None, None],
        total_rows[0][None, None, None],
        total_rows[1][None, None, None],
        sink_grad,
    )


def solution(mesh):
    return jax.shard_map(
        shards,
        mesh=mesh,
        in_specs=(
            P("dp", "ctx", "expert", None, None),
            P("dp", "ctx", "expert", None, None),
            P("dp", "ctx", "expert", None, None),
            P("dp", "ctx", "expert", None, None),
            P(),
            P("dp", "ctx", "expert"),
            P("dp", "ctx", "expert"),
        ),
        out_specs=(
            P("dp", "ctx", "expert", None, None),
            P("dp", "ctx", "expert", None, None),
            P("dp", "ctx", "expert", None, None),
            P(),
        ),
        check_vma=False,
    )
```

profile of v0, /device:TPU:1, one launch (start us, length us, event | category | flops | bytes accessed | tf_op | source)
XLA Modules:
  0.0 184.2 jit_solution(15168091977733769732)
XLA Ops:
  1.4 1.3 collective-permute-start.3
  5.3 5.2 %collective-permute-start = (bf16[2,127,256]{1,2,0:T(8,128)(2,1)}, bf16[2,127,256]{1,2,0:T(8,128)(2,1)}, u32[]{:S(2)}, u32[]{:S(2)}) collective-permute-start(bf16[2,127,256]{1,2,0:T(8,128)(2,1)} %pad_maximum_fusion.4), channel_id=1, source_target_pairs={{0,32},{32,64},{64,96},{1,33},{33,65},{65,97},{2,34},{34,66},{66,9... | collective-permute-start | bytes 390152 | tf_op jit(solution)/shard_map/ppermute | solution.py:15
  10.5 1.3 fusion.106
  12.3 1.0 copy.15
  14.5 8.8 %collective-permute-start.5 = (bf16[1,3]{1,0:T(2,128)(2,1)S(1)}, bf16[1,3]{1,0:T(2,128)(2,1)S(1)}, u32[]{:S(2)}, u32[]{:S(2)}) collective-permute-start(bf16[1,3]{1,0:T(2,128)(2,1)S(1)} %bitcast.286), channel_id=1, source_target_pairs={{1,0},{2,1},{3,2},{4,3},{5,4},{6,5},{7,6},{8,7},{9,8},{10,9},{11,1... | collective-permute-start | bytes 26 | tf_op jit(solution)/shard_map/ppermute | solution.py:28
  23.2 1.9 %collective-permute-start.4 = (bf16[1,3]{1,0:T(2,128)(2,1)S(1)}, bf16[1,3]{1,0:T(2,128)(2,1)S(1)}, u32[]{:S(2)}, u32[]{:S(2)}) collective-permute-start(bf16[1,3]{1,0:T(2,128)(2,1)S(1)} %bitcast.287), channel_id=1, source_target_pairs={{0,1},{1,2},{2,3},{3,4},{4,5},{5,6},{6,7},{7,8},{8,9},{9,10},{10,1... | collective-permute-start | bytes 26 | tf_op jit(solution)/shard_map/ppermute | solution.py:26
  25.2 2.4 %collective-permute-start.2 = (bf16[1,2,127,256]{2,3,1,0:T(8,128)(2,1)}, bf16[1,2,127,256]{2,3,1,0:T(8,128)(2,1)S(1)}, u32[]{:S(2)}, u32[]{:S(2)}) collective-permute-start(bf16[1,2,127,256]{2,3,1,0:T(8,128)(2,1)} %bitcast.3), channel_id=1, source_target_pairs={{1,0},{2,1},{3,2},{4,3},{5,4},{6,5},{7,6},{8,7},{9,8},{10,9},{11,1... | collective-permute-start | bytes 390152 | tf_op jit(solution)/shard_map/ppermute | solution.py:28
  27.6 3.2 %collective-permute-start.1 = (bf16[1,2,127,256]{2,3,1,0:T(8,128)(2,1)}, bf16[1,2,127,256]{2,3,1,0:T(8,128)(2,1)S(1)}, u32[]{:S(2)}, u32[]{:S(2)}) collective-permute-start(bf16[1,2,127,256]{2,3,1,0:T(8,128)(2,1)} %bitcast.3), channel_id=1, source_target_pairs={{0,1},{1,2},{2,3},{3,4},{4,5},{5,6},{6,7},{7,8},{8,9},{9,10},{10,1... | collective-permute-start | bytes 390152 | tf_op jit(solution)/shard_map/ppermute | solution.py:26
  31.7 1.3 collective-permute-done.1
  35.3 2.2 %fusion.9 = (f32[8,256]{1,0:T(8,128)S(1)}, f32[8,256]{1,0:T(8,128)S(1)}, f32[8,256]{1,0:T(8,128)S(1)}, f32[8,256]{1,0:T(8,128)S(1)}, f32[383,256,8]{1,0,2:T(8,128)S(1)}) fusion(f32[383,256,8]{1,0,2:T(8,128)S(1)} %get-tuple-element.35, f32[8,256]{1,0:T(8,128)S(1)} %broadcast_maximum_fusion.3, pred[256,383]{0,1:T(8,128)(4,1)S(1)} %fusion.43, ...), kind=kOutput, calls=%fused_computation.21 | convolution fusion | flops 110688000 | bytes 13147392 | tf_op jit(solution)/shard_map/ihd,jd->hij/dot_general | solution.py:68
  37.7 2.1 %fusion.11 = (f32[8,256]{1,0:T(8,128)S(1)}, f32[8,256]{1,0:T(8,128)S(1)}, f32[8,256]{1,0:T(8,128)S(1)}) fusion(f32[383,256,8]{1,0,2:T(8,128)S(1)} %get-tuple-element.36, f32[8,256]{1,0:T(8,128)S(1)} %broadcast_maximum_fusion.2, pred[256,383]{0,1:T(8,128)(4,1)S(1)} %fusion.43, f32[8,256]{1,0:T(8,128)S(1)} %broadcast_maximum_fusion.1, ...), kind=kLoop, calls=%fused_computation.23 | loop fusion | flops 9406464 | bytes 9559808 | tf_op jit(solution)/shard_map/reduce_sum | solution.py:75
  42.1 1.2 fusion.1
  45.4 1.0 convolution_bitcast_fusion.1
  46.5 1.2 fusion.3
  50.9 1.2 fusion.5
  55.4 1.4 fusion.7
  58.7 1.3 collective-permute-start.6
  60.0 1.1 pad_maximum_fusion
  61.5 3.9 %collective-permute-done.6 = bf16[2,127,256]{1,2,0:T(8,128)(2,1)S(1)} collective-permute-done((bf16[2,127,256]{1,2,0:T(8,128)(2,1)S(1)}, bf16[2,127,256]{1,2,0:T(8,128)(2,1)S(1)}, u32[]{:S(2)}, u32[]{:S(2)}) %collective-permute-start.6) | collective-permute-done | bytes 130080 | tf_op jit(solution)/shard_map/ppermute | solution.py:15
  65.4 2.2 %collective-permute-start.8 = (bf16[1,2,127,256]{2,3,1,0:T(8,128)(2,1)S(1)}, bf16[1,2,127,256]{2,3,1,0:T(8,128)(2,1)S(1)}, u32[]{:S(2)}, u32[]{:S(2)}) collective-permute-start(bf16[1,2,127,256]{2,3,1,0:T(8,128)(2,1)S(1)} %bitcast.284), channel_id=1, source_target_pairs={{1,0},{2,1},{3,2},{4,3},{5,4},{6,5},{7,6},{8,7},{9,8},{10,9},{11,1... | collective-permute-start | bytes 390152 | tf_op jit(solution)/shard_map/ppermute | solution.py:28
  67.6 4.1 %collective-permute-start.7 = (bf16[1,2,127,256]{2,3,1,0:T(8,128)(2,1)S(1)}, bf16[1,2,127,256]{2,3,1,0:T(8,128)(2,1)S(1)}, u32[]{:S(2)}, u32[]{:S(2)}) collective-permute-start(bf16[1,2,127,256]{2,3,1,0:T(8,128)(2,1)S(1)} %bitcast.285), channel_id=1, source_target_pairs={{0,1},{1,2},{2,3},{3,4},{4,5},{5,6},{6,7},{7,8},{8,9},{9,10},{10,1... | collective-permute-start | bytes 390152 | tf_op jit(solution)/shard_map/ppermute | solution.py:26
  71.9 107.7 %psum.7 = f32[32]{0:T(128)} all-reduce(f32[32]{0:T(128)S(1)} %pad_maximum_fusion.8), channel_id=1, replica_groups=mesh['dp'=4,'ctx'=4,'expert'=32] {'dp','ctx','expert'}, use_global_device_ids=true, to_apply=%region_17.18 | all-reduce | flops 32 | bytes 256 | tf_op jit(solution)/shard_map/psum | solution.py:166
  179.6 2.0 %fusion.47 = bf16[2,127,256]{1,2,0:T(8,128)(2,1)S(1)} fusion(s32[]{:T(128)S(6)} %select_n.22, f32[1,256,256]{1,2,0:T(8,128)S(1)} %slice_bitcast_fusion.1, f32[1,256,256]{1,2,0:T(8,128)S(1)} %slice_bitcast_fusion, bf16[1,2,127,256]{2,3,1,0:T(8,128)(2,1)S(1)} %collective-permute-done.8, bf16[2,127,256]{1,2,0:T(8,128)(2,1)S(1)} %collective-permute-done.6, ...), kind=kLoop, calls=%fused_computation.92 | loop fusion | flops 715264 | bytes 1044496 | tf_op jit(solution)/shard_map/dynamic_update_slice | solution.py:164
  181.6 1.0 add.78
  (91 shorter events, 21.5 us)
Async XLA Ops:
  0.6 11.6 %copy-start.1 = (bf16[1,1,1,256,256]{4,3,2,1,0:T(8,128)(2,1)S(1)}, bf16[1,1,1,256,256]{4,3,2,1,0:T(8,128)(2,1)}, u32[]{:S(2)}) copy-start(bf16[1,1,1,256,256]{4,3,2,1,0:T(8,128)(2,1)} %param.8) | copy-start | bytes 393220
  0.6 11.1 %copy-start = (bf16[1,1,1,256,2048]{4,3,2,1,0:T(8,128)(2,1)S(1)}, bf16[1,1,1,256,2048]{4,3,2,1,0:T(8,128)(2,1)}, u32[]{:S(2)}) copy-start(bf16[1,1,1,256,2048]{4,3,2,1,0:T(8,128)(2,1)} %param.10) | copy-start | bytes 3145732
  0.7 11.5 %copy-start.2 = (f32[32]{0:T(128)S(1)}, f32[32]{0:T(128)}, u32[]{:S(2)}) copy-start(f32[32]{0:T(128)} %param.11) | copy-start | bytes 388
  1.4 13.0 %collective-permute-start.3 = (bf16[3]{0:T(256)(128)(2,1)S(1)}, bf16[3]{0:T(256)(128)(2,1)S(1)}, u32[]{:S(2)}, u32[]{:S(2)}) collective-permute-start(bf16[3]{0:T(256)(128)(2,1)S(1)} %and_convert_fusion), channel_id=1, source_target_pairs={{32,0},{64,32},{96,64},{33,1},{65,33},{97,65},{34,2},{66,34},{98,6... | collective-permute-start | bytes 26 | tf_op jit(solution)/shard_map/ppermute | solution.py:15
  5.3 19.9 %collective-permute-start = (bf16[2,127,256]{1,2,0:T(8,128)(2,1)}, bf16[2,127,256]{1,2,0:T(8,128)(2,1)}, u32[]{:S(2)}, u32[]{:S(2)}) collective-permute-start(bf16[2,127,256]{1,2,0:T(8,128)(2,1)} %pad_maximum_fusion.4), channel_id=1, source_target_pairs={{0,32},{32,64},{64,96},{1,33},{33,65},{65,97},{2,34},{34,66},{66,9... | collective-permute-start | bytes 390152 | tf_op jit(solution)/shard_map/ppermute | solution.py:15
  14.5 16.3 %collective-permute-start.5 = (bf16[1,3]{1,0:T(2,128)(2,1)S(1)}, bf16[1,3]{1,0:T(2,128)(2,1)S(1)}, u32[]{:S(2)}, u32[]{:S(2)}) collective-permute-start(bf16[1,3]{1,0:T(2,128)(2,1)S(1)} %bitcast.286), channel_id=1, source_target_pairs={{1,0},{2,1},{3,2},{4,3},{5,4},{6,5},{7,6},{8,7},{9,8},{10,9},{11,1... | collective-permute-start | bytes 26 | tf_op jit(solution)/shard_map/ppermute | solution.py:28
  23.2 7.5 %collective-permute-start.4 = (bf16[1,3]{1,0:T(2,128)(2,1)S(1)}, bf16[1,3]{1,0:T(2,128)(2,1)S(1)}, u32[]{:S(2)}, u32[]{:S(2)}) collective-permute-start(bf16[1,3]{1,0:T(2,128)(2,1)S(1)} %bitcast.287), channel_id=1, source_target_pairs={{0,1},{1,2},{2,3},{3,4},{4,5},{5,6},{6,7},{7,8},{8,9},{9,10},{10,1... | collective-permute-start | bytes 26 | tf_op jit(solution)/shard_map/ppermute | solution.py:26
  25.2 6.5 %collective-permute-start.2 = (bf16[1,2,127,256]{2,3,1,0:T(8,128)(2,1)}, bf16[1,2,127,256]{2,3,1,0:T(8,128)(2,1)S(1)}, u32[]{:S(2)}, u32[]{:S(2)}) collective-permute-start(bf16[1,2,127,256]{2,3,1,0:T(8,128)(2,1)} %bitcast.3), channel_id=1, source_target_pairs={{1,0},{2,1},{3,2},{4,3},{5,4},{6,5},{7,6},{8,7},{9,8},{10,9},{11,1... | collective-permute-start | bytes 390152 | tf_op jit(solution)/shard_map/ppermute | solution.py:28
  27.6 5.4 %collective-permute-start.1 = (bf16[1,2,127,256]{2,3,1,0:T(8,128)(2,1)}, bf16[1,2,127,256]{2,3,1,0:T(8,128)(2,1)S(1)}, u32[]{:S(2)}, u32[]{:S(2)}) collective-permute-start(bf16[1,2,127,256]{2,3,1,0:T(8,128)(2,1)} %bitcast.3), channel_id=1, source_target_pairs={{0,1},{1,2},{2,3},{3,4},{4,5},{5,6},{6,7},{7,8},{8,9},{9,10},{10,1... | collective-permute-start | bytes 390152 | tf_op jit(solution)/shard_map/ppermute | solution.py:26
  58.7 6.7 %collective-permute-start.6 = (bf16[2,127,256]{1,2,0:T(8,128)(2,1)S(1)}, bf16[2,127,256]{1,2,0:T(8,128)(2,1)S(1)}, u32[]{:S(2)}, u32[]{:S(2)}) collective-permute-start(bf16[2,127,256]{1,2,0:T(8,128)(2,1)S(1)} %pad_maximum_fusion.5), channel_id=1, source_target_pairs={{32,0},{64,32},{96,64},{33,1},{65,33},{97,65},{34,2},{66,34},{98,6... | collective-permute-start | bytes 390152 | tf_op jit(solution)/shard_map/ppermute | solution.py:15
  65.4 114.2 %collective-permute-start.8 = (bf16[1,2,127,256]{2,3,1,0:T(8,128)(2,1)S(1)}, bf16[1,2,127,256]{2,3,1,0:T(8,128)(2,1)S(1)}, u32[]{:S(2)}, u32[]{:S(2)}) collective-permute-start(bf16[1,2,127,256]{2,3,1,0:T(8,128)(2,1)S(1)} %bitcast.284), channel_id=1, source_target_pairs={{1,0},{2,1},{3,2},{4,3},{5,4},{6,5},{7,6},{8,7},{9,8},{10,9},{11,1... | collective-permute-start | bytes 390152 | tf_op jit(solution)/shard_map/ppermute | solution.py:28
  67.6 112.0 %collective-permute-start.7 = (bf16[1,2,127,256]{2,3,1,0:T(8,128)(2,1)S(1)}, bf16[1,2,127,256]{2,3,1,0:T(8,128)(2,1)S(1)}, u32[]{:S(2)}, u32[]{:S(2)}) collective-permute-start(bf16[1,2,127,256]{2,3,1,0:T(8,128)(2,1)S(1)} %bitcast.285), channel_id=1, source_target_pairs={{0,1},{1,2},{2,3},{3,4},{4,5},{5,6},{6,7},{7,8},{8,9},{9,10},{10,1... | collective-permute-start | bytes 390152 | tf_op jit(solution)/shard_map/ppermute | solution.py:26
where the time goes:
time: 185 us; the launch traced here: 184 us
  blocking collectives  108 us (58%)
  starting transfers between devices  30.4 us (16%)
  matrix products  21.1 us (11%)
  local copies, waits for them, and re-layouts  8.82 us (5%)
  other arithmetic  8.2 us (4%)
  waiting for transfers between devices  5.41 us (3%)
  between operations  2.64 us (1%)
    psum x1, blocking collectives, shards(): sink_grad = lax.psum(sink_terms, ('dp', 'ctx', 'expert'))  108 us
    ppermute x3, starting transfers between devices, padded(): lax.ppermute(head, axis, [((i + 1) % count, i) for i in range(ends)])  13.4 us
    ppermute x3, starting transfers between devices, padded(): lax.ppermute(tail, axis, [(i, (i + 1) % count) for i in range(ends)])  9.22 us
    ppermute x3, starting transfers between devices, passed_along(): return lax.ppermute(shard, axis, pairs)  7.79 us
    dot_general x4, matrix products, attend_backward(): jnp.einsum('ihd,jd->hij', grouped_d, group_values, preferred_element_type...  5.06 us
    dot_general x4, matrix products, attend_backward(): jnp.einsum('ihd,jd->hij', grouped_q, group_keys, preferred_element_type=j...  4.21 us
    ppermute x3, waiting for transfers between devices, passed_along(): return lax.ppermute(shard, axis, pairs)  3.95 us
    dot_general x4, matrix products, attend_backward(): jnp.einsum('hij,ihd->jd', probs_low, grouped_d, preferred_element_type=jn...  3.9 us
  transfers between devices with their start and end apart: 9, of which 3 were waited for; matrix products, arithmetic and copies ran while one was open for 4% of the time, Pallas kernels for 0%

commit v1 on v0

--- a/solution.py
+++ b/solution.py
@@ -13,6 +13,14 @@
     peers = lax.axis_size(axis)
     pairs = [(i, i + by) for i in range(peers) if 0 <= i + by < peers]
     return lax.ppermute(shard, axis, pairs)
+
+
+def summed_over(terms, axes):
+    peers = 1
+    for axis in axes:
+        peers *= lax.axis_size(axis)
+    copies = jnp.broadcast_to(terms[None], (peers,) + terms.shape)
+    return jnp.sum(lax.all_to_all(copies, axes, 0, 0, tiled=True), axis=0)
 
 
 def padded(cells, sides, width):
@@ -163,7 +171,7 @@
     own_rows = jnp.stack([key_all[tail_len:], value_all[tail_len:]])
     placed = lax.dynamic_update_slice_in_dim(jnp.zeros_like(own_rows), incoming, tail_start, 1)
     total_rows = (own_rows + placed).astype(jnp.bfloat16)
-    sink_grad = lax.psum(sink_terms, ("dp", "ctx", "expert"))
+    sink_grad = summed_over(summed_over(sink_terms, ("dp", "ctx")), ("expert",))
     return (
         query_grad[None, None, None],
         total_rows[0][None, None, None],

time: 185 us -> 111 us (0.60)
  blocking collectives: 108 us -> 0 us
  starting transfers between devices: 30.4 us -> 50.3 us
  waiting for transfers between devices: 5.41 us -> 17.2 us
    psum x1 -> x0, blocking collectives: 108 us -> none  [shards(): sink_grad = lax.psum(sink_terms, ('dp', 'ctx', 'expert'))]
    all_to_all x0 -> x2, starting transfers between devices: none -> 19.9 us  [summed_over(): return jnp.sum(lax.all_to_all(copies, axes, 0, 0, tiled=True), axis=0)]
    all_to_all x0 -> x2, waiting for transfers between devices: none -> 11.7 us  [summed_over(): return jnp.sum(lax.all_to_all(copies, axes, 0, 0, tiled=True), axis=0)]
  transfers between devices with their start and end apart: 9 -> 11, of which waited for: 3 -> 4; matrix products, arithmetic and copies ran while one was open for 4% -> 9% of each run, Pallas kernels for 0% -> 0%
where the time goes in v1:
time: 111 us; the launch traced here: 110 us
  starting transfers between devices  50.3 us (45%)
  matrix products  21.1 us (19%)
  waiting for transfers between devices  17.2 us (15%)
  local copies, waits for them, and re-layouts  10.1 us (9%)
  other arithmetic  8.79 us (8%)
  between operations  2.66 us (2%)
    all_to_all x2, starting transfers between devices, summed_over(): return jnp.sum(lax.all_to_all(copies, axes, 0, 0, tiled=True), axis=0)  19.9 us
    ppermute x3, starting transfers between devices, padded(): lax.ppermute(head, axis, [((i + 1) % count, i) for i in range(ends)])  13.4 us
    all_to_all x2, waiting for transfers between devices, summed_over(): return jnp.sum(lax.all_to_all(copies, axes, 0, 0, tiled=True), axis=0)  11.7 us
    ppermute x3, starting transfers between devices, padded(): lax.ppermute(tail, axis, [(i, (i + 1) % count) for i in range(ends)])  9.22 us
    ppermute x3, starting transfers between devices, passed_along(): return lax.ppermute(shard, axis, pairs)  7.79 us
    dot_general x4, matrix products, attend_backward(): jnp.einsum('ihd,jd->hij', grouped_d, group_values, preferred_element_type...  5.09 us
    dot_general x4, matrix products, attend_backward(): jnp.einsum('ihd,jd->hij', grouped_q, group_keys, preferred_element_type=j...  4.21 us
    ppermute x3, waiting for transfers between devices, passed_along(): return lax.ppermute(shard, axis, pairs)  4.13 us
  transfers between devices with their start and end apart: 11, of which 4 were waited for; matrix products, arithmetic and copies ran while one was open for 9% of the time, Pallas kernels for 0%

profile of v1, /device:TPU:1, one launch (start us, length us, event | category | flops | bytes accessed | tf_op | source)
XLA Modules:
  0.0 110.2 jit_solution(11889677500330811800)
XLA Ops:
  1.4 1.3 %collective-permute-start.3 = (bf16[3]{0:T(256)(128)(2,1)S(1)}, bf16[3]{0:T(256)(128)(2,1)S(1)}, u32[]{:S(2)}, u32[]{:S(2)}) collective-permute-start(bf16[3]{0:T(256)(128)(2,1)S(1)} %and_convert_fusion), channel_id=1, source_target_pairs={{32,0},{64,32},{96,64},{33,1},{65,33},{97,65},{34,2},{66,34},{98,6... | collective-permute-start | bytes 26 | tf_op jit(solution)/shard_map/ppermute | solution.py:15
  5.3 5.2 %collective-permute-start = (bf16[2,127,256]{1,2,0:T(8,128)(2,1)}, bf16[2,127,256]{1,2,0:T(8,128)(2,1)}, u32[]{:S(2)}, u32[]{:S(2)}) collective-permute-start(bf16[2,127,256]{1,2,0:T(8,128)(2,1)} %pad_maximum_fusion.4), channel_id=1, source_target_pairs={{0,32},{32,64},{64,96},{1,33},{33,65},{65,97},{2,34},{34,66},{66,9... | collective-permute-start | bytes 390152 | tf_op jit(solution)/shard_map/ppermute | solution.py:15
  10.5 1.3 %fusion.106 = (bf16[256,512]{1,0:T(8,128)(2,1)S(1)}, bf16[256,512]{1,0:T(8,128)(2,1)S(1)}, bf16[256,512]{1,0:T(8,128)(2,1)S(1)}, bf16[256,512]{1,0:T(8,128)(2,1)S(1)}) fusion(bf16[256,2048]{1,0:T(8,128)(2,1)} %bitcast.258), kind=kLoop, calls=%fused_computation.175 | loop fusion | bytes 2097152 | tf_op jit(solution)/shard_map/slice | solution.py:70
  14.5 8.8 %collective-permute-start.5 = (bf16[1,3]{1,0:T(2,128)(2,1)S(1)}, bf16[1,3]{1,0:T(2,128)(2,1)S(1)}, u32[]{:S(2)}, u32[]{:S(2)}) collective-permute-start(bf16[1,3]{1,0:T(2,128)(2,1)S(1)} %bitcast.290), channel_id=1, source_target_pairs={{1,0},{2,1},{3,2},{4,3},{5,4},{6,5},{7,6},{8,7},{9,8},{10,9},{11,1... | collective-permute-start | bytes 26 | tf_op jit(solution)/shard_map/ppermute | solution.py:36
  23.2 1.9 %collective-permute-start.4 = (bf16[1,3]{1,0:T(2,128)(2,1)S(1)}, bf16[1,3]{1,0:T(2,128)(2,1)S(1)}, u32[]{:S(2)}, u32[]{:S(2)}) collective-permute-start(bf16[1,3]{1,0:T(2,128)(2,1)S(1)} %bitcast.291), channel_id=1, source_target_pairs={{0,1},{1,2},{2,3},{3,4},{4,5},{5,6},{6,7},{7,8},{8,9},{9,10},{10,1... | collective-permute-start | bytes 26 | tf_op jit(solution)/shard_map/ppermute | solution.py:34
  25.2 2.4 %collective-permute-start.2 = (bf16[1,2,127,256]{2,3,1,0:T(8,128)(2,1)}, bf16[1,2,127,256]{2,3,1,0:T(8,128)(2,1)S(1)}, u32[]{:S(2)}, u32[]{:S(2)}) collective-permute-start(bf16[1,2,127,256]{2,3,1,0:T(8,128)(2,1)} %bitcast.3), channel_id=1, source_target_pairs={{1,0},{2,1},{3,2},{4,3},{5,4},{6,5},{7,6},{8,7},{9,8},{10,9},{11,1... | collective-permute-start | bytes 390152 | tf_op jit(solution)/shard_map/ppermute | solution.py:36
  27.6 3.2 %collective-permute-start.1 = (bf16[1,2,127,256]{2,3,1,0:T(8,128)(2,1)}, bf16[1,2,127,256]{2,3,1,0:T(8,128)(2,1)S(1)}, u32[]{:S(2)}, u32[]{:S(2)}) collective-permute-start(bf16[1,2,127,256]{2,3,1,0:T(8,128)(2,1)} %bitcast.3), channel_id=1, source_target_pairs={{0,1},{1,2},{2,3},{3,4},{4,5},{5,6},{6,7},{7,8},{8,9},{9,10},{10,1... | collective-permute-start | bytes 390152 | tf_op jit(solution)/shard_map/ppermute | solution.py:34
  31.7 1.3 %collective-permute-done.1 = bf16[1,2,127,256]{2,3,1,0:T(8,128)(2,1)S(1)} collective-permute-done((bf16[1,2,127,256]{2,3,1,0:T(8,128)(2,1)}, bf16[1,2,127,256]{2,3,1,0:T(8,128)(2,1)S(1)}, u32[]{:S(2)}, u32[]{:S(2)}) %collective-permute-start.1) | collective-permute-done | bytes 130080 | tf_op jit(solution)/shard_map/ppermute | solution.py:34
  35.3 2.2 %fusion.9 = (f32[8,256]{1,0:T(8,128)S(1)}, f32[8,256]{1,0:T(8,128)S(1)}, f32[8,256]{1,0:T(8,128)S(1)}, f32[8,256]{1,0:T(8,128)S(1)}, f32[383,256,8]{1,0,2:T(8,128)S(1)}) fusion(f32[383,256,8]{1,0,2:T(8,128)S(1)} %get-tuple-element.43, f32[8,256]{1,0:T(8,128)S(1)} %broadcast_maximum_fusion.3, pred[256,383]{0,1:T(8,128)(4,1)S(1)} %fusion.43, ...), kind=kOutput, calls=%fused_computation.21 | convolution fusion | flops 110688000 | bytes 13147392 | tf_op jit(solution)/shard_map/ihd,jd->hij/dot_general | solution.py:76
  37.7 2.1 %fusion.11 = (f32[8,256]{1,0:T(8,128)S(1)}, f32[8,256]{1,0:T(8,128)S(1)}, f32[8,256]{1,0:T(8,128)S(1)}) fusion(f32[383,256,8]{1,0,2:T(8,128)S(1)} %get-tuple-element.44, f32[8,256]{1,0:T(8,128)S(1)} %broadcast_maximum_fusion.2, pred[256,383]{0,1:T(8,128)(4,1)S(1)} %fusion.43, f32[8,256]{1,0:T(8,128)S(1)} %broadcast_maximum_fusion.1, ...), kind=kLoop, calls=%fused_computation.23 | loop fusion | flops 9406464 | bytes 9559808 | tf_op jit(solution)/shard_map/reduce_sum | solution.py:83
  42.1 1.2 %fusion.1 = bf16[8,256,383]{1,2,0:T(8,128)(2,1)S(1)} fusion(bf16[383,64,1]{0,1,2:T(8,128)(2,1)S(1)} %fusion.64, bf16[256,8,64]{0,2,1:T(8,128)(2,1)S(1)} %bitcast.283, f32[8,256]{1,0:T(8,128)S(1)} %fusion.27, f32[8,256]{1,0:T(8,128)S(1)} %fusion.69, f32[8,256]{1,0:T(8,128)S(1)} %broadcast_maximum_fusion, f32[383,256,8]{1,0,2:T(8,128)S(1)} %fusion.109, ...), kind=kOutput, calls=%fused_computation.2 | convolution fusion | flops 105891840 | bytes 5140096 | tf_op jit(solution)/shard_map/ihd,jd->hij/dot_general | solution.py:91
  46.5 1.2 %fusion.3 = bf16[8,256,383]{1,2,0:T(8,128)(2,1)S(1)} fusion(bf16[256,8,64]{0,2,1:T(8,128)(2,1)S(1)} %bitcast.280, f32[8,256]{1,0:T(8,128)S(1)} %fusion.26, bf16[256,256]{0,1:T(8,128)(2,1)S(1)} %bitcast.267, bf16[127,256]{0,1:T(8,128)(2,1)S(1)} %get-tuple-element.33, f32[8,256]{1,0:T(8,128)S(1)} %fusion.68, f32[8,256]{1,0:T(8,128)S(1)} %broadcast_maximum_fusion.1, ...), kind=kOutput, calls=%fused_computation.6 | convolution fusion | flops 105989888 | bytes 5287168 | tf_op jit(solution)/shard_map/ihd,jd->hij/dot_general | solution.py:91
  51.1 1.2 %fusion.5 = bf16[8,256,383]{1,2,0:T(8,128)(2,1)S(1)} fusion(bf16[256,8,64]{0,2,1:T(8,128)(2,1)S(1)} %bitcast.277, f32[8,256]{1,0:T(8,128)S(1)} %fusion.25, bf16[256,256]{0,1:T(8,128)(2,1)S(1)} %bitcast.269, bf16[127,256]{0,1:T(8,128)(2,1)S(1)} %get-tuple-element.33, f32[8,256]{1,0:T(8,128)S(1)} %fusion.67, f32[8,256]{1,0:T(8,128)S(1)} %broadcast_maximum_fusion.2, ...), kind=kOutput, calls=%fused_computation.10 | convolution fusion | flops 105989888 | bytes 5287168 | tf_op jit(solution)/shard_map/ihd,jd->hij/dot_general | solution.py:91
  55.6 1.5 %fusion.7 = bf16[8,256,383]{1,2,0:T(8,128)(2,1)S(1)} fusion(bf16[256,8,64]{0,2,1:T(8,128)(2,1)S(1)} %bitcast.274, f32[8,256]{1,0:T(8,128)S(1)} %fusion.24, bf16[256,256]{0,1:T(8,128)(2,1)S(1)} %bitcast.271, bf16[127,256]{0,1:T(8,128)(2,1)S(1)} %get-tuple-element.33, f32[8,256]{1,0:T(8,128)S(1)} %fusion.66, f32[8,256]{1,0:T(8,128)S(1)} %broadcast_maximum_fusion.3, ...), kind=kOutput, calls=%fused_computation.14 | convolution fusion | flops 105989888 | bytes 5287168 | tf_op jit(solution)/shard_map/ihd,jd->hij/dot_general | solution.py:91
  58.8 3.5 %all-to-all-start = ((f32[16,1,32]{2,1,0:T(1,128)}), f32[16,1,32]{2,1,0:T(1,128)S(1)}, u32[]{:S(2)}, u32[]{:S(2)}) async-start(f32[16,1,32]{2,1,0:T(1,128)} %broadcast_in_dim.39), calls=%async_computation | async-start | bytes 16384 | tf_op jit(solution)/shard_map/all_to_all | solution.py:23
  63.0 1.3 %collective-permute-start.6 = (bf16[2,127,256]{1,2,0:T(8,128)(2,1)S(1)}, bf16[2,127,256]{1,2,0:T(8,128)(2,1)S(1)}, u32[]{:S(2)}, u32[]{:S(2)}) collective-permute-start(bf16[2,127,256]{1,2,0:T(8,128)(2,1)S(1)} %pad_maximum_fusion.5), channel_id=1, source_target_pairs={{32,0},{64,32},{96,64},{33,1},{65,33},{97,65},{34,2},{66,34},{98,6... | collective-permute-start | bytes 390152 | tf_op jit(solution)/shard_map/ppermute | solution.py:15
  64.3 1.1 %pad_maximum_fusion = bf16[1,1,1,256,2048]{4,3,2,1,0:T(8,128)(2,1)} fusion(bf16[1,1,1,256,512]{4,3,2,1,0:T(8,128)(2,1)S(1)} %copy.102, bf16[1,1,1,256,512]{4,3,2,1,0:T(8,128)(2,1)S(1)} %copy.101, bf16[1,1,1,256,512]{4,3,2,1,0:T(8,128)(2,1)S(1)} %copy.100, bf16[1,1,1,256,512]{4,3,2,1,0:T(8,128)(2,1)S(1)} %copy.99), kind=kLoop, calls=%fused_computation.60 | loop fusion | flops 4194304 | bytes 2097152 | tf_op jit(solution)/shard_map/concatenate | solution.py:111
  65.6 4.1 %collective-permute-done.6 = bf16[2,127,256]{1,2,0:T(8,128)(2,1)S(1)} collective-permute-done((bf16[2,127,256]{1,2,0:T(8,128)(2,1)S(1)}, bf16[2,127,256]{1,2,0:T(8,128)(2,1)S(1)}, u32[]{:S(2)}, u32[]{:S(2)}) %collective-permute-start.6) | collective-permute-done | bytes 130080 | tf_op jit(solution)/shard_map/ppermute | solution.py:15
  69.7 2.2 %collective-permute-start.8 = (bf16[1,2,127,256]{2,3,1,0:T(8,128)(2,1)S(1)}, bf16[1,2,127,256]{2,3,1,0:T(8,128)(2,1)S(1)}, u32[]{:S(2)}, u32[]{:S(2)}) collective-permute-start(bf16[1,2,127,256]{2,3,1,0:T(8,128)(2,1)S(1)} %bitcast.286), channel_id=1, source_target_pairs={{1,0},{2,1},{3,2},{4,3},{5,4},{6,5},{7,6},{8,7},{9,8},{10,9},{11,1... | collective-permute-start | bytes 390152 | tf_op jit(solution)/shard_map/ppermute | solution.py:36
  71.9 4.1 %collective-permute-start.7 = (bf16[1,2,127,256]{2,3,1,0:T(8,128)(2,1)S(1)}, bf16[1,2,127,256]{2,3,1,0:T(8,128)(2,1)S(1)}, u32[]{:S(2)}, u32[]{:S(2)}) collective-permute-start(bf16[1,2,127,256]{2,3,1,0:T(8,128)(2,1)S(1)} %bitcast.287), channel_id=1, source_target_pairs={{0,1},{1,2},{2,3},{3,4},{4,5},{5,6},{6,7},{7,8},{8,9},{9,10},{10,1... | collective-permute-start | bytes 390152 | tf_op jit(solution)/shard_map/ppermute | solution.py:34
  76.8 16.5 %all-to-all-start.1 = ((f32[32,1,32]{2,1,0:T(1,128)}), f32[32,1,32]{2,1,0:T(1,128)S(1)}, u32[]{:S(2)}, u32[]{:S(2)}) async-start(f32[32,1,32]{2,1,0:T(1,128)} %broadcast_in_dim.40), calls=%async_computation.1 | async-start | bytes 32768 | tf_op jit(solution)/shard_map/all_to_all | solution.py:23
  93.3 11.7 %all-to-all-done.1 = f32[32,1,32]{2,1,0:T(1,128)S(1)} async-done(((f32[32,1,32]{2,1,0:T(1,128)}), f32[32,1,32]{2,1,0:T(1,128)S(1)}, u32[]{:S(2)}, u32[]{:S(2)}) %all-to-all-start.1) | async-done | bytes 4128 | tf_op jit(solution)/shard_map/all_to_all | solution.py:23
  105.6 2.0 %fusion.47 = bf16[2,127,256]{1,2,0:T(8,128)(2,1)S(1)} fusion(s32[]{:T(128)S(6)} %select_n.22, f32[1,256,256]{1,2,0:T(8,128)S(1)} %slice_bitcast_fusion.1, f32[1,256,256]{1,2,0:T(8,128)S(1)} %slice_bitcast_fusion, bf16[1,2,127,256]{2,3,1,0:T(8,128)(2,1)S(1)} %collective-permute-done.8, bf16[2,127,256]{1,2,0:T(8,128)(2,1)S(1)} %collective-permute-done.6, ...), kind=kLoop, calls=%fused_computation.92 | loop fusion | flops 715264 | bytes 1044496 | tf_op jit(solution)/shard_map/dynamic_update_slice | solution.py:172
  107.6 1.0 add.76
  (98 shorter events, 25.2 us)
Async XLA Ops:
  0.6 11.6 %copy-start.1 = (bf16[1,1,1,256,256]{4,3,2,1,0:T(8,128)(2,1)S(1)}, bf16[1,1,1,256,256]{4,3,2,1,0:T(8,128)(2,1)}, u32[]{:S(2)}) copy-start(bf16[1,1,1,256,256]{4,3,2,1,0:T(8,128)(2,1)} %param.8) | copy-start | bytes 393220
  0.6 11.1 %copy-start = (bf16[1,1,1,256,2048]{4,3,2,1,0:T(8,128)(2,1)S(1)}, bf16[1,1,1,256,2048]{4,3,2,1,0:T(8,128)(2,1)}, u32[]{:S(2)}) copy-start(bf16[1,1,1,256,2048]{4,3,2,1,0:T(8,128)(2,1)} %param.10) | copy-start | bytes 3145732
  0.7 11.5 %copy-start.2 = (f32[32]{0:T(128)S(1)}, f32[32]{0:T(128)}, u32[]{:S(2)}) copy-start(f32[32]{0:T(128)} %param.11) | copy-start | bytes 388
  1.4 13.0 %collective-permute-start.3 = (bf16[3]{0:T(256)(128)(2,1)S(1)}, bf16[3]{0:T(256)(128)(2,1)S(1)}, u32[]{:S(2)}, u32[]{:S(2)}) collective-permute-start(bf16[3]{0:T(256)(128)(2,1)S(1)} %and_convert_fusion), channel_id=1, source_target_pairs={{32,0},{64,32},{96,64},{33,1},{65,33},{97,65},{34,2},{66,34},{98,6... | collective-permute-start | bytes 26 | tf_op jit(solution)/shard_map/ppermute | solution.py:15
  5.3 19.9 %collective-permute-start = (bf16[2,127,256]{1,2,0:T(8,128)(2,1)}, bf16[2,127,256]{1,2,0:T(8,128)(2,1)}, u32[]{:S(2)}, u32[]{:S(2)}) collective-permute-start(bf16[2,127,256]{1,2,0:T(8,128)(2,1)} %pad_maximum_fusion.4), channel_id=1, source_target_pairs={{0,32},{32,64},{64,96},{1,33},{33,65},{65,97},{2,34},{34,66},{66,9... | collective-permute-start | bytes 390152 | tf_op jit(solution)/shard_map/ppermute | solution.py:15
  14.5 16.3 %collective-permute-start.5 = (bf16[1,3]{1,0:T(2,128)(2,1)S(1)}, bf16[1,3]{1,0:T(2,128)(2,1)S(1)}, u32[]{:S(2)}, u32[]{:S(2)}) collective-permute-start(bf16[1,3]{1,0:T(2,128)(2,1)S(1)} %bitcast.290), channel_id=1, source_target_pairs={{1,0},{2,1},{3,2},{4,3},{5,4},{6,5},{7,6},{8,7},{9,8},{10,9},{11,1... | collective-permute-start | bytes 26 | tf_op jit(solution)/shard_map/ppermute | solution.py:36
  23.2 7.5 %collective-permute-start.4 = (bf16[1,3]{1,0:T(2,128)(2,1)S(1)}, bf16[1,3]{1,0:T(2,128)(2,1)S(1)}, u32[]{:S(2)}, u32[]{:S(2)}) collective-permute-start(bf16[1,3]{1,0:T(2,128)(2,1)S(1)} %bitcast.291), channel_id=1, source_target_pairs={{0,1},{1,2},{2,3},{3,4},{4,5},{5,6},{6,7},{7,8},{8,9},{9,10},{10,1... | collective-permute-start | bytes 26 | tf_op jit(solution)/shard_map/ppermute | solution.py:34
  25.2 6.5 %collective-permute-start.2 = (bf16[1,2,127,256]{2,3,1,0:T(8,128)(2,1)}, bf16[1,2,127,256]{2,3,1,0:T(8,128)(2,1)S(1)}, u32[]{:S(2)}, u32[]{:S(2)}) collective-permute-start(bf16[1,2,127,256]{2,3,1,0:T(8,128)(2,1)} %bitcast.3), channel_id=1, source_target_pairs={{1,0},{2,1},{3,2},{4,3},{5,4},{6,5},{7,6},{8,7},{9,8},{10,9},{11,1... | collective-permute-start | bytes 390152 | tf_op jit(solution)/shard_map/ppermute | solution.py:36
  27.6 5.4 %collective-permute-start.1 = (bf16[1,2,127,256]{2,3,1,0:T(8,128)(2,1)}, bf16[1,2,127,256]{2,3,1,0:T(8,128)(2,1)S(1)}, u32[]{:S(2)}, u32[]{:S(2)}) collective-permute-start(bf16[1,2,127,256]{2,3,1,0:T(8,128)(2,1)} %bitcast.3), channel_id=1, source_target_pairs={{0,1},{1,2},{2,3},{3,4},{4,5},{5,6},{6,7},{7,8},{8,9},{9,10},{10,1... | collective-permute-start | bytes 390152 | tf_op jit(solution)/shard_map/ppermute | solution.py:34
  58.8 17.4 %all-to-all-start = ((f32[16,1,32]{2,1,0:T(1,128)}), f32[16,1,32]{2,1,0:T(1,128)S(1)}, u32[]{:S(2)}, u32[]{:S(2)}) async-start(f32[16,1,32]{2,1,0:T(1,128)} %broadcast_in_dim.39), calls=%async_computation | async-start | bytes 16384 | tf_op jit(solution)/shard_map/all_to_all | solution.py:23
  63.0 6.7 %collective-permute-start.6 = (bf16[2,127,256]{1,2,0:T(8,128)(2,1)S(1)}, bf16[2,127,256]{1,2,0:T(8,128)(2,1)S(1)}, u32[]{:S(2)}, u32[]{:S(2)}) collective-permute-start(bf16[2,127,256]{1,2,0:T(8,128)(2,1)S(1)} %pad_maximum_fusion.5), channel_id=1, source_target_pairs={{32,0},{64,32},{96,64},{33,1},{65,33},{97,65},{34,2},{66,34},{98,6... | collective-permute-start | bytes 390152 | tf_op jit(solution)/shard_map/ppermute | solution.py:15
  69.7 35.9 %collective-permute-start.8 = (bf16[1,2,127,256]{2,3,1,0:T(8,128)(2,1)S(1)}, bf16[1,2,127,256]{2,3,1,0:T(8,128)(2,1)S(1)}, u32[]{:S(2)}, u32[]{:S(2)}) collective-permute-start(bf16[1,2,127,256]{2,3,1,0:T(8,128)(2,1)S(1)} %bitcast.286), channel_id=1, source_target_pairs={{1,0},{2,1},{3,2},{4,3},{5,4},{6,5},{7,6},{8,7},{9,8},{10,9},{11,1... | collective-permute-start | bytes 390152 | tf_op jit(solution)/shard_map/ppermute | solution.py:36
  71.9 33.6 %collective-permute-start.7 = (bf16[1,2,127,256]{2,3,1,0:T(8,128)(2,1)S(1)}, bf16[1,2,127,256]{2,3,1,0:T(8,128)(2,1)S(1)}, u32[]{:S(2)}, u32[]{:S(2)}) collective-permute-start(bf16[1,2,127,256]{2,3,1,0:T(8,128)(2,1)S(1)} %bitcast.287), channel_id=1, source_target_pairs={{0,1},{1,2},{2,3},{3,4},{4,5},{5,6},{6,7},{7,8},{8,9},{9,10},{10,1... | collective-permute-start | bytes 390152 | tf_op jit(solution)/shard_map/ppermute | solution.py:34
  76.8 28.2 %all-to-all-start.1 = ((f32[32,1,32]{2,1,0:T(1,128)}), f32[32,1,32]{2,1,0:T(1,128)S(1)}, u32[]{:S(2)}, u32[]{:S(2)}) async-start(f32[32,1,32]{2,1,0:T(1,128)} %broadcast_in_dim.40), calls=%async_computation.1 | async-start | bytes 32768 | tf_op jit(solution)/shard_map/all_to_all | solution.py:23

commit v2 on v0

v2 whole, which is shorter than its diff:
```python
import jax
import jax.numpy as jnp
from jax import lax
from jax.experimental import pallas as pl
from jax.experimental.pallas import tpu as pltpu
from jax.sharding import PartitionSpec as P

HQ = 32
HK = 4
HD = 64
WIN = 128
GROUP = HQ // HK
GCOLS = GROUP * HD
STEPS = 2
PER_STEP = HK // STEPS
LOW = -1e30
F32 = jnp.float32
BF16 = jnp.bfloat16

NT = (((1,), (1,)), ((), ()))
TN = (((0,), (0,)), ((), ()))
NN = (((1,), (0,)), ((), ()))


def mm(a, b, dims):
    return lax.dot_general(a, b, dims, preferred_element_type=F32)


def upper():
    c = lax.broadcasted_iota(jnp.int32, (WIN, WIN), 0)
    r = lax.broadcasted_iota(jnp.int32, (WIN, WIN), 1)
    return c > r


def one_head(s, dp, sink, alive):
    top = jnp.maximum(jnp.max(s, axis=0, keepdims=True), sink)
    e = jnp.exp(s - top)
    sink_e = jnp.exp(sink - top)
    inv = 1.0 / (jnp.sum(e, axis=0, keepdims=True) + sink_e)
    if alive is not None:
        inv = jnp.where(alive, inv, 0.0)
    p = e * inv
    low = p.astype(BF16)
    delta = jnp.sum(low.astype(F32) * dp, axis=0, keepdims=True)
    ds = (p * (dp - delta)).astype(BF16)
    return low, ds, sink_e * inv * delta


def forward_group(sub, keys, values, q, d, seen_upper, sinks, first, bias, alive, low, ds, sink_out, sink_base):
    for pair in range(GROUP // 2):
        at = pair * 2 * HD
        q2 = jnp.concatenate([q[:, at : at + HD], q[:, at + HD : at + 2 * HD]], axis=0)
        d2 = jnp.concatenate([d[:, at : at + HD], d[:, at + HD : at + 2 * HD]], axis=0)
        s2 = mm(keys, q2, NT)
        dp2 = mm(values, d2, NT)
        for one in range(2):
            h = pair * 2 + one
            lanes = slice(one * WIN, (one + 1) * WIN)
            s_up = s2[:WIN, lanes]
            if bias is not None:
                s_up = s_up + bias
            s = jnp.where(seen_upper, s_up, s2[WIN:, lanes])
            dp = jnp.where(seen_upper, dp2[:WIN, lanes], dp2[WIN:, lanes])
            l_h, ds_h, sink_h = one_head(s, dp, sinks[first + h], alive)
            cols = slice(h * WIN, (h + 1) * WIN)
            low[sub, :, cols] = l_h
            ds[sub, :, cols] = ds_h
            sink_out[pl.ds(sink_base + h, 1), :] = sink_h


def backward_group(keys, q, d, mask_up, low, ds):
    up8 = jnp.concatenate([mask_up] * GROUP, axis=1)
    low_up = low * up8
    ds_up = ds * up8
    low_all = jnp.concatenate([low_up, low - low_up], axis=0)
    ds_all = jnp.concatenate([ds_up, ds - ds_up], axis=0)
    q8 = jnp.concatenate([q[:, h * HD : (h + 1) * HD] for h in range(GROUP)], axis=0)
    d8 = jnp.concatenate([d[:, h * HD : (h + 1) * HD] for h in range(GROUP)], axis=0)
    dk = mm(ds_all, q8, NN) * (HD**-0.5)
    dv = mm(low_all, d8, NN)
    dqt = mm(keys, ds_all, TN).astype(BF16)
    parts = []
    for pair in range(GROUP // 2):
        at = pair * 2 * WIN
        two = jnp.concatenate([dqt[:, at : at + WIN], dqt[:, at + WIN : at + 2 * WIN]], axis=0)
        parts.append(two.T)
    return jnp.concatenate(parts, axis=1), dk, dv


def tail_kernel(length, k_ref, v_ref, out_ref):
    c = lax.broadcasted_iota(jnp.int32, (WIN, 2 * WIN), 0)
    j = lax.broadcasted_iota(jnp.int32, (WIN, 2 * WIN), 1)
    pick = jnp.where(j == c + (length[0] - WIN), 1.0, 0.0).astype(BF16)
    out_ref[:, : HK * HD] = mm(pick, k_ref[...], NN).astype(BF16)
    out_ref[:, HK * HD :] = mm(pick, v_ref[...], NN).astype(BF16)


def late_kernel(length, sinks, q_ref, d_ref, k_ref, v_ref, dq_ref, dk_ref, dv_ref, sink_ref, low, ds):
    step = pl.program_id(0)
    seen_upper = upper()
    mask_up = jnp.where(seen_upper, 1.0, 0.0).astype(BF16)
    alive = lax.broadcasted_iota(jnp.int32, (1, WIN), 1) < length[0] - WIN
    for sub in range(PER_STEP):
        cols = slice(sub * GCOLS, (sub + 1) * GCOLS)
        kv = slice(sub * HD, (sub + 1) * HD)
        keys = k_ref[:, kv] * (HD**-0.5)
        values = v_ref[:, kv]
        q = q_ref[:, cols]
        d = d_ref[:, cols]
        forward_group(sub, keys, values, q, d, seen_upper, sinks, (step * PER_STEP + sub) * GROUP, None, alive, low, ds, sink_ref, sub * GROUP)
        dq, dk, dv = backward_group(keys, q, d, mask_up, low[sub], ds[sub])
        dq_ref[:, cols] = dq
        dk_ref[:, kv] = dk
        dv_ref[:, kv] = dv


def early_kernel(place, sinks, q_ref, d_ref, k_ref, v_ref, ka, kb, kc, va, vb, vc, late_sink, low, ds, keys_out, sink_ref, sink_rows):
    step = pl.program_id(0)
    slot = place[0]
    bias = jnp.where(place[1] > 0, 0.0, LOW)
    seen_upper = upper()

    @pl.when(step == 0)
    def _():
        sink_rows[...] = jnp.zeros_like(sink_rows)

    def chosen(a, b, c):
        return jnp.where(slot == 0, a[...], jnp.where(slot == 1, b[...], c[...]))

    tail_k = chosen(ka, kb, kc)
    tail_v = chosen(va, vb, vc)
    for sub in range(PER_STEP):
        cols = slice(sub * GCOLS, (sub + 1) * GCOLS)
        kv = slice(sub * HD, (sub + 1) * HD)
        keys = jnp.concatenate([tail_k[:, kv], k_ref[:, kv]], axis=0) * (HD**-0.5)
        values = jnp.concatenate([tail_v[:, kv], v_ref[:, kv]], axis=0)
        keys_out[:, kv] = keys
        forward_group(sub, keys, values, q_ref[:, cols], d_ref[:, cols], seen_upper, sinks, (step * PER_STEP + sub) * GROUP, bias, None, low, ds, sink_rows, (step * PER_STEP + sub) * GROUP)

    @pl.when(step == STEPS - 1)
    def _():
        sink_rows[:HQ, :] = sink_rows[:HQ, :] + late_sink[...]
        total = -jnp.sum(sink_rows[...].T, axis=0, keepdims=True)
        sink_ref[...] = jnp.broadcast_to(total, sink_ref.shape)


def grads_kernel(place, q_ref, d_ref, keys_ref, low, ds, dq_in, dq_ref, tk_ref, tv_ref, ok_ref, ov_ref):
    del dq_in
    mask_up = jnp.where(upper(), 1.0, 0.0).astype(BF16)
    row = lax.broadcasted_iota(jnp.int32, (WIN, HD), 0)
    flag = (place[0] + 1).astype(F32)
    for sub in range(PER_STEP):
        cols = slice(sub * GCOLS, (sub + 1) * GCOLS)
        kv = slice(sub * HD, (sub + 1) * HD)
        dq, dk, dv = backward_group(keys_ref[:, kv], q_ref[:, cols], d_ref[:, cols], mask_up, low[sub], ds[sub])
        dq_ref[:, cols] = dq
        tk_ref[:, kv] = jnp.where(row == 0, flag, dk[:WIN]).astype(BF16)
        tv_ref[:, kv] = dv[:WIN].astype(BF16)
        ok_ref[:, kv] = dk[WIN:]
        ov_ref[:, kv] = dv[WIN:]


def final_kernel(length, dk_late, dv_late, ok, ov, ka, kb, kc, va, vb, vc, dk_ref, dv_ref):
    j = lax.broadcasted_iota(jnp.int32, (2 * WIN, WIN), 0)
    c = lax.broadcasted_iota(jnp.int32, (2 * WIN, WIN), 1)
    put = jnp.where((j == c + (length[0] - WIN)) & (c > 0), 1.0, 0.0).astype(BF16)
    dk = dk_late[...]
    dv = dv_late[...]
    for k_in, v_in, mark in ((ka, va, 3.0), (kb, vb, 2.0), (kc, vc, 1.0)):
        mine = jnp.max(k_in[:16, :WIN].astype(F32)[0:1, 0:1]) == mark
        picked = jnp.where(mine, put, jnp.zeros_like(put))
        dk = dk + mm(picked, k_in[...], NN)
        dv = dv + mm(picked, v_in[...], NN)
    half = slice(0, WIN)
    rest = slice(WIN, 2 * WIN)
    dk_ref[half, :] = (dk[half] + ok[...]).astype(BF16)
    dk_ref[rest, :] = dk[rest].astype(BF16)
    dv_ref[half, :] = (dv[half] + ov[...]).astype(BF16)
    dv_ref[rest, :] = dv[rest].astype(BF16)


SMEM = pl.BlockSpec(memory_space=pltpu.SMEM)
WHOLE = pl.BlockSpec(memory_space=pltpu.VMEM)
ANY = pl.BlockSpec(memory_space=pl.ANY)
PARAMS = pltpu.CompilerParams(vmem_limit_bytes=48 * 1024 * 1024)
KV = HK * HD
KV_STEP = KV // STEPS
COLS = HQ * HD
COLS_STEP = COLS // STEPS


def shaped(shape, dtype):
    return jax.ShapeDtypeStruct(shape, dtype)


def blocks(rows, cols, at):
    return pl.BlockSpec((rows, cols), lambda p: (at, p))


def cost(flops, size):
    return pl.CostEstimate(flops=flops, bytes_accessed=size, transcendentals=0)


def tails(length, k, v):
    return pl.pallas_call(
        tail_kernel,
        out_shape=shaped((WIN, 2 * KV), BF16),
        in_specs=[SMEM, WHOLE, WHOLE],
        out_specs=WHOLE,
        compiler_params=PARAMS,
        cost_estimate=cost(2 * 128 * 256 * 512, 400_000),
        name="tails",
    )(length, k, v)


def late_rows(length, sinks, q, d, k, v):
    return pl.pallas_call(
        late_kernel,
        grid=(STEPS,),
        out_shape=(
            shaped((2 * WIN, COLS), BF16),
            shaped((2 * WIN, KV), F32),
            shaped((2 * WIN, KV), F32),
            shaped((HQ, WIN), F32),
        ),
        in_specs=[
            SMEM,
            SMEM,
            blocks(WIN, COLS_STEP, 1),
            blocks(WIN, COLS_STEP, 1),
            blocks(2 * WIN, KV_STEP, 0),
            blocks(2 * WIN, KV_STEP, 0),
        ],
        out_specs=(
            blocks(WIN, COLS_STEP, 1),
            blocks(2 * WIN, KV_STEP, 0),
            blocks(2 * WIN, KV_STEP, 0),
            pl.BlockSpec((HQ // STEPS, WIN), lambda p: (p, 0)),
        ),
        scratch_shapes=[
            pltpu.VMEM((PER_STEP, WIN, GROUP * WIN), BF16),
            pltpu.VMEM((PER_STEP, WIN, GROUP * WIN), BF16),
        ],
        compiler_params=PARAMS,
        cost_estimate=cost(5 * 2 * 32 * 128 * 256 * 64 * 2, 2_500_000),
        name="late_rows",
    )(length, sinks, q, d, k, v)


def early_rows(place, sinks, q, d, k, v, lo, mid, hi, late_sink, copies):
    tail_k = blocks(WIN, KV_STEP, 0)
    tail_v = pl.BlockSpec((WIN, KV_STEP), lambda p: (0, STEPS + p))
    packed = pl.BlockSpec((PER_STEP, WIN, GROUP * WIN), lambda p: (p, 0, 0))
    return pl.pallas_call(
        early_kernel,
        grid=(STEPS,),
        out_shape=(
            shaped((HK, WIN, GROUP * WIN), BF16),
            shaped((HK, WIN, GROUP * WIN), BF16),
            shaped((2 * WIN, KV), BF16),
            shaped((copies, WIN), F32),
        ),
        in_specs=[
            SMEM,
            SMEM,
            blocks(WIN, COLS_STEP, 0),
            blocks(WIN, COLS_STEP, 0),
            blocks(WIN, KV_STEP, 0),
            blocks(WIN, KV_STEP, 0),
            tail_k,
            tail_k,
            tail_k,
            tail_v,
            tail_v,
            tail_v,
            pl.BlockSpec((HQ, WIN), lambda p: (0, 0)),
        ],
        out_specs=(packed, packed, blocks(2 * WIN, KV_STEP, 0), pl.BlockSpec((copies, WIN), lambda p: (0, 0))),
        scratch_shapes=[pltpu.VMEM((WIN, WIN), F32)],
        compiler_params=PARAMS,
        cost_estimate=cost(2 * 2 * 32 * 128 * 256 * 64 * 2, 2_500_000),
        name="early_rows",
    )(place, sinks, q, d, k, v, lo, mid, hi, lo, mid, hi, late_sink)


def early_grads(place, q, d, keys, low, ds, dq):
    packed = pl.BlockSpec((PER_STEP, WIN, GROUP * WIN), lambda p: (p, 0, 0))
    tail = blocks(WIN, KV_STEP, 0)
    return pl.pallas_call(
        grads_kernel,
        grid=(STEPS,),
        out_shape=(
            shaped((2 * WIN, COLS), BF16),
            shaped((WIN, KV), BF16),
            shaped((WIN, KV), BF16),
            shaped((WIN, KV), F32),
            shaped((WIN, KV), F32),
        ),
        in_specs=[
            SMEM,
            blocks(WIN, COLS_STEP, 0),
            blocks(WIN, COLS_STEP, 0),
            blocks(2 * WIN, KV_STEP, 0),
            packed,
            packed,
            ANY,
        ],
        out_specs=(blocks(WIN, COLS_STEP, 0), tail, tail, tail, tail),
        input_output_aliases={6: 0},
        compiler_params=PARAMS,
        cost_estimate=cost(3 * 2 * 32 * 128 * 256 * 64 * 2, 2_500_000),
        name="early_grads",
    )(place, q, d, keys, low, ds, dq)


def finish(length, dk_late, dv_late, ok, ov, lo, mid, hi):
    return pl.pallas_call(
        final_kernel,
        out_shape=(shaped((2 * WIN, KV), BF16), shaped((2 * WIN, KV), BF16)),
        in_specs=[SMEM] + [WHOLE] * 10,
        out_specs=(WHOLE, WHOLE),
        compiler_params=PARAMS,
        cost_estimate=cost(2 * 3 * 256 * 128 * 512, 2_000_000),
        name="finish",
    )(length, dk_late, dv_late, ok, ov, lo[0], mid[0], hi[0], lo[1], mid[1], hi[1])


def moved(rows, axis, by):
    count = lax.axis_size(axis)
    pairs = [(i, i + by) for i in range(count) if 0 <= i + by < count]
    return lax.ppermute(rows, axis, pairs)


def summed_over(copies, axes):
    return jnp.sum(lax.all_to_all(copies, axes, 0, 0, tiled=True), axis=0)


def shards(query_rows, key_rows, value_rows, output_grad, sink_logits, parent_branch, segment_length):
    q = query_rows[0, 0, 0]
    k = key_rows[0, 0, 0]
    v = value_rows[0, 0, 0]
    d = output_grad[0, 0, 0]
    length = segment_length.reshape(1)
    branch = lax.axis_index("expert")
    level = lax.axis_index("ctx")
    slot = parent_branch[0, 0, 0] - branch + 1
    place = jnp.stack([slot, (level > 0).astype(jnp.int32)]).astype(jnp.int32)

    own_tail = tails(length, k, v)
    mid = moved(own_tail, "ctx", 1)
    dq, dk_late, dv_late, late_sink = late_rows(length, sink_logits, q, d, k, v)
    lo = moved(mid, "expert", 1)
    hi = moved(mid, "expert", -1)
    plane = lax.axis_size("dp") * lax.axis_size("ctx")
    low, ds, keys, sink_copies = early_rows(place, sink_logits, q, d, k, v, lo, mid, hi, late_sink, plane)

    in_plane = summed_over(sink_copies, ("dp", "ctx"))
    dq, tail_k, tail_v, ok, ov = early_grads(place, q, d, keys, low, ds, dq)
    spread = jnp.broadcast_to(in_plane[None], (lax.axis_size("expert"),) + in_plane.shape)
    sink_grad = summed_over(spread, ("expert",))[:HQ]

    up = moved(jnp.stack([tail_k, tail_v]), "ctx", -1)
    up_lo = moved(up, "expert", 1)
    up_hi = moved(up, "expert", -1)
    dk, dv = finish(length, dk_late, dv_late, ok, ov, up_lo, up, up_hi)
    return dq[None, None, None], dk[None, None, None], dv[None, None, None], sink_grad


def solution(mesh):
    part = P("dp", "ctx", "expert", None, None)
    scalar = P("dp", "ctx", "expert")
    return jax.shard_map(
        shards,
        mesh=mesh,
        in_specs=(part, part, part, part, P(), scalar, scalar),
        out_specs=(part, part, part, P()),
        check_vma=False,
    )
```

time: 185 us -> 85.1 us (0.46)
  blocking collectives: 108 us -> 40.9 us
  matrix products: 21.1 us -> 0 us
  Pallas kernels: 0 us -> 13.6 us
  starting transfers between devices: 30.4 us -> 19.4 us
  other arithmetic: 8.2 us -> 0.65 us
  local copies, waits for them, and re-layouts: 8.82 us -> 4.96 us
  waiting for transfers between devices: 5.41 us -> 3.17 us
    psum x1 -> x0, blocking collectives: 108 us -> none  [shards(): sink_grad = lax.psum(sink_terms, ('dp', 'ctx', 'expert'))]
    all_to_all x0 -> x2, blocking collectives: none -> 40.9 us  [summed_over(): return jnp.sum(lax.all_to_all(copies, axes, 0, 0, tiled=True), axis=0)]
    dot_general x24 -> x0, matrix products: 21.1 us -> none  [the longest x4 5.06 us: attend_backward(): jnp.einsum('ihd,jd->hij', grouped_d, group_values, preferred_element_type...]
    pallas_call x0 -> x5, Pallas kernels: none -> 13.6 us  [the longest x1 5.57 us: late_rows(): pl.pallas_call(late_kernel, grid=(STEPS,), out_shape=(shaped((2 * WIN, CO...]
    ppermute x9 -> x6, starting transfers between devices: 30.4 us -> 19.4 us  [moved(): return lax.ppermute(rows, axis, pairs)]
    slice x12 -> x0, local copies, waits for them, and re-layouts: 3.08 us -> none  [the longest x5 1.8 us: attend_backward(): query_rows[:, first_col:last_col].reshape(tokens, group_size, HD)]
    reduce_sum x6 -> x2, other arithmetic: 3.08 us -> 0.56 us  [summed_over(): return jnp.sum(lax.all_to_all(copies, axes, 0, 0, tiled=True), axis=0)]
    unnamed x10 -> x18, local copies, waits for them, and re-layouts: 2.64 us -> 4.92 us
  transfers between devices with their start and end apart: 9 -> 6, of which waited for: 3 -> 3; matrix products, arithmetic and copies ran while one was open for 4% -> 1% of each run, Pallas kernels for 0% -> 7%
where the time goes in v2:
time: 85.1 us; the launch traced here: 84.7 us
  blocking collectives  40.9 us (48%)
  starting transfers between devices  19.4 us (23%)
  Pallas kernels  13.6 us (16%)
  local copies, waits for them, and re-layouts  4.96 us (6%)
  waiting for transfers between devices  3.17 us (4%)
  between operations  2.07 us (2%)
    all_to_all x2, blocking collectives, summed_over(): return jnp.sum(lax.all_to_all(copies, axes, 0, 0, tiled=True), axis=0)  40.9 us
    ppermute x6, starting transfers between devices, moved(): return lax.ppermute(rows, axis, pairs)  19.4 us
    pallas_call x1, Pallas kernels, late_rows(): pl.pallas_call(late_kernel, grid=(STEPS,), out_shape=(shaped((2 * WIN, CO...  5.57 us
    unnamed x18, local copies, waits for them, and re-layouts  4.92 us
    pallas_call x1, Pallas kernels, early_rows(): pl.pallas_call(early_kernel, grid=(STEPS,), out_shape=(shaped((HK, WIN, G...  3.37 us
    pallas_call x1, Pallas kernels, early_grads(): pl.pallas_call(grads_kernel, grid=(STEPS,), out_shape=(shaped((2 * WIN, C...  3.36 us
    ppermute x6, waiting for transfers between devices, moved(): return lax.ppermute(rows, axis, pairs)  3.17 us
  transfers between devices with their start and end apart: 6, of which 3 were waited for; matrix products, arithmetic and copies ran while one was open for 1% of the time, Pallas kernels for 7%

profile of v2, /device:TPU:1, one launch (start us, length us, event | category | flops | bytes accessed | tf_op | source)
XLA Modules:
  0.0 84.7 jit_solution(12082579014712970645)
XLA Ops:
  1.3 0.9 %copy-done.4 = bf16[1,1,1,256,256]{4,3,2,1,0:T(8,128)(2,1)S(1)} copy-done((bf16[1,1,1,256,256]{4,3,2,1,0:T(8,128)(2,1)S(1)}, bf16[1,1,1,256,256]{4,3,2,1,0:T(8,128)(2,1)}, u32[]{:S(2)}) %copy-start.4) | copy-done | bytes 131096
  2.2 0.9 %copy-done.6 = bf16[1,1,1,256,256]{4,3,2,1,0:T(8,128)(2,1)S(1)} copy-done((bf16[1,1,1,256,256]{4,3,2,1,0:T(8,128)(2,1)S(1)}, bf16[1,1,1,256,256]{4,3,2,1,0:T(8,128)(2,1)}, u32[]{:S(2)}) %copy-start.6) | copy-done | bytes 131096
  3.1 0.2 tails.1
  3.3 4.0 %collective-permute-start = (bf16[128,512]{1,0:T(8,128)(2,1)S(1)}, bf16[128,512]{1,0:T(8,128)(2,1)S(1)}, u32[]{:S(2)}, u32[]{:S(2)}) collective-permute-start(bf16[128,512]{1,0:T(8,128)(2,1)S(1)} %tails.1), channel_id=1, source_target_pairs={{0,32},{32,64},{64,96},{1,33},{33,65},{65,97},{2,34},{34,66},{66,9... | collective-permute-start | bytes 393224 | tf_op jit(solution)/shard_map/ppermute | solution.py:331
  7.9 1.3 %collective-permute-done.kb.vb = bf16[128,512]{1,0:T(8,128)(2,1)S(1)} collective-permute-done((bf16[128,512]{1,0:T(8,128)(2,1)S(1)}, bf16[128,512]{1,0:T(8,128)(2,1)S(1)}, u32[]{:S(2)}, u32[]{:S(2)}) %collective-permute-start) | collective-permute-done | bytes 131104 | tf_op jit(solution)/shard_map/ppermute | solution.py:331
  9.2 6.7 %collective-permute-start.2 = (bf16[128,512]{1,0:T(8,128)(2,1)S(1)}, bf16[128,512]{1,0:T(8,128)(2,1)S(1)}, u32[]{:S(2)}, u32[]{:S(2)}) collective-permute-start(bf16[128,512]{1,0:T(8,128)(2,1)S(1)} %collective-permute-done.kb.vb), channel_id=1, source_target_pairs={{1,0},{2,1},{3,2},{4,3},{5,4},{6,5},{7,6},{8,7},{9,8},{10,9},{11,1... | collective-permute-start | bytes 393224 | tf_op jit(solution)/shard_map/ppermute | solution.py:331
  15.9 1.9 %collective-permute-start.1 = (bf16[128,512]{1,0:T(8,128)(2,1)S(1)}, bf16[128,512]{1,0:T(8,128)(2,1)S(1)}, u32[]{:S(2)}, u32[]{:S(2)}) collective-permute-start(bf16[128,512]{1,0:T(8,128)(2,1)S(1)} %collective-permute-done.kb.vb), channel_id=1, source_target_pairs={{0,1},{1,2},{2,3},{3,4},{4,5},{5,6},{6,7},{7,8},{8,9},{9,10},{10,1... | collective-permute-start | bytes 393224 | tf_op jit(solution)/shard_map/ppermute | solution.py:331
  17.8 0.1 pad_add_fusion.place
  17.9 0.6 copy-done.8
  18.5 1.2 %copy-done = bf16[1,1,1,256,2048]{4,3,2,1,0:T(8,128)(2,1)S(1)} copy-done((bf16[1,1,1,256,2048]{4,3,2,1,0:T(8,128)(2,1)S(1)}, bf16[1,1,1,256,2048]{4,3,2,1,0:T(8,128)(2,1)}, u32[]{:S(2)}) %copy-start) | copy-done | bytes 1048600
  19.8 1.2 %copy-done.2 = bf16[1,1,1,256,2048]{4,3,2,1,0:T(8,128)(2,1)S(1)} copy-done((bf16[1,1,1,256,2048]{4,3,2,1,0:T(8,128)(2,1)S(1)}, bf16[1,1,1,256,2048]{4,3,2,1,0:T(8,128)(2,1)}, u32[]{:S(2)}) %copy-start.2) | copy-done | bytes 1048600
  21.0 5.6 %late_rows.1 = (bf16[256,2048]{1,0:T(8,128)(2,1)}, f32[256,256]{1,0:T(8,128)S(1)}, f32[256,256]{1,0:T(8,128)S(1)}, f32[32,128]{1,0:T(8,128)S(1)}) custom-call(s32[1]{0:T(128)} %bitcast.32.length, f32[32]{0:T(128)S(1)} %copy-done.8, bf16[256,2048]{1,0:T(8,128)(2,1)S(1)} %bitcast.34, bf16[256,2048]{1,0:T(8,128)(2,1)S(1)} %bitcast.37, ...), custom_call_target="tpu_custom_call" | custom-call | flops 1342177280 | bytes 2500000 | tf_op jit(solution)/shard_map/late_rows/pallas_call | solution.py:217
  26.6 0.0 copy-start.3
  26.6 3.4 %early_rows.1 = (bf16[4,128,1024]{2,1,0:T(8,128)(2,1)S(1)}, bf16[4,128,1024]{2,1,0:T(8,128)(2,1)S(1)}, bf16[256,256]{1,0:T(8,128)(2,1)S(1)}, f32[16,128]{1,0:T(8,128)S(1)}) custom-call(s32[2]{0:T(128)S(1)} %pad_add_fusion.place, f32[32]{0:T(128)S(1)} %copy-done.8, bf16[256,2048]{1,0:T(8,128)(2,1)S(1)} %bitcast.35, bf16[256,2048]{1,0:T(8,128)(2,1)S(1)} %bitcast.38, ...), custom_call_target="tpu_custom_call" | custom-call | flops 536870912 | bytes 2500000 | tf_op jit(solution)/shard_map/early_rows/pallas_call | solution.py:254
  30.0 3.4 %early_grads.1 = (bf16[256,2048]{1,0:T(8,128)(2,1)}, bf16[128,256]{1,0:T(8,128)(2,1)S(1)}, bf16[128,256]{1,0:T(8,128)(2,1)S(1)}, f32[128,256]{1,0:T(8,128)S(1)}, f32[128,256]{1,0:T(8,128)S(1)}) custom-call(s32[2]{0:T(128)S(1)} %pad_add_fusion.place, bf16[256,2048]{1,0:T(8,128)(2,1)S(1)} %bitcast.36, ...), custom_call_target="tpu_custom_call", output_to_operand_aliasing={{0}: (6, {})} | custom-call | flops 805306368 | bytes 2500000 | tf_op jit(solution)/shard_map/early_grads/pallas_call | solution.py:289
  33.4 1.3 %collective-permute-start.3 = (bf16[2,128,256]{2,1,0:T(8,128)(2,1)S(1)}, bf16[2,128,256]{2,1,0:T(8,128)(2,1)S(1)}, u32[]{:S(2)}, u32[]{:S(2)}) collective-permute-start(bf16[2,128,256]{2,1,0:T(8,128)(2,1)S(1)} %pad_maximum_fusion), channel_id=1, source_target_pairs={{32,0},{64,32},{96,64},{33,1},{65,33},{97,65},{34,2},{66,34},{98,6... | collective-permute-start | bytes 393224 | tf_op jit(solution)/shard_map/ppermute | solution.py:331
  34.7 13.3 %all_to_all.15 = f32[16,1,128]{2,1,0:T(1,128)S(1)} all-to-all(f32[16,1,128]{2,1,0:T(1,128)S(1)} %bitcast.48), channel_id=1, replica_groups=mesh['dp'=4,'ctx'=4,'expert'=32] {'dp','ctx'}, dimensions={0} | all-to-all | bytes 16384 | tf_op jit(solution)/shard_map/all_to_all | solution.py:335
  48.0 27.5 %all_to_all.16 = f32[32,1,128]{2,1,0:T(1,128)S(1)} all-to-all(f32[32,1,128]{2,1,0:T(1,128)S(1)} %broadcast_in_dim.18), channel_id=1, replica_groups=mesh['dp'=4,'ctx'=4,'expert'=32] {'expert'}, dimensions={0} | all-to-all | bytes 32768 | tf_op jit(solution)/shard_map/all_to_all | solution.py:335
  75.6 0.5 reduce_sum.19
  76.1 2.8 %collective-permute-start.5 = (bf16[2,128,256]{2,1,0:T(8,128)(2,1)S(1)}, bf16[2,128,256]{2,1,0:T(8,128)(2,1)S(1)}, u32[]{:S(2)}, u32[]{:S(2)}) collective-permute-start(bf16[2,128,256]{2,1,0:T(8,128)(2,1)S(1)} %collective-permute-done.3), channel_id=1, source_target_pairs={{1,0},{2,1},{3,2},{4,3},{5,4},{6,5},{7,6},{8,7},{9,8},{10,9},{11,1... | collective-permute-start | bytes 393224 | tf_op jit(solution)/shard_map/ppermute | solution.py:331
  78.9 2.7 %collective-permute-start.4 = (bf16[2,128,256]{2,1,0:T(8,128)(2,1)S(1)}, bf16[2,128,256]{2,1,0:T(8,128)(2,1)S(1)}, u32[]{:S(2)}, u32[]{:S(2)}) collective-permute-start(bf16[2,128,256]{2,1,0:T(8,128)(2,1)S(1)} %collective-permute-done.3), channel_id=1, source_target_pairs={{0,1},{1,2},{2,3},{3,4},{4,5},{5,6},{6,7},{7,8},{8,9},{9,10},{10,1... | collective-permute-start | bytes 393224 | tf_op jit(solution)/shard_map/ppermute | solution.py:331
  81.7 0.7 collective-permute-done.5
  82.4 1.2 %collective-permute-done.4 = bf16[2,128,256]{2,1,0:T(8,128)(2,1)S(1)} collective-permute-done((bf16[2,128,256]{2,1,0:T(8,128)(2,1)S(1)}, bf16[2,128,256]{2,1,0:T(8,128)(2,1)S(1)}, u32[]{:S(2)}, u32[]{:S(2)}) %collective-permute-start.4) | collective-permute-done | bytes 131104 | tf_op jit(solution)/shard_map/ppermute | solution.py:331
  83.6 1.1 %finish.1 = (bf16[256,256]{1,0:T(8,128)(2,1)}, bf16[256,256]{1,0:T(8,128)(2,1)}) custom-call(s32[1]{0:T(128)} %bitcast.33.length, f32[256,256]{1,0:T(8,128)S(1)} %get-tuple-element.25.dk_late, f32[256,256]{1,0:T(8,128)S(1)} %get-tuple-element.26.dv_late, f32[128,256]{1,0:T(8,128)S(1)} %get-tuple-element.27.ok, f32[128,256]{1,0:T(8,128)S(1)} %get-tuple-element.28.ov, ...), custom_call_target="tpu_custom_call" | custom-call | flops 100663296 | bytes 2000000 | tf_op jit(solution)/shard_map/finish/pallas_call | solution.py:317
  (21 shorter events, 0.1 us)
Async XLA Ops:
  1.3 0.9 %copy-start.4 = (bf16[1,1,1,256,256]{4,3,2,1,0:T(8,128)(2,1)S(1)}, bf16[1,1,1,256,256]{4,3,2,1,0:T(8,128)(2,1)}, u32[]{:S(2)}) copy-start(bf16[1,1,1,256,256]{4,3,2,1,0:T(8,128)(2,1)} %param.8) | copy-start | bytes 393220
  2.2 0.9 %copy-start.6 = (bf16[1,1,1,256,256]{4,3,2,1,0:T(8,128)(2,1)S(1)}, bf16[1,1,1,256,256]{4,3,2,1,0:T(8,128)(2,1)}, u32[]{:S(2)}) copy-start(bf16[1,1,1,256,256]{4,3,2,1,0:T(8,128)(2,1)} %param.9) | copy-start | bytes 393220
  3.1 14.8 %copy-start.5 = (bf16[1,1,1,256,256]{4,3,2,1,0:T(8,128)(2,1)S(1)}, bf16[1,1,1,256,256]{4,3,2,1,0:T(8,128)(2,1)}, u32[]{:S(2)}) copy-start(bf16[1,1,1,256,256]{4,3,2,1,0:T(8,128)(2,1)} %param.8) | copy-start | bytes 393220
  3.1 14.8 %copy-start.7 = (bf16[1,1,1,256,256]{4,3,2,1,0:T(8,128)(2,1)S(1)}, bf16[1,1,1,256,256]{4,3,2,1,0:T(8,128)(2,1)}, u32[]{:S(2)}) copy-start(bf16[1,1,1,256,256]{4,3,2,1,0:T(8,128)(2,1)} %param.9) | copy-start | bytes 393220
  3.3 5.9 %collective-permute-start = (bf16[128,512]{1,0:T(8,128)(2,1)S(1)}, bf16[128,512]{1,0:T(8,128)(2,1)S(1)}, u32[]{:S(2)}, u32[]{:S(2)}) collective-permute-start(bf16[128,512]{1,0:T(8,128)(2,1)S(1)} %tails.1), channel_id=1, source_target_pairs={{0,32},{32,64},{64,96},{1,33},{33,65},{65,97},{2,34},{34,66},{66,9... | collective-permute-start | bytes 393224 | tf_op jit(solution)/shard_map/ppermute | solution.py:331
  9.2 17.4 %collective-permute-start.2 = (bf16[128,512]{1,0:T(8,128)(2,1)S(1)}, bf16[128,512]{1,0:T(8,128)(2,1)S(1)}, u32[]{:S(2)}, u32[]{:S(2)}) collective-permute-start(bf16[128,512]{1,0:T(8,128)(2,1)S(1)} %collective-permute-done.kb.vb), channel_id=1, source_target_pairs={{1,0},{2,1},{3,2},{4,3},{5,4},{6,5},{7,6},{8,7},{9,8},{10,9},{11,1... | collective-permute-start | bytes 393224 | tf_op jit(solution)/shard_map/ppermute | solution.py:331
  15.9 10.7 %collective-permute-start.1 = (bf16[128,512]{1,0:T(8,128)(2,1)S(1)}, bf16[128,512]{1,0:T(8,128)(2,1)S(1)}, u32[]{:S(2)}, u32[]{:S(2)}) collective-permute-start(bf16[128,512]{1,0:T(8,128)(2,1)S(1)} %collective-permute-done.kb.vb), channel_id=1, source_target_pairs={{0,1},{1,2},{2,3},{3,4},{4,5},{5,6},{6,7},{7,8},{8,9},{9,10},{10,1... | collective-permute-start | bytes 393224 | tf_op jit(solution)/shard_map/ppermute | solution.py:331
  17.9 0.7 copy-start.8
  18.5 1.2 %copy-start = (bf16[1,1,1,256,2048]{4,3,2,1,0:T(8,128)(2,1)S(1)}, bf16[1,1,1,256,2048]{4,3,2,1,0:T(8,128)(2,1)}, u32[]{:S(2)}) copy-start(bf16[1,1,1,256,2048]{4,3,2,1,0:T(8,128)(2,1)} %param.7) | copy-start | bytes 3145732
  19.8 1.2 %copy-start.2 = (bf16[1,1,1,256,2048]{4,3,2,1,0:T(8,128)(2,1)S(1)}, bf16[1,1,1,256,2048]{4,3,2,1,0:T(8,128)(2,1)}, u32[]{:S(2)}) copy-start(bf16[1,1,1,256,2048]{4,3,2,1,0:T(8,128)(2,1)} %param.10) | copy-start | bytes 3145732
  26.6 3.4 %copy-start.1 = (bf16[1,1,1,256,2048]{4,3,2,1,0:T(8,128)(2,1)S(1)}, bf16[1,1,1,256,2048]{4,3,2,1,0:T(8,128)(2,1)}, u32[]{:S(2)}) copy-start(bf16[1,1,1,256,2048]{4,3,2,1,0:T(8,128)(2,1)} %param.7) | copy-start | bytes 3145732
  26.6 3.4 %copy-start.3 = (bf16[1,1,1,256,2048]{4,3,2,1,0:T(8,128)(2,1)S(1)}, bf16[1,1,1,256,2048]{4,3,2,1,0:T(8,128)(2,1)}, u32[]{:S(2)}) copy-start(bf16[1,1,1,256,2048]{4,3,2,1,0:T(8,128)(2,1)} %param.10) | copy-start | bytes 3145732
  33.4 42.8 %collective-permute-start.3 = (bf16[2,128,256]{2,1,0:T(8,128)(2,1)S(1)}, bf16[2,128,256]{2,1,0:T(8,128)(2,1)S(1)}, u32[]{:S(2)}, u32[]{:S(2)}) collective-permute-start(bf16[2,128,256]{2,1,0:T(8,128)(2,1)S(1)} %pad_maximum_fusion), channel_id=1, source_target_pairs={{32,0},{64,32},{96,64},{33,1},{65,33},{97,65},{34,2},{66,34},{98,6... | collective-permute-start | bytes 393224 | tf_op jit(solution)/shard_map/ppermute | solution.py:331
  76.1 6.3 %collective-permute-start.5 = (bf16[2,128,256]{2,1,0:T(8,128)(2,1)S(1)}, bf16[2,128,256]{2,1,0:T(8,128)(2,1)S(1)}, u32[]{:S(2)}, u32[]{:S(2)}) collective-permute-start(bf16[2,128,256]{2,1,0:T(8,128)(2,1)S(1)} %collective-permute-done.3), channel_id=1, source_target_pairs={{1,0},{2,1},{3,2},{4,3},{5,4},{6,5},{7,6},{8,7},{9,8},{10,9},{11,1... | collective-permute-start | bytes 393224 | tf_op jit(solution)/shard_map/ppermute | solution.py:331
  78.9 4.7 %collective-permute-start.4 = (bf16[2,128,256]{2,1,0:T(8,128)(2,1)S(1)}, bf16[2,128,256]{2,1,0:T(8,128)(2,1)S(1)}, u32[]{:S(2)}, u32[]{:S(2)}) collective-permute-start(bf16[2,128,256]{2,1,0:T(8,128)(2,1)S(1)} %collective-permute-done.3), channel_id=1, source_target_pairs={{0,1},{1,2},{2,3},{3,4},{4,5},{5,6},{6,7},{7,8},{8,9},{9,10},{10,1... | collective-permute-start | bytes 393224 | tf_op jit(solution)/shard_map/ppermute | solution.py:331

commit v3 on v2

v3 whole, which is shorter than its diff:
```python
import functools

import jax
import jax.numpy as jnp
from jax import lax
from jax.experimental import pallas as pl
from jax.experimental.pallas import tpu as pltpu
from jax.sharding import PartitionSpec as P

HQ = 32
HK = 4
HD = 64
WIN = 128
GROUP = HQ // HK
GCOLS = GROUP * HD
PART = HK // 2
LOW = -1e30
F32 = jnp.float32
BF16 = jnp.bfloat16

NT = (((1,), (1,)), ((), ()))
TN = (((0,), (0,)), ((), ()))
NN = (((1,), (0,)), ((), ()))


def mm(a, b, dims):
    return lax.dot_general(a, b, dims, preferred_element_type=F32)


def upper():
    c = lax.broadcasted_iota(jnp.int32, (WIN, WIN), 0)
    r = lax.broadcasted_iota(jnp.int32, (WIN, WIN), 1)
    return c > r


def one_head(s, dp, sink, alive):
    top = jnp.maximum(jnp.max(s, axis=0, keepdims=True), sink)
    e = jnp.exp(s - top)
    sink_e = jnp.exp(sink - top)
    inv = 1.0 / (jnp.sum(e, axis=0, keepdims=True) + sink_e)
    if alive is not None:
        inv = jnp.where(alive, inv, 0.0)
    p = e * inv
    low = p.astype(BF16)
    delta = jnp.sum(low.astype(F32) * dp, axis=0, keepdims=True)
    ds = (p * (dp - delta)).astype(BF16)
    return low, ds, sink_e * inv * delta


def forward_group(sub, keys, values, q, d, seen_upper, sinks, first, bias, alive, low, ds, sink_out, sink_base):
    for pair in range(GROUP // 2):
        at = pair * 2 * HD
        q2 = jnp.concatenate([q[:, at : at + HD], q[:, at + HD : at + 2 * HD]], axis=0)
        d2 = jnp.concatenate([d[:, at : at + HD], d[:, at + HD : at + 2 * HD]], axis=0)
        s2 = mm(keys, q2, NT)
        dp2 = mm(values, d2, NT)
        for one in range(2):
            h = pair * 2 + one
            lanes = slice(one * WIN, (one + 1) * WIN)
            s_up = s2[:WIN, lanes]
            if bias is not None:
                s_up = s_up + bias
            s = jnp.where(seen_upper, s_up, s2[WIN:, lanes])
            dp = jnp.where(seen_upper, dp2[:WIN, lanes], dp2[WIN:, lanes])
            l_h, ds_h, sink_h = one_head(s, dp, sinks[first + h], alive)
            cols = slice(h * WIN, (h + 1) * WIN)
            low[sub, :, cols] = l_h
            ds[sub, :, cols] = ds_h
            sink_out[pl.ds(sink_base + h, 1), :] = sink_h


def stacked(rows):
    return jnp.concatenate([rows[:, h * HD : (h + 1) * HD] for h in range(GROUP)], axis=0)


def upper_mask():
    mask = jnp.where(upper(), 1.0, 0.0).astype(BF16)
    return jnp.concatenate([mask] * GROUP, axis=1)


def query_side(keys, ds_all):
    dqt = mm(keys, ds_all, TN).astype(BF16)
    parts = []
    for pair in range(GROUP // 2):
        at = pair * 2 * WIN
        two = jnp.concatenate([dqt[:, at : at + WIN], dqt[:, at + WIN : at + 2 * WIN]], axis=0)
        parts.append(two.T)
    return jnp.concatenate(parts, axis=1)


def one_hot(hit):
    return jnp.where(hit, 1.0, 0.0).astype(BF16)


def start_all(copies):
    for copy in copies:
        copy.start()


def carried(g, sources, targets, sems):
    copies = [pltpu.make_async_copy(src.at[g], dst.at[g], sems.at[2 * g + n]) for n, (src, dst) in enumerate(zip(sources, targets))]
    start_all(copies)
    return copies


def load_kernel(length, k_in, v_in, k_ref, v_ref, tail_ref, sems):
    copies = [pltpu.make_async_copy(src, dst, sems.at[n]) for n, (src, dst) in enumerate(((k_in, k_ref), (v_in, v_ref)))]
    start_all(copies)
    c = lax.broadcasted_iota(jnp.int32, (WIN, 2 * WIN), 0)
    j = lax.broadcasted_iota(jnp.int32, (WIN, 2 * WIN), 1)
    pick = one_hot(j == c + (length[0, 0, 0] - WIN))
    for copy, ref, part in zip(copies, (k_ref, v_ref), range(2)):
        copy.wait()
        tail_ref[part] = mm(pick, ref[...], NN).astype(BF16)


def late_kernel(length, sinks, k_ref, v_ref, q_in, d_in, q_ref, d_ref, low_out, ds_out, sink_ref, low, ds, sems, out_sems, *, first):
    copies = {}
    for at, rows in enumerate((slice(WIN, 2 * WIN), slice(0, WIN))):
        for g in range(PART):
            for n, (src, dst) in enumerate(((q_in, q_ref), (d_in, d_ref))):
                here = slice(g * GCOLS, (g + 1) * GCOLS)
                there = slice((first + g) * GCOLS, (first + g + 1) * GCOLS)
                copies[at, g, n] = pltpu.make_async_copy(src.at[rows, there], dst.at[rows, here], sems.at[(at * PART + g) * 2 + n])
                copies[at, g, n].start()
    seen_upper = upper()
    alive = lax.broadcasted_iota(jnp.int32, (1, WIN), 1) < length[0, 0, 0] - WIN
    written = []
    for g in range(PART):
        copies[0, g, 0].wait()
        copies[0, g, 1].wait()
        cols = slice(g * GCOLS, (g + 1) * GCOLS)
        kv = slice((first + g) * HD, (first + g + 1) * HD)
        keys = k_ref[:, kv] * (HD**-0.5)
        forward_group(g, keys, v_ref[:, kv], q_ref[WIN:, cols], d_ref[WIN:, cols], seen_upper, sinks, (first + g) * GROUP, None, alive, low, ds, sink_ref, g * GROUP)
        written += carried(g, (low, ds), (low_out, ds_out), out_sems)
    for g in range(PART):
        copies[1, g, 0].wait()
        copies[1, g, 1].wait()
    for copy in written:
        copy.wait()


def early_kernel(parent, branch, level, sinks, qa, qb, da, db, k_ref, v_ref, lo, mid, hi, late_a, late_b, low_out, ds_out, keys_ref, sink_ref, sink_rows, low, ds, out_sems):
    slot = parent[0, 0, 0] - branch[0] + 1
    bias = jnp.where(level[0] > 0, 0.0, LOW)
    seen_upper = upper()
    sink_rows[HQ:, :] = jnp.zeros((WIN - HQ, WIN), F32)
    written = []
    tail = jnp.where(slot == 0, lo[...], jnp.where(slot == 1, mid[...], hi[...]))
    for g in range(HK):
        q_ref, d_ref = ((qa, da), (qb, db))[g // PART]
        cols = slice(g % PART * GCOLS, (g % PART + 1) * GCOLS)
        kv = slice(g * HD, (g + 1) * HD)
        keys = jnp.concatenate([tail[0, :, kv], k_ref[:WIN, kv]], axis=0) * (HD**-0.5)
        values = jnp.concatenate([tail[1, :, kv], v_ref[:WIN, kv]], axis=0)
        keys_ref[:, kv] = keys
        forward_group(g, keys, values, q_ref[:WIN, cols], d_ref[:WIN, cols], seen_upper, sinks, g * GROUP, bias, None, low, ds, sink_rows, g * GROUP)
        written += carried(g, (low, ds), (low_out, ds_out), out_sems)
    half = HQ // 2
    sink_rows[:half, :] = sink_rows[:half, :] + late_a[...]
    sink_rows[half:HQ, :] = sink_rows[half:HQ, :] + late_b[...]
    total = -jnp.sum(sink_rows[...].T, axis=0, keepdims=True)
    sink_ref[...] = jnp.broadcast_to(total, sink_ref.shape)
    for copy in written:
        copy.wait()


def backward_group(g, q_ref, d_ref, cols, rows, low, ds, mask):
    ds_up = ds * mask
    ds_down = ds - ds_up
    low_up = low * mask
    low_down = low - low_up
    q8 = stacked(q_ref[rows, cols])
    d8 = stacked(d_ref[rows, cols])
    ds_all = jnp.concatenate([ds_up, ds_down], axis=0)
    low_all = jnp.concatenate([low_up, low_down], axis=0)
    return ds_all, mm(ds_all, q8, NN) * (HD**-0.5), mm(low_all, d8, NN)


def early_grads_kernel(parent, branch, qa, qb, da, db, keys_ref, low_in, ds_in, dq_out, own_ref, tail_ref, dq_ref, low, ds, sems, in_sems):
    came = [carried(g, (low_in, ds_in), (low, ds), in_sems) for g in range(HK)]
    mask = upper_mask()
    flag = (parent[0, 0, 0] - branch[0] + 2).astype(F32)
    row = lax.broadcasted_iota(jnp.int32, (WIN, HD), 0)
    rows = slice(0, WIN)
    copies = []
    for g in range(HK):
        q_ref, d_ref = ((qa, da), (qb, db))[g // PART]
        cols = slice(g % PART * GCOLS, (g % PART + 1) * GCOLS)
        kv = slice(g * HD, (g + 1) * HD)
        for copy in came[g]:
            copy.wait()
        ds_all, dk, dv = backward_group(g, q_ref, d_ref, cols, rows, low[g], ds[g], mask)
        tail_ref[0, :, kv] = jnp.where(row == 0, flag, dk[:WIN]).astype(BF16)
        tail_ref[1, :, kv] = dv[:WIN].astype(BF16)
        own_ref[0, :, kv] = dk[WIN:]
        own_ref[1, :, kv] = dv[WIN:]
        out = slice(g * GCOLS, (g + 1) * GCOLS)
        dq_ref[:, out] = query_side(keys_ref[:, kv], ds_all)
        copies.append(pltpu.make_async_copy(dq_ref.at[:, out], dq_out.at[rows, out], sems.at[g]))
        copies[-1].start()
    for copy in copies:
        copy.wait()


def late_grads_kernel(qa, qb, da, db, k_ref, low_a, low_b, ds_a, ds_b, dq_in, dq_out, own_ref, dq_ref, low, ds, sems, in_sems):
    del dq_in
    came = []
    for g in range(HK):
        low_in, ds_in = ((low_a, ds_a), (low_b, ds_b))[g // PART]
        for n, (src, dst) in enumerate(((low_in, low), (ds_in, ds))):
            came.append(pltpu.make_async_copy(src.at[g % PART], dst.at[g], in_sems.at[2 * g + n]))
    start_all(came)
    mask = upper_mask()
    rows = slice(WIN, 2 * WIN)
    copies = []
    for g in range(HK):
        q_ref, d_ref = ((qa, da), (qb, db))[g // PART]
        cols = slice(g % PART * GCOLS, (g % PART + 1) * GCOLS)
        kv = slice(g * HD, (g + 1) * HD)
        came[2 * g].wait()
        came[2 * g + 1].wait()
        ds_all, own_ref[0, :, kv], own_ref[1, :, kv] = backward_group(g, q_ref, d_ref, cols, rows, low[g], ds[g], mask)
        out = slice(g * GCOLS, (g + 1) * GCOLS)
        dq_ref[:, out] = query_side(k_ref[:, kv] * (HD**-0.5), ds_all)
        copies.append(pltpu.make_async_copy(dq_ref.at[:, out], dq_out.at[rows, out], sems.at[g]))
        copies[-1].start()
    for copy in copies:
        copy.wait()


def finish_kernel(length, own, early_own, lo, mid, hi, dk_ref, dv_ref):
    j = lax.broadcasted_iota(jnp.int32, (2 * WIN, WIN), 0)
    c = lax.broadcasted_iota(jnp.int32, (2 * WIN, WIN), 1)
    put = (j == c + (length[0, 0, 0] - WIN)) & (c > 0)
    picked = []
    for child, mark in ((lo, 3.0), (mid, 2.0), (hi, 1.0)):
        mine = jnp.max(child[0, :16, :WIN].astype(F32)[0:1, 0:1]) == mark
        picked.append(one_hot(put & mine))
    pick = jnp.concatenate(picked, axis=1)
    for part, out in enumerate((dk_ref, dv_ref)):
        children = jnp.concatenate([lo[part], mid[part], hi[part]], axis=0)
        total = own[part] + mm(pick, children, NN)
        out[:WIN, :] = (total[:WIN] + early_own[part]).astype(BF16)
        out[WIN:, :] = total[WIN:].astype(BF16)


def add_up_kernel(rows, out):
    out[...] = jnp.broadcast_to(jnp.sum(rows[...], axis=0, keepdims=True), out.shape)


SMEM = pl.BlockSpec(memory_space=pltpu.SMEM)
VMEM = pl.BlockSpec(memory_space=pltpu.VMEM)
RESULT = pl.BlockSpec(memory_space=pltpu.VMEM)
HBM = pl.BlockSpec(memory_space=pltpu.HBM)
PARAMS = pltpu.CompilerParams(vmem_limit_bytes=40 * 1024 * 1024)
KV = HK * HD
COLS = HQ * HD
DMA = pltpu.SemaphoreType.DMA
PACKED = (HK, WIN, GROUP * WIN)
PACKED_PART = (PART, WIN, GROUP * WIN)


def shaped(shape, dtype):
    return jax.ShapeDtypeStruct(shape, dtype)


def cost(products, size):
    return pl.CostEstimate(flops=products * 2 * 32 * 128 * 256 * 64, bytes_accessed=size, transcendentals=0)


SMALL = pl.CostEstimate(flops=1000, bytes_accessed=1000, transcendentals=0)


def held(operand, spec):
    space = {id(VMEM): pltpu.VMEM, id(HBM): pltpu.HBM}.get(id(spec), pl.ANY)
    return pltpu.with_memory_space_constraint(operand, space)


def made(spec, shape, dtype):
    space = {id(VMEM): pltpu.VMEM, id(HBM): pltpu.HBM}.get(id(spec), shaped)
    return space(shape, dtype)


def call(kernel, name, ins, outs, scratch, estimate, *operands, aliases=None):
    operands = [held(operand, spec) for operand, spec in zip(operands, ins)]
    return pl.pallas_call(
        kernel,
        in_specs=ins,
        out_specs=tuple(spec for spec, _, _ in outs),
        out_shape=tuple(made(*out) for out in outs),
        scratch_shapes=scratch,
        compiler_params=PARAMS,
        input_output_aliases=aliases or {},
        cost_estimate=estimate,
        name=name,
    )(*operands)


def load(length, k, v):
    return call(
        load_kernel,
        "load",
        [SMEM, HBM, HBM],
        [(VMEM, (2 * WIN, KV), BF16), (VMEM, (2 * WIN, KV), BF16), (VMEM, (2, WIN, KV), BF16)],
        [DMA((2,))],
        cost(1, 400_000),
        length, k, v,
    )


def late_rows(length, sinks, k, v, q, d, first):
    return call(
        functools.partial(late_kernel, first=first),
        "late_rows",
        [SMEM, SMEM, VMEM, VMEM, HBM, HBM],
        [
            (VMEM, (2 * WIN, COLS // 2), BF16),
            (VMEM, (2 * WIN, COLS // 2), BF16),
            (HBM, PACKED_PART, BF16),
            (HBM, PACKED_PART, BF16),
            (VMEM, (HQ // 2, WIN), F32),
        ],
        [pltpu.VMEM(PACKED_PART, BF16), pltpu.VMEM(PACKED_PART, BF16), DMA((4 * PART,)), DMA((2 * PART,))],
        cost(4, 2_500_000),
        length, sinks, k, v, q, d,
    )


def early_rows(parent, branch, level, sinks, qa, qb, da, db, k, v, lo, mid, hi, late_a, late_b, copies):
    return call(
        early_kernel,
        "early_rows",
        [SMEM] * 4 + [VMEM] * 11,
        [
            (HBM, PACKED, BF16),
            (HBM, PACKED, BF16),
            (VMEM, (2 * WIN, KV), BF16),
            (RESULT, (copies, WIN), F32),
        ],
        [pltpu.VMEM((WIN, WIN), F32), pltpu.VMEM(PACKED, BF16), pltpu.VMEM(PACKED, BF16), DMA((2 * HK,))],
        cost(4, 5_000_000),
        parent, branch, level, sinks, qa, qb, da, db, k, v, lo, mid, hi, late_a, late_b,
    )


def early_grads(parent, branch, qa, qb, da, db, keys, low, ds):
    return call(
        early_grads_kernel,
        "early_grads",
        [SMEM] * 2 + [VMEM] * 5 + [HBM] * 2,
        [(HBM, (2 * WIN, COLS), BF16), (VMEM, (2, WIN, KV), F32), (VMEM, (2, WIN, KV), BF16)],
        [pltpu.VMEM((WIN, COLS), BF16), pltpu.VMEM(PACKED, BF16), pltpu.VMEM(PACKED, BF16), DMA((HK,)), DMA((2 * HK,))],
        SMALL,
        parent, branch, qa, qb, da, db, keys, low, ds,
    )


def late_grads(qa, qb, da, db, k, low_a, low_b, ds_a, ds_b, dq):
    return call(
        late_grads_kernel,
        "late_grads",
        [VMEM] * 5 + [HBM] * 5,
        [(HBM, (2 * WIN, COLS), BF16), (VMEM, (2, 2 * WIN, KV), F32)],
        [pltpu.VMEM((WIN, COLS), BF16), pltpu.VMEM(PACKED, BF16), pltpu.VMEM(PACKED, BF16), DMA((HK,)), DMA((2 * HK,))],
        SMALL,
        qa, qb, da, db, k, low_a, low_b, ds_a, ds_b, dq,
        aliases={9: 0},
    )


def finish(length, own, early_own, lo, mid, hi):
    return call(
        finish_kernel,
        "finish",
        [SMEM] + [VMEM] * 5,
        [(RESULT, (2 * WIN, KV), BF16), (RESULT, (2 * WIN, KV), BF16)],
        [],
        SMALL,
        length, own, early_own, lo, mid, hi,
    )


def add_up(rows, copies):
    return call(add_up_kernel, "add_up", [VMEM], [(VMEM, (copies, WIN), F32)], [], cost(100, 100), rows)[0]


def moved(rows, axis, by):
    count = lax.axis_size(axis)
    pairs = [(i, i + by) for i in range(count) if 0 <= i + by < count]
    return lax.ppermute(rows, axis, pairs)


def raised(rows, by):
    levels, branches = lax.axis_size("ctx"), lax.axis_size("expert")
    pairs = [
        (level * branches + b, (level - 1) * branches + b + by)
        for level in range(1, levels)
        for b in range(branches)
        if 0 <= b + by < branches
    ]
    return lax.ppermute(rows, ("ctx", "expert"), pairs)


def shards(query_rows, key_rows, value_rows, output_grad, sink_logits, parent_branch, segment_length):
    q = query_rows[0, 0, 0]
    k = key_rows[0, 0, 0]
    v = value_rows[0, 0, 0]
    d = output_grad[0, 0, 0]
    branch = lax.axis_index("expert").astype(jnp.int32).reshape(1)
    level = lax.axis_index("ctx").astype(jnp.int32).reshape(1)
    plane = lax.axis_size("dp") * lax.axis_size("ctx")
    experts = lax.axis_size("expert")

    k, v, own_tail = load(segment_length, k, v)
    mid = moved(own_tail, "ctx", 1)
    qa, da, low_a, ds_a, late_a = late_rows(segment_length, sink_logits, k, v, q, d, 0)
    mid, late_a, parent = lax.optimization_barrier((mid, late_a, parent_branch))
    lo = moved(mid, "expert", 1)
    hi = moved(mid, "expert", -1)
    qb, db, low_b, ds_b, late_b = late_rows(segment_length, sink_logits, k, v, q, d, PART)
    low, ds, keys, sinks = early_rows(parent, branch, level, sink_logits, qa, qb, da, db, k, v, lo, mid, hi, late_a, late_b, experts)

    column = lax.all_to_all(sinks, "expert", 0, 0, tiled=True)
    dq, early_own, tail = early_grads(parent, branch, qa, qb, da, db, keys, low, ds)
    up = raised(tail, 0)
    dq, own = late_grads(qa, qb, da, db, k, low_a, low_b, ds_a, ds_b, dq)
    up_lo = raised(tail, 1)
    up_hi = raised(tail, -1)
    everywhere = lax.all_to_all(add_up(column, plane), ("dp", "ctx"), 0, 0, tiled=True)
    dk, dv = finish(segment_length, own, early_own, up_lo, up, up_hi)
    everywhere, dk = lax.optimization_barrier((everywhere, dk))
    sink_grad = jnp.sum(everywhere, axis=0)[:HQ]
    return dq[None, None, None], dk[None, None, None], dv[None, None, None], sink_grad


def solution(mesh):
    part = P("dp", "ctx", "expert", None, None)
    scalar = P("dp", "ctx", "expert")
    return jax.shard_map(
        shards,
        mesh=mesh,
        in_specs=(part, part, part, part, P(), scalar, scalar),
        out_specs=(part, part, part, P()),
        check_vma=False,
    )
```

time: 85.1 us -> 68.1 us (0.80)
  blocking collectives: 40.9 us -> 0 us
  starting transfers between devices: 19.4 us -> 36.3 us
  Pallas kernels: 13.6 us -> 23.5 us
  local copies, waits for them, and re-layouts: 4.96 us -> 0.65 us
  waiting for transfers between devices: 3.17 us -> 4.57 us
    all_to_all x2 -> x0, blocking collectives: 40.9 us -> none  [summed_over(): return jnp.sum(lax.all_to_all(copies, axes, 0, 0, tiled=True), axis=0)]
    all_to_all x0 -> x2, starting transfers between devices: none -> 20.4 us  [the longest x1 13.1 us: shards(): column = lax.all_to_all(sinks, 'expert', 0, 0, tiled=True)]
    pallas_call x5 -> x8, Pallas kernels: 13.6 us -> 23.5 us  [call(): pl.pallas_call(kernel, in_specs=ins, out_specs=tuple((spec for spec, _, _...]
    ppermute x6 -> x3, starting transfers between devices: 19.4 us -> 12 us  [moved(): return lax.ppermute(rows, axis, pairs)]
    all_to_all x0 -> x2, waiting for transfers between devices: none -> 4.56 us  [the longest x1 3.51 us: shards(): column = lax.all_to_all(sinks, 'expert', 0, 0, tiled=True)]
    unnamed x18 -> x2, local copies, waits for them, and re-layouts: 4.92 us -> 0.65 us
    ppermute x0 -> x3, starting transfers between devices: none -> 3.88 us  [raised(): return lax.ppermute(rows, ('ctx', 'expert'), pairs)]
    ppermute x6 -> x3, waiting for transfers between devices: 3.17 us -> 0.01 us  [moved(): return lax.ppermute(rows, axis, pairs)]
  transfers between devices with their start and end apart: 6 -> 8, of which waited for: 3 -> 2; matrix products, arithmetic and copies ran while one was open for 1% -> 0% of each run, Pallas kernels for 7% -> 26%
where the time goes in v3:
time: 68.1 us; the launch traced here: 67.6 us
  starting transfers between devices  36.3 us (53%)
  Pallas kernels  23.5 us (35%)
  waiting for transfers between devices  4.57 us (7%)
  between operations  2.1 us (3%)
    pallas_call x8, Pallas kernels, call(): pl.pallas_call(kernel, in_specs=ins, out_specs=tuple((spec for spec, _, _...  23.5 us
    all_to_all x1, starting transfers between devices, shards(): column = lax.all_to_all(sinks, 'expert', 0, 0, tiled=True)  13.1 us
    ppermute x3, starting transfers between devices, moved(): return lax.ppermute(rows, axis, pairs)  12 us
    all_to_all x1, starting transfers between devices, shards(): lax.all_to_all(add_up(column, plane), ('dp', 'ctx'), 0, 0, tiled=True)  7.36 us
    ppermute x3, starting transfers between devices, raised(): return lax.ppermute(rows, ('ctx', 'expert'), pairs)  3.88 us
    all_to_all x1, waiting for transfers between devices, shards(): column = lax.all_to_all(sinks, 'expert', 0, 0, tiled=True)  3.51 us
  transfers between devices with their start and end apart: 8, of which 2 were waited for; matrix products, arithmetic and copies ran while one was open for 0% of the time, Pallas kernels for 26%

profile of v3, /device:TPU:1, one launch (start us, length us, event | category | flops | bytes accessed | tf_op | source)
XLA Modules:
  0.0 67.6 jit_solution(13112510542226221554)
XLA Ops:
  1.3 1.3 %load.1 = (bf16[256,256]{1,0:T(8,128)(2,1)S(1)}, bf16[256,256]{1,0:T(8,128)(2,1)S(1)}, bf16[2,128,256]{2,1,0:T(8,128)(2,1)S(1)}) custom-call(s32[1,1,1]{2,1,0:T(1,128)S(6)} %copy.16.length, bf16[256,256]{1,0:T(8,128)(2,1)} %bitcast.26, bf16[256,256]{1,0:T(8,128)(2,1)} %bitcast.27), custom_call_target="tpu_custom_call" | custom-call | flops 134217728 | bytes 400000 | tf_op jit(solution)/shard_map/load/pallas_call | solution.py:288
  2.6 4.0 %collective-permute-start = (bf16[2,128,256]{2,1,0:T(8,128)(2,1)S(1)}, bf16[2,128,256]{2,1,0:T(8,128)(2,1)S(1)}, u32[]{:S(2)}, u32[]{:S(2)}) collective-permute-start(bf16[2,128,256]{2,1,0:T(8,128)(2,1)S(1)} %get-tuple-element.43), channel_id=1, source_target_pairs={{0,32},{32,64},{64,96},{1,33},{33,65},{65,97},{2,34},{34,66},{66,9... | collective-permute-start | bytes 393224 | tf_op jit(solution)/shard_map/ppermute | solution.py:392
  6.5 0.0 copy-start
  6.5 0.6 copy-done
  7.2 3.8 %late_rows.2 = (bf16[256,1024]{1,0:T(8,128)(2,1)S(1)}, bf16[256,1024]{1,0:T(8,128)(2,1)S(1)}, bf16[2,128,1024]{2,1,0:T(8,128)(2,1)}, bf16[2,128,1024]{2,1,0:T(8,128)(2,1)}, f32[16,128]{1,0:T(8,128)S(1)}) custom-call(s32[1,1,1]{2,1,0:T(1,128)S(6)} %copy.16.length, f32[32]{0:T(128)S(1)} %copy-done, bf16[256,256]{1,0:T(8,128)(2,1)S(1)} %get-tuple-element.33.k_ref, ...), custom_call_target="tpu_custom_call" | custom-call | flops 536870912 | bytes 2500000 | tf_op jit(solution)/shard_map/late_rows/pallas_call | solution.py:288
  11.0 6.1 %collective-permute-start.2 = (bf16[2,128,256]{2,1,0:T(8,128)(2,1)S(1)}, bf16[2,128,256]{2,1,0:T(8,128)(2,1)S(1)}, u32[]{:S(2)}, u32[]{:S(2)}) collective-permute-start(bf16[2,128,256]{2,1,0:T(8,128)(2,1)S(1)} %collective-permute-done.mid), channel_id=1, source_target_pairs={{1,0},{2,1},{3,2},{4,3},{5,4},{6,5},{7,6},{8,7},{9,8},{10,9},{11,1... | collective-permute-start | bytes 393224 | tf_op jit(solution)/shard_map/ppermute | solution.py:392
  17.2 1.9 %collective-permute-start.1 = (bf16[2,128,256]{2,1,0:T(8,128)(2,1)S(1)}, bf16[2,128,256]{2,1,0:T(8,128)(2,1)S(1)}, u32[]{:S(2)}, u32[]{:S(2)}) collective-permute-start(bf16[2,128,256]{2,1,0:T(8,128)(2,1)S(1)} %collective-permute-done.mid), channel_id=1, source_target_pairs={{0,1},{1,2},{2,3},{3,4},{4,5},{5,6},{6,7},{7,8},{8,9},{9,10},{10,1... | collective-permute-start | bytes 393224 | tf_op jit(solution)/shard_map/ppermute | solution.py:392
  19.7 3.8 %late_rows.3 = (bf16[256,1024]{1,0:T(8,128)(2,1)S(1)}, bf16[256,1024]{1,0:T(8,128)(2,1)S(1)}, bf16[2,128,1024]{2,1,0:T(8,128)(2,1)}, bf16[2,128,1024]{2,1,0:T(8,128)(2,1)}, f32[16,128]{1,0:T(8,128)S(1)}) custom-call(s32[1,1,1]{2,1,0:T(1,128)S(6)} %copy.16.length, f32[32]{0:T(128)S(1)} %copy-done, bf16[256,256]{1,0:T(8,128)(2,1)S(1)} %get-tuple-element.33.k_ref, ...), custom_call_target="tpu_custom_call" | custom-call | flops 536870912 | bytes 2500000 | tf_op jit(solution)/shard_map/late_rows/pallas_call | solution.py:288
  23.6 0.0 collective-permute-done.2.hi
  23.6 0.0 collective-permute-done.1.lo
  23.6 4.3 %early_rows.1 = (bf16[4,128,1024]{2,1,0:T(8,128)(2,1)}, bf16[4,128,1024]{2,1,0:T(8,128)(2,1)}, bf16[256,256]{1,0:T(8,128)(2,1)S(1)}, f32[32,128]{1,0:T(8,128)}) custom-call(s32[1,1,1]{2,1,0:T(1,128)S(6)} %copy.15.parent, s32[1]{0:T(128)} %bitcast.4.branch, s32[1]{0:T(128)} %bitcast.5.level, f32[32]{0:T(128)S(1)} %copy-done, ...), custom_call_target="tpu_custom_call" | custom-call | flops 536870912 | bytes 5000000 | tf_op jit(solution)/shard_map/early_rows/pallas_call | solution.py:288
  27.9 13.1 %all-to-all-start = ((f32[32,1,128]{2,1,0:T(1,128)}), f32[32,1,128]{2,1,0:T(1,128)S(1)}, u32[]{:S(2)}, u32[]{:S(2)}) async-start(f32[32,1,128]{2,1,0:T(1,128)} %bitcast.8), calls=%async_computation | async-start | bytes 32768 | tf_op jit(solution)/shard_map/all_to_all | solution.py:425
  41.0 4.3 %early_grads.1 = (bf16[256,2048]{1,0:T(8,128)(2,1)}, f32[2,128,256]{2,1,0:T(8,128)S(1)}, bf16[2,128,256]{2,1,0:T(8,128)(2,1)S(1)}) custom-call(s32[1,1,1]{2,1,0:T(1,128)S(6)} %copy.15.parent, s32[1]{0:T(128)} %bitcast.4.branch, bf16[256,1024]{1,0:T(8,128)(2,1)S(1)} %get-tuple-element.35.qa, bf16[256,1024]{1,0:T(8,128)(2,1)S(1)} %get-tuple-element.36.qb, ...), custom_call_target="tpu_custom_call" | custom-call | flops 1000 | bytes 1000 | tf_op jit(solution)/shard_map/early_grads/pallas_call | solution.py:288
  45.3 1.3 %collective-permute-start.5 = (bf16[2,128,256]{2,1,0:T(8,128)(2,1)S(1)}, bf16[2,128,256]{2,1,0:T(8,128)(2,1)S(1)}, u32[]{:S(2)}, u32[]{:S(2)}) collective-permute-start(bf16[2,128,256]{2,1,0:T(8,128)(2,1)S(1)} %get-tuple-element.57), channel_id=1, source_target_pairs={{33,0},{34,1},{35,2},{36,3},{37,4},{38,5},{39,6},{40,7},{41,8},{42... | collective-permute-start | bytes 393224 | tf_op jit(solution)/shard_map/ppermute | solution.py:403
  46.6 1.3 %collective-permute-start.4 = (bf16[2,128,256]{2,1,0:T(8,128)(2,1)S(1)}, bf16[2,128,256]{2,1,0:T(8,128)(2,1)S(1)}, u32[]{:S(2)}, u32[]{:S(2)}) collective-permute-start(bf16[2,128,256]{2,1,0:T(8,128)(2,1)S(1)} %get-tuple-element.57), channel_id=1, source_target_pairs={{32,0},{33,1},{34,2},{35,3},{36,4},{37,5},{38,6},{39,7},{40,8},{41... | collective-permute-start | bytes 393224 | tf_op jit(solution)/shard_map/ppermute | solution.py:403
  47.9 1.3 %collective-permute-start.3 = (bf16[2,128,256]{2,1,0:T(8,128)(2,1)S(1)}, bf16[2,128,256]{2,1,0:T(8,128)(2,1)S(1)}, u32[]{:S(2)}, u32[]{:S(2)}) collective-permute-start(bf16[2,128,256]{2,1,0:T(8,128)(2,1)S(1)} %get-tuple-element.57), channel_id=1, source_target_pairs={{32,1},{33,2},{34,3},{35,4},{36,5},{37,6},{38,7},{39,8},{40,9},{41... | collective-permute-start | bytes 393224 | tf_op jit(solution)/shard_map/ppermute | solution.py:403
  49.2 3.5 %all-to-all-done = f32[32,1,128]{2,1,0:T(1,128)S(1)} async-done(((f32[32,1,128]{2,1,0:T(1,128)}), f32[32,1,128]{2,1,0:T(1,128)S(1)}, u32[]{:S(2)}, u32[]{:S(2)}) %all-to-all-start) | async-done | bytes 16416 | tf_op jit(solution)/shard_map/all_to_all | solution.py:425
  52.7 0.6 add_up.1
  53.3 7.4 %all-to-all-start.1 = ((f32[16,1,128]{2,1,0:T(1,128)}), f32[16,1,128]{2,1,0:T(1,128)S(1)}, u32[]{:S(2)}, u32[]{:S(2)}) async-start(f32[16,1,128]{2,1,0:T(1,128)} %bitcast.11), calls=%async_computation.1 | async-start | bytes 16384 | tf_op jit(solution)/shard_map/all_to_all | solution.py:431
  60.7 4.3 %late_grads.1 = (bf16[256,2048]{1,0:T(8,128)(2,1)}, f32[2,256,256]{2,1,0:T(8,128)S(1)}) custom-call(bf16[256,1024]{1,0:T(8,128)(2,1)S(1)} %get-tuple-element.35.qa, bf16[256,1024]{1,0:T(8,128)(2,1)S(1)} %get-tuple-element.36.qb, bf16[256,1024]{1,0:T(8,128)(2,1)S(1)} %get-tuple-element.37.da, ...), custom_call_target="tpu_custom_call", output_to_operand_aliasing={{0}: (9, {})} | custom-call | flops 1000 | bytes 1000 | tf_op jit(solution)/shard_map/late_grads/pallas_call | solution.py:288
  65.0 0.0 collective-permute-done.4.mid
  65.0 1.0 %finish.1 = (bf16[256,256]{1,0:T(8,128)(2,1)}, bf16[256,256]{1,0:T(8,128)(2,1)}) custom-call(s32[1,1,1]{2,1,0:T(1,128)S(6)} %copy.16.length, f32[2,256,256]{2,1,0:T(8,128)S(1)} %get-tuple-element.55.own, f32[2,128,256]{2,1,0:T(8,128)S(1)} %get-tuple-element.56.early_own, bf16[2,128,256]{2,1,0:T(8,128)(2,1)S(1)} %collective-permute-done.3.lo, ...), custom_call_target="tpu_custom_call" | custom-call | flops 1000 | bytes 1000 | tf_op jit(solution)/shard_map/finish/pallas_call | solution.py:288
  66.0 1.1 %all-to-all-done.1 = f32[16,1,128]{2,1,0:T(1,128)S(1)} async-done(((f32[16,1,128]{2,1,0:T(1,128)}), f32[16,1,128]{2,1,0:T(1,128)S(1)}, u32[]{:S(2)}, u32[]{:S(2)}) %all-to-all-start.1) | async-done | bytes 8224 | tf_op jit(solution)/shard_map/all_to_all | solution.py:431
  67.1 0.5 reduce_sum.9
  (3 shorter events, 0.0 us)
Async XLA Ops:
  2.6 8.4 %collective-permute-start = (bf16[2,128,256]{2,1,0:T(8,128)(2,1)S(1)}, bf16[2,128,256]{2,1,0:T(8,128)(2,1)S(1)}, u32[]{:S(2)}, u32[]{:S(2)}) collective-permute-start(bf16[2,128,256]{2,1,0:T(8,128)(2,1)S(1)} %get-tuple-element.43), channel_id=1, source_target_pairs={{0,32},{32,64},{64,96},{1,33},{33,65},{65,97},{2,34},{34,66},{66,9... | collective-permute-start | bytes 393224 | tf_op jit(solution)/shard_map/ppermute | solution.py:392
  6.5 0.7 copy-start
  11.0 12.5 %collective-permute-start.2 = (bf16[2,128,256]{2,1,0:T(8,128)(2,1)S(1)}, bf16[2,128,256]{2,1,0:T(8,128)(2,1)S(1)}, u32[]{:S(2)}, u32[]{:S(2)}) collective-permute-start(bf16[2,128,256]{2,1,0:T(8,128)(2,1)S(1)} %collective-permute-done.mid), channel_id=1, source_target_pairs={{1,0},{2,1},{3,2},{4,3},{5,4},{6,5},{7,6},{8,7},{9,8},{10,9},{11,1... | collective-permute-start | bytes 393224 | tf_op jit(solution)/shard_map/ppermute | solution.py:392
  17.2 6.4 %collective-permute-start.1 = (bf16[2,128,256]{2,1,0:T(8,128)(2,1)S(1)}, bf16[2,128,256]{2,1,0:T(8,128)(2,1)S(1)}, u32[]{:S(2)}, u32[]{:S(2)}) collective-permute-start(bf16[2,128,256]{2,1,0:T(8,128)(2,1)S(1)} %collective-permute-done.mid), channel_id=1, source_target_pairs={{0,1},{1,2},{2,3},{3,4},{4,5},{5,6},{6,7},{7,8},{8,9},{9,10},{10,1... | collective-permute-start | bytes 393224 | tf_op jit(solution)/shard_map/ppermute | solution.py:392
  27.9 24.8 %all-to-all-start = ((f32[32,1,128]{2,1,0:T(1,128)}), f32[32,1,128]{2,1,0:T(1,128)S(1)}, u32[]{:S(2)}, u32[]{:S(2)}) async-start(f32[32,1,128]{2,1,0:T(1,128)} %bitcast.8), calls=%async_computation | async-start | bytes 32768 | tf_op jit(solution)/shard_map/all_to_all | solution.py:425
  45.3 19.7 %collective-permute-start.5 = (bf16[2,128,256]{2,1,0:T(8,128)(2,1)S(1)}, bf16[2,128,256]{2,1,0:T(8,128)(2,1)S(1)}, u32[]{:S(2)}, u32[]{:S(2)}) collective-permute-start(bf16[2,128,256]{2,1,0:T(8,128)(2,1)S(1)} %get-tuple-element.57), channel_id=1, source_target_pairs={{33,0},{34,1},{35,2},{36,3},{37,4},{38,5},{39,6},{40,7},{41,8},{42... | collective-permute-start | bytes 393224 | tf_op jit(solution)/shard_map/ppermute | solution.py:403
  46.6 18.4 %collective-permute-start.4 = (bf16[2,128,256]{2,1,0:T(8,128)(2,1)S(1)}, bf16[2,128,256]{2,1,0:T(8,128)(2,1)S(1)}, u32[]{:S(2)}, u32[]{:S(2)}) collective-permute-start(bf16[2,128,256]{2,1,0:T(8,128)(2,1)S(1)} %get-tuple-element.57), channel_id=1, source_target_pairs={{32,0},{33,1},{34,2},{35,3},{36,4},{37,5},{38,6},{39,7},{40,8},{41... | collective-permute-start | bytes 393224 | tf_op jit(solution)/shard_map/ppermute | solution.py:403
  47.9 17.1 %collective-permute-start.3 = (bf16[2,128,256]{2,1,0:T(8,128)(2,1)S(1)}, bf16[2,128,256]{2,1,0:T(8,128)(2,1)S(1)}, u32[]{:S(2)}, u32[]{:S(2)}) collective-permute-start(bf16[2,128,256]{2,1,0:T(8,128)(2,1)S(1)} %get-tuple-element.57), channel_id=1, source_target_pairs={{32,1},{33,2},{34,3},{35,4},{36,5},{37,6},{38,7},{39,8},{40,9},{41... | collective-permute-start | bytes 393224 | tf_op jit(solution)/shard_map/ppermute | solution.py:403
  53.3 13.8 %all-to-all-start.1 = ((f32[16,1,128]{2,1,0:T(1,128)}), f32[16,1,128]{2,1,0:T(1,128)S(1)}, u32[]{:S(2)}, u32[]{:S(2)}) async-start(f32[16,1,128]{2,1,0:T(1,128)} %bitcast.11), calls=%async_computation.1 | async-start | bytes 16384 | tf_op jit(solution)/shard_map/all_to_all | solution.py:431

commit v4 on v3

v4 whole, which is shorter than its diff:
```python
import functools

import jax
import jax.numpy as jnp
from jax import lax
from jax.experimental import pallas as pl
from jax.experimental.pallas import tpu as pltpu
from jax.sharding import PartitionSpec as P

HQ = 32
HK = 4
HD = 64
WIN = 128
GROUP = HQ // HK
GCOLS = GROUP * HD
LOW = -1e30
F32 = jnp.float32
BF16 = jnp.bfloat16

NT = (((1,), (1,)), ((), ()))
TN = (((0,), (0,)), ((), ()))
NN = (((1,), (0,)), ((), ()))


def mm(a, b, dims):
    return lax.dot_general(a, b, dims, preferred_element_type=F32)


def upper():
    c = lax.broadcasted_iota(jnp.int32, (WIN, WIN), 0)
    r = lax.broadcasted_iota(jnp.int32, (WIN, WIN), 1)
    return c > r


def one_head(s, dp, sink, alive):
    top = jnp.maximum(jnp.max(s, axis=0, keepdims=True), sink)
    e = jnp.exp(s - top)
    sink_e = jnp.exp(sink - top)
    inv = 1.0 / (jnp.sum(e, axis=0, keepdims=True) + sink_e)
    if alive is not None:
        inv = jnp.where(alive, inv, 0.0)
    p = e * inv
    low = p.astype(BF16)
    delta = jnp.sum(low.astype(F32) * dp, axis=0, keepdims=True)
    ds = (p * (dp - delta)).astype(BF16)
    return low, ds, sink_e * inv * delta


def forward_group(sub, keys, values, q, d, seen_upper, sinks, first, bias, alive, low, ds, sink_out, sink_base):
    for pair in range(GROUP // 2):
        at = pair * 2 * HD
        q2 = jnp.concatenate([q[:, at : at + HD], q[:, at + HD : at + 2 * HD]], axis=0)
        d2 = jnp.concatenate([d[:, at : at + HD], d[:, at + HD : at + 2 * HD]], axis=0)
        s2 = mm(keys, q2, NT)
        dp2 = mm(values, d2, NT)
        for one in range(2):
            h = pair * 2 + one
            lanes = slice(one * WIN, (one + 1) * WIN)
            s_up = s2[:WIN, lanes]
            if bias is not None:
                s_up = s_up + bias
            s = jnp.where(seen_upper, s_up, s2[WIN:, lanes])
            dp = jnp.where(seen_upper, dp2[:WIN, lanes], dp2[WIN:, lanes])
            l_h, ds_h, sink_h = one_head(s, dp, sinks[first + h], alive)
            cols = slice(h * WIN, (h + 1) * WIN)
            low[sub, :, cols] = l_h
            ds[sub, :, cols] = ds_h
            sink_out[pl.ds(sink_base + h, 1), :] = sink_h


def stacked(rows):
    return jnp.concatenate([rows[:, h * HD : (h + 1) * HD] for h in range(GROUP)], axis=0)


def upper_mask():
    mask = jnp.where(upper(), 1.0, 0.0).astype(BF16)
    return jnp.concatenate([mask] * GROUP, axis=1)


def query_side(keys, ds_all):
    dqt = mm(keys, ds_all, TN).astype(BF16)
    parts = []
    for pair in range(GROUP // 2):
        at = pair * 2 * WIN
        two = jnp.concatenate([dqt[:, at : at + WIN], dqt[:, at + WIN : at + 2 * WIN]], axis=0)
        parts.append(two.T)
    return jnp.concatenate(parts, axis=1)


def one_hot(hit):
    return jnp.where(hit, 1.0, 0.0).astype(BF16)


def start_all(copies):
    for copy in copies:
        copy.start()


def carried(g, sources, targets, sems):
    copies = [pltpu.make_async_copy(src.at[g], dst.at[g], sems.at[2 * g + n]) for n, (src, dst) in enumerate(zip(sources, targets))]
    start_all(copies)
    return copies


def columns_of(g, first, sources, targets, sems):
    cols = slice(g * GCOLS, (g + 1) * GCOLS)
    copies = [
        pltpu.make_async_copy(src.at[pl.ds(first, WIN), cols], dst.at[:, cols], sems.at[2 * g + n])
        for n, (src, dst) in enumerate(zip(sources, targets))
    ]
    start_all(copies)
    return copies


def load_kernel(length, k_in, v_in, q_in, d_in, k_ref, v_ref, tail_ref, q_first, d_first, sems, first_sems):
    copies = [pltpu.make_async_copy(src, dst, sems.at[n]) for n, (src, dst) in enumerate(((k_in, k_ref), (v_in, v_ref)))]
    start_all(copies)
    firsts = columns_of(0, WIN, (q_in, d_in), (q_first, d_first), first_sems)
    c = lax.broadcasted_iota(jnp.int32, (WIN, 2 * WIN), 0)
    j = lax.broadcasted_iota(jnp.int32, (WIN, 2 * WIN), 1)
    pick = one_hot(j == c + (length[0, 0, 0] - WIN))
    for copy, ref, part in zip(copies, (k_ref, v_ref), range(2)):
        copy.wait()
        tail_ref[part] = mm(pick, ref[...], NN).astype(BF16)
    for copy in firsts:
        copy.wait()


def late_kernel(length, sinks_in, k_ref, v_ref, q_first, d_first, q_in, d_in, q_early, d_early, q_last, d_last, low_out, ds_out, low_last, ds_last, sink_ref, q_ref, d_ref, low, ds, sinks, sems, early_sems, out_sems, sink_sem):
    sinks_copy = pltpu.make_async_copy(sinks_in, sinks, sink_sem)
    sinks_copy.start()
    came = {g: columns_of(g, WIN, (q_in, d_in), (q_ref, d_ref), sems) for g in range(1, LAST)}
    cols = slice(LAST * GCOLS, HK * GCOLS)
    came[LAST] = [
        pltpu.make_async_copy(src.at[pl.ds(WIN, WIN), cols], dst, sems.at[2 * LAST + n])
        for n, (src, dst) in enumerate(((q_in, q_last), (d_in, d_last)))
    ]
    brought = [
        pltpu.make_async_copy(src.at[pl.ds(0, WIN), :], dst, early_sems.at[n])
        for n, (src, dst) in enumerate(((q_in, q_early), (d_in, d_early)))
    ]
    start_all(came[LAST] + brought)
    seen_upper = upper()
    alive = lax.broadcasted_iota(jnp.int32, (1, WIN), 1) < length[0, 0, 0] - WIN
    written = []
    sinks_copy.wait()
    for g in range(HK):
        cols = slice(g * GCOLS, (g + 1) * GCOLS)
        kv = slice(g * HD, (g + 1) * HD)
        for copy in came.get(g, ()):
            copy.wait()
        if g == 0:
            q, d = q_first[...], d_first[...]
        elif g < LAST:
            q, d = q_ref[:, cols], d_ref[:, cols]
        else:
            q, d = q_last[...], d_last[...]
        to = (g, low, ds) if g < LAST else (0, low_last, ds_last)
        keys = k_ref[:, kv] * (HD**-0.5)
        forward_group(to[0], keys, v_ref[:, kv], q, d, seen_upper, sinks, g * GROUP, None, alive, to[1], to[2], sink_ref, g * GROUP)
        if g < LAST:
            written += carried(g, (low, ds), (low_out, ds_out), out_sems)
    for copy in brought + written:
        copy.wait()


def early_kernel(parent, branch, level, sinks_in, q_ref, d_ref, k_ref, v_ref, lo, mid, hi, late_sink, low_out, ds_out, low_last, ds_last, keys_ref, sink_ref, sink_rows, low, ds, sinks, out_sems, sink_sem):
    sinks_copy = pltpu.make_async_copy(sinks_in, sinks, sink_sem)
    sinks_copy.start()
    slot = parent[0, 0, 0] - branch[0] + 1
    bias = jnp.where(level[0] > 0, 0.0, LOW)
    seen_upper = upper()
    sink_rows[HQ:, :] = jnp.zeros((WIN - HQ, WIN), F32)
    written = []
    tail = jnp.where(slot == 0, lo[...], jnp.where(slot == 1, mid[...], hi[...]))
    sinks_copy.wait()
    for g in range(HK):
        cols = slice(g * GCOLS, (g + 1) * GCOLS)
        kv = slice(g * HD, (g + 1) * HD)
        keys = jnp.concatenate([tail[0, :, kv], k_ref[:WIN, kv]], axis=0) * (HD**-0.5)
        values = jnp.concatenate([tail[1, :, kv], v_ref[:WIN, kv]], axis=0)
        keys_ref[:, kv] = keys
        to = (g, low, ds) if g < LAST else (0, low_last, ds_last)
        forward_group(to[0], keys, values, q_ref[:, cols], d_ref[:, cols], seen_upper, sinks, g * GROUP, bias, None, to[1], to[2], sink_rows, g * GROUP)
        if g < LAST:
            written += carried(g, (low, ds), (low_out, ds_out), out_sems)
    sink_rows[:HQ, :] = sink_rows[:HQ, :] + late_sink[...]
    total = -jnp.sum(sink_rows[...].T, axis=0, keepdims=True)
    sink_ref[...] = jnp.broadcast_to(total, sink_ref.shape)
    for copy in written:
        copy.wait()


def one_side(keys, q, d, low, ds, mask):
    ds_up = ds * mask
    low_up = low * mask
    ds_all = jnp.concatenate([ds_up, ds - ds_up], axis=0)
    low_all = jnp.concatenate([low_up, low - low_up], axis=0)
    dk = mm(ds_all, stacked(q), NN) * (HD**-0.5)
    dv = mm(low_all, stacked(d), NN)
    return query_side(keys, ds_all), dk, dv


def early_grads_kernel(parent, branch, q_ref, d_ref, keys_ref, low_last, ds_last, low_in, ds_in, dq_out, own_ref, tail_ref, dq_ref, low, ds, sems, in_sems):
    came = [carried(g, (low_in, ds_in), (low, ds), in_sems) for g in range(LAST)]
    mask = upper_mask()
    flag = (parent[0, 0, 0] - branch[0] + 2).astype(F32)
    row = lax.broadcasted_iota(jnp.int32, (WIN, HD), 0)
    rows = slice(0, WIN)
    copies = []
    for g in (LAST,) + tuple(range(LAST)):
        cols = slice(g * GCOLS, (g + 1) * GCOLS)
        kv = slice(g * HD, (g + 1) * HD)
        if g < LAST:
            for copy in came[g]:
                copy.wait()
        low_g, ds_g = (low[g], ds[g]) if g < LAST else (low_last[0], ds_last[0])
        dq_ref[:, cols], dk, dv = one_side(keys_ref[:, kv], q_ref[:, cols], d_ref[:, cols], low_g, ds_g, mask)
        copies.append(pltpu.make_async_copy(dq_ref.at[:, cols], dq_out.at[rows, cols], sems.at[g]))
        copies[-1].start()
        tail_ref[0, :, kv] = jnp.where(row == 0, flag, dk[:WIN]).astype(BF16)
        tail_ref[1, :, kv] = dv[:WIN].astype(BF16)
        own_ref[0, :, kv] = dk[WIN:]
        own_ref[1, :, kv] = dv[WIN:]
    for copy in copies:
        copy.wait()


def late_grads_kernel(length, q_last, d_last, k_ref, own, lo, mid, hi, low_last, ds_last, q_in, d_in, low_in, ds_in, dq_in, dq_out, dk_ref, dv_ref, dq_ref, q_ref, d_ref, low, ds, sems, in_sems, q_sems):
    del dq_in
    came = []
    for g in range(LAST):
        came.append(carried(g, (low_in, ds_in), (low, ds), in_sems) + columns_of(g, WIN, (q_in, d_in), (q_ref, d_ref), q_sems))
    mask = upper_mask()
    j = lax.broadcasted_iota(jnp.int32, (2 * WIN, WIN), 0)
    c = lax.broadcasted_iota(jnp.int32, (2 * WIN, WIN), 1)
    put = (j == c + (length[0, 0, 0] - WIN)) & (c > 0)
    picked = []
    for child, mark in ((lo, 3.0), (mid, 2.0), (hi, 1.0)):
        mine = jnp.max(child[0, :16, :WIN].astype(F32)[0:1, 0:1]) == mark
        picked.append(one_hot(put & mine))
    pick = jnp.concatenate(picked, axis=1)
    sums = []
    for part in range(2):
        children = jnp.concatenate([lo[part], mid[part], hi[part]], axis=0)
        sums.append(mm(pick, children, NN))
    rows = slice(WIN, 2 * WIN)
    copies = []
    for g in (LAST,) + tuple(range(LAST)):
        cols = slice(g * GCOLS, (g + 1) * GCOLS)
        kv = slice(g * HD, (g + 1) * HD)
        if g < LAST:
            for copy in came[g]:
                copy.wait()
        if g < LAST:
            q_g, d_g, low_g, ds_g = q_ref[:, cols], d_ref[:, cols], low[g], ds[g]
        else:
            q_g, d_g, low_g, ds_g = q_last[...], d_last[...], low_last[0], ds_last[0]
        dq_ref[:, cols], dk, dv = one_side(k_ref[:, kv] * (HD**-0.5), q_g, d_g, low_g, ds_g, mask)
        copies.append(pltpu.make_async_copy(dq_ref.at[:, cols], dq_out.at[rows, cols], sems.at[g]))
        copies[-1].start()
        for part, (late, out) in enumerate(((dk, dk_ref), (dv, dv_ref))):
            total = late + sums[part][:, kv]
            out[:WIN, kv] = (total[:WIN] + own[part, :, kv]).astype(BF16)
            out[WIN:, kv] = total[WIN:].astype(BF16)
    for copy in copies:
        copy.wait()


def add_up_kernel(rows, out):
    out[...] = jnp.broadcast_to(jnp.sum(rows[...], axis=0, keepdims=True), out.shape)


SMEM = pl.BlockSpec(memory_space=pltpu.SMEM)
VMEM = pl.BlockSpec(memory_space=pltpu.VMEM)
RESULT = pl.BlockSpec(memory_space=pltpu.VMEM)
HBM = pl.BlockSpec(memory_space=pltpu.HBM)
PARAMS = pltpu.CompilerParams(vmem_limit_bytes=40 * 1024 * 1024)
KV = HK * HD
COLS = HQ * HD
DMA = pltpu.SemaphoreType.DMA
LAST = HK - 1
PACKED = (LAST, WIN, GROUP * WIN)
PACKED_LAST = (1, WIN, GROUP * WIN)


def shaped(shape, dtype):
    return jax.ShapeDtypeStruct(shape, dtype)


def cost(products, size):
    return pl.CostEstimate(flops=products * 2 * 32 * 128 * 256 * 64, bytes_accessed=size, transcendentals=0)


SMALL = pl.CostEstimate(flops=1000, bytes_accessed=1000, transcendentals=0)


def held(operand, spec):
    space = {id(VMEM): pltpu.VMEM, id(HBM): pltpu.HBM}.get(id(spec), pl.ANY)
    return pltpu.with_memory_space_constraint(operand, space)


def made(spec, shape, dtype):
    space = {id(VMEM): pltpu.VMEM, id(HBM): pltpu.HBM}.get(id(spec), shaped)
    return space(shape, dtype)


def call(kernel, name, ins, outs, scratch, estimate, *operands, aliases=None):
    operands = [held(operand, spec) for operand, spec in zip(operands, ins)]
    return pl.pallas_call(
        kernel,
        in_specs=ins,
        out_specs=tuple(spec for spec, _, _ in outs),
        out_shape=tuple(made(*out) for out in outs),
        scratch_shapes=scratch,
        compiler_params=PARAMS,
        input_output_aliases=aliases or {},
        cost_estimate=estimate,
        name=name,
    )(*operands)


def load(length, k, v, q, d):
    return call(
        load_kernel,
        "load",
        [SMEM] + [HBM] * 4,
        [
            (VMEM, (2 * WIN, KV), BF16),
            (VMEM, (2 * WIN, KV), BF16),
            (VMEM, (2, WIN, KV), BF16),
            (VMEM, (WIN, GCOLS), BF16),
            (VMEM, (WIN, GCOLS), BF16),
        ],
        [DMA((2,)), DMA((2,))],
        cost(1, 400_000),
        length, k, v, q, d,
    )


def late_rows(length, sinks, k, v, q_first, d_first, q, d):
    return call(
        late_kernel,
        "late_rows",
        [SMEM, HBM] + [VMEM] * 4 + [HBM] * 2,
        [
            (VMEM, (WIN, COLS), BF16),
            (VMEM, (WIN, COLS), BF16),
            (VMEM, (WIN, GCOLS), BF16),
            (VMEM, (WIN, GCOLS), BF16),
            (HBM, PACKED, BF16),
            (HBM, PACKED, BF16),
            (VMEM, PACKED_LAST, BF16),
            (VMEM, PACKED_LAST, BF16),
            (VMEM, (HQ, WIN), F32),
        ],
        [pltpu.VMEM((WIN, COLS), BF16)] * 2
        + [pltpu.VMEM(PACKED, BF16)] * 2
        + [pltpu.SMEM((HQ,), F32), DMA((2 * HK,)), DMA((2,)), DMA((2 * HK,)), DMA],
        cost(4, 2_500_000),
        length, sinks, k, v, q_first, d_first, q, d,
    )


def early_rows(parent, branch, level, sinks, q, d, k, v, lo, mid, hi, late_sink, copies):
    return call(
        early_kernel,
        "early_rows",
        [SMEM] * 3 + [HBM] + [VMEM] * 8,
        [
            (HBM, PACKED, BF16),
            (HBM, PACKED, BF16),
            (VMEM, PACKED_LAST, BF16),
            (VMEM, PACKED_LAST, BF16),
            (VMEM, (2 * WIN, KV), BF16),
            (RESULT, (copies, WIN), F32),
        ],
        [
            pltpu.VMEM((WIN, WIN), F32),
            pltpu.VMEM(PACKED, BF16),
            pltpu.VMEM(PACKED, BF16),
            pltpu.SMEM((HQ,), F32),
            DMA((2 * HK,)),
            DMA,
        ],
        cost(4, 5_000_000),
        parent, branch, level, sinks, q, d, k, v, lo, mid, hi, late_sink,
    )


def early_grads(parent, branch, q, d, keys, low_last, ds_last, low, ds):
    return call(
        early_grads_kernel,
        "early_grads",
        [SMEM] * 2 + [VMEM] * 5 + [HBM] * 2,
        [(HBM, (2 * WIN, COLS), BF16), (VMEM, (2, WIN, KV), F32), (VMEM, (2, WIN, KV), BF16)],
        [pltpu.VMEM((WIN, COLS), BF16), pltpu.VMEM(PACKED, BF16), pltpu.VMEM(PACKED, BF16), DMA((HK,)), DMA((2 * HK,))],
        SMALL,
        parent, branch, q, d, keys, low_last, ds_last, low, ds,
    )


def late_grads(length, q_last, d_last, k, own, lo, mid, hi, low_last, ds_last, q, d, low, ds, dq):
    return call(
        late_grads_kernel,
        "late_grads",
        [SMEM] + [VMEM] * 9 + [HBM] * 5,
        [(HBM, (2 * WIN, COLS), BF16), (RESULT, (2 * WIN, KV), BF16), (RESULT, (2 * WIN, KV), BF16)],
        [pltpu.VMEM((WIN, COLS), BF16)] * 3
        + [pltpu.VMEM(PACKED, BF16)] * 2
        + [DMA((HK,)), DMA((2 * HK,)), DMA((2 * HK,))],
        SMALL,
        length, q_last, d_last, k, own, lo, mid, hi, low_last, ds_last, q, d, low, ds, dq,
        aliases={14: 0},
    )


def add_up(rows, copies):
    return call(add_up_kernel, "add_up", [VMEM], [(VMEM, (copies, WIN), F32)], [], cost(100, 100), rows)[0]


def sent(rows, levels_on, by):
    levels, branches = lax.axis_size("ctx"), lax.axis_size("expert")
    pairs = [
        (level * branches + b, (level + levels_on) * branches + b + by)
        for level in range(levels)
        for b in range(branches)
        if 0 <= level + levels_on < levels and 0 <= b + by < branches
    ]
    return lax.ppermute(rows, ("ctx", "expert"), pairs)


def shards(query_rows, key_rows, value_rows, output_grad, sink_logits, parent_branch, segment_length):
    q = query_rows[0, 0, 0]
    k = key_rows[0, 0, 0]
    v = value_rows[0, 0, 0]
    d = output_grad[0, 0, 0]
    branch = lax.axis_index("expert").astype(jnp.int32).reshape(1)
    level = lax.axis_index("ctx").astype(jnp.int32).reshape(1)
    plane = lax.axis_size("dp") * lax.axis_size("ctx")
    experts = lax.axis_size("expert")

    k, v, tail, q_first, d_first = load(segment_length, k, v, q, d)
    tail, parent = lax.optimization_barrier((tail, parent_branch))
    length = segment_length
    mid, lo, hi = (sent(tail, 1, by) for by in (0, 1, -1))
    q_e, d_e, q_l3, d_l3, low_l, ds_l, low_l3, ds_l3, late_sink = late_rows(length, sink_logits, k, v, q_first, d_first, q, d)
    low_e, ds_e, low_e3, ds_e3, keys, sinks = early_rows(parent, branch, level, sink_logits, q_e, d_e, k, v, lo, mid, hi, late_sink, experts)

    column = lax.all_to_all(sinks, "expert", 0, 0, tiled=True)
    dq, early_own, tail = early_grads(parent, branch, q_e, d_e, keys, low_e3, ds_e3, low_e, ds_e)
    mid, lo, hi = (sent(tail, -1, by) for by in (0, 1, -1))
    everywhere = lax.all_to_all(add_up(column, plane), ("dp", "ctx"), 0, 0, tiled=True)
    dq, dk, dv = late_grads(length, q_l3, d_l3, k, early_own, lo, mid, hi, low_l3, ds_l3, q, d, low_l, ds_l, dq)
    everywhere, dk = lax.optimization_barrier((everywhere, dk))
    sink_grad = jnp.sum(everywhere, axis=0)[:HQ]
    return dq[None, None, None], dk[None, None, None], dv[None, None, None], sink_grad


def solution(mesh):
    part = P("dp", "ctx", "expert", None, None)
    scalar = P("dp", "ctx", "expert")
    return jax.shard_map(
        shards,
        mesh=mesh,
        in_specs=(part, part, part, part, P(), scalar, scalar),
        out_specs=(part, part, part, P()),
        check_vma=False,
    )
```

time: 68.1 us -> 65 us (0.954)
  Pallas kernels: 23.5 us -> 18.8 us
  waiting for transfers between devices: 4.57 us -> 5.77 us
  starting transfers between devices: 36.3 us -> 37.4 us
    pallas_call x8 -> x6, Pallas kernels: 23.5 us -> 18.8 us  [call(): pl.pallas_call(kernel, in_specs=ins, out_specs=tuple((spec for spec, _, _...]
    all_to_all x1, starting transfers between devices: 13.1 us -> 15.4 us  [shards(): column = lax.all_to_all(sinks, 'expert', 0, 0, tiled=True)]
  transfers between devices with their start and end apart: 8 -> 8, of which waited for: 2 -> 2; matrix products, arithmetic and copies ran while one was open for 0% -> 0% of each run, Pallas kernels for 26% -> 20%
where the time goes in v4:
time: 65 us; the launch traced here: 64.5 us
  starting transfers between devices  37.4 us (58%)
  Pallas kernels  18.8 us (29%)
  waiting for transfers between devices  5.77 us (9%)
  between operations  2.08 us (3%)
    pallas_call x6, Pallas kernels, call(): pl.pallas_call(kernel, in_specs=ins, out_specs=tuple((spec for spec, _, _...  18.8 us
    all_to_all x1, starting transfers between devices, shards(): column = lax.all_to_all(sinks, 'expert', 0, 0, tiled=True)  15.4 us
    ppermute x6, starting transfers between devices, sent(): return lax.ppermute(rows, ('ctx', 'expert'), pairs)  15.2 us
    all_to_all x1, starting transfers between devices, shards(): lax.all_to_all(add_up(column, plane), ('dp', 'ctx'), 0, 0, tiled=True)  6.75 us
    all_to_all x1, waiting for transfers between devices, shards(): column = lax.all_to_all(sinks, 'expert', 0, 0, tiled=True)  4.12 us
    all_to_all x1, waiting for transfers between devices, shards(): lax.all_to_all(add_up(column, plane), ('dp', 'ctx'), 0, 0, tiled=True)  1.64 us
  transfers between devices with their start and end apart: 8, of which 2 were waited for; matrix products, arithmetic and copies ran while one was open for 0% of the time, Pallas kernels for 20%

profile of v4, /device:TPU:1, one launch (start us, length us, event | category | flops | bytes accessed | tf_op | source)
XLA Modules:
  0.0 64.5 jit_solution(7759733499022920511)
XLA Ops:
  1.3 1.3 %load.1 = (bf16[256,256]{1,0:T(8,128)(2,1)S(1)}, bf16[256,256]{1,0:T(8,128)(2,1)S(1)}, bf16[2,128,256]{2,1,0:T(8,128)(2,1)S(1)}, bf16[128,512]{1,0:T(8,128)(2,1)S(1)}, bf16[128,512]{1,0:T(8,128)(2,1)S(1)}) custom-call(s32[1,1,1]{2,1,0:T(1,128)S(6)} %copy.16.length, bf16[256,256]{1,0:T(8,128)(2,1)} %bitcast.26, bf16[256,256]{1,0:T(8,128)(2,1)} %bitcast.27, ...), custom_call_target="tpu_custom_call" | custom-call | flops 134217728 | bytes 400000 | tf_op jit(solution)/shard_map/load/pallas_call | solution.py:310
  2.6 4.5 %collective-permute-start.2 = (bf16[2,128,256]{2,1,0:T(8,128)(2,1)S(1)}, bf16[2,128,256]{2,1,0:T(8,128)(2,1)S(1)}, u32[]{:S(2)}, u32[]{:S(2)}) collective-permute-start(bf16[2,128,256]{2,1,0:T(8,128)(2,1)S(1)} %get-tuple-element.44), channel_id=1, source_target_pairs={{1,32},{2,33},{3,34},{4,35},{5,36},{6,37},{7,38},{8,39},{9,40},{10... | collective-permute-start | bytes 393224 | tf_op jit(solution)/shard_map/ppermute | solution.py:430
  7.1 3.1 %collective-permute-start.1 = (bf16[2,128,256]{2,1,0:T(8,128)(2,1)S(1)}, bf16[2,128,256]{2,1,0:T(8,128)(2,1)S(1)}, u32[]{:S(2)}, u32[]{:S(2)}) collective-permute-start(bf16[2,128,256]{2,1,0:T(8,128)(2,1)S(1)} %get-tuple-element.44), channel_id=1, source_target_pairs={{0,32},{1,33},{2,34},{3,35},{4,36},{5,37},{6,38},{7,39},{8,40},{9,... | collective-permute-start | bytes 393224 | tf_op jit(solution)/shard_map/ppermute | solution.py:430
  10.2 3.7 %collective-permute-start = (bf16[2,128,256]{2,1,0:T(8,128)(2,1)S(1)}, bf16[2,128,256]{2,1,0:T(8,128)(2,1)S(1)}, u32[]{:S(2)}, u32[]{:S(2)}) collective-permute-start(bf16[2,128,256]{2,1,0:T(8,128)(2,1)S(1)} %get-tuple-element.44), channel_id=1, source_target_pairs={{0,33},{1,34},{2,35},{3,36},{4,37},{5,38},{6,39},{7,40},{8,41},{9,... | collective-permute-start | bytes 393224 | tf_op jit(solution)/shard_map/ppermute | solution.py:430
  14.6 3.9 %late_rows.1 = (bf16[128,2048]{1,0:T(8,128)(2,1)S(1)}, bf16[128,2048]{1,0:T(8,128)(2,1)S(1)}, bf16[128,512]{1,0:T(8,128)(2,1)S(1)}, bf16[128,512]{1,0:T(8,128)(2...) custom-call(s32[1,1,1]{2,1,0:T(1,128)S(6)} %copy.16.length, ...), custom_call_target="tpu_custom_call" | custom-call | flops 536870912 | bytes 2500000 | tf_op jit(solution)/shard_map/late_rows/pallas_call | solution.py:310
  18.5 0.0 collective-permute-done.2.hi
  18.5 0.0 collective-permute-done.1.mid
  18.5 0.0 collective-permute-done.lo
  18.5 4.6 %early_rows.1 = (bf16[3,128,1024]{2,1,0:T(8,128)(2,1)}, bf16[3,128,1024]{2,1,0:T(8,128)(2,1)}, bf16[1,128,1024]{2,1,0:T(8,128)(2,1)S(1)}, bf16[1,128,1024]{2,1,0...) custom-call(s32[1,1,1]{2,1,0:T(1,128)S(6)} %copy.15.parent, s32[1]{0:T(128)} %bitcast.4.branch, ...), custom_call_target="tpu_custom_call" | custom-call | flops 536870912 | bytes 5000000 | tf_op jit(solution)/shard_map/early_rows/pallas_call | solution.py:310
  23.1 15.4 %all-to-all-start = ((f32[32,1,128]{2,1,0:T(1,128)}), f32[32,1,128]{2,1,0:T(1,128)S(1)}, u32[]{:S(2)}, u32[]{:S(2)}) async-start(f32[32,1,128]{2,1,0:T(1,128)} %bitcast.8), calls=%async_computation | async-start | bytes 32768 | tf_op jit(solution)/shard_map/all_to_all | solution.py:450
  38.5 3.7 %early_grads.1 = (bf16[256,2048]{1,0:T(8,128)(2,1)}, f32[2,128,256]{2,1,0:T(8,128)S(1)}, bf16[2,128,256]{2,1,0:T(8,128)(2,1)S(1)}) custom-call(s32[1,1,1]{2,1,0:T(1,128)S(6)} %copy.15.parent, s32[1]{0:T(128)} %bitcast.4.branch, bf16[128,2048]{1,0:T(8,128)(2,1)S(1)} %get-tuple-element.42.q_ref, bf16[128,2048]{1,0:T(8,128)(2,1)S(1)} %get-tuple-element.43.d_ref, ...), custom_call_target="tpu_custom_call" | custom-call | flops 1000 | bytes 1000 | tf_op jit(solution)/shard_map/early_grads/pallas_call | solution.py:310
  42.2 1.3 %collective-permute-start.5 = (bf16[2,128,256]{2,1,0:T(8,128)(2,1)S(1)}, bf16[2,128,256]{2,1,0:T(8,128)(2,1)S(1)}, u32[]{:S(2)}, u32[]{:S(2)}) collective-permute-start(bf16[2,128,256]{2,1,0:T(8,128)(2,1)S(1)} %get-tuple-element.52), channel_id=1, source_target_pairs={{33,0},{34,1},{35,2},{36,3},{37,4},{38,5},{39,6},{40,7},{41,8},{42... | collective-permute-start | bytes 393224 | tf_op jit(solution)/shard_map/ppermute | solution.py:430
  43.5 1.3 %collective-permute-start.4 = (bf16[2,128,256]{2,1,0:T(8,128)(2,1)S(1)}, bf16[2,128,256]{2,1,0:T(8,128)(2,1)S(1)}, u32[]{:S(2)}, u32[]{:S(2)}) collective-permute-start(bf16[2,128,256]{2,1,0:T(8,128)(2,1)S(1)} %get-tuple-element.52), channel_id=1, source_target_pairs={{32,0},{33,1},{34,2},{35,3},{36,4},{37,5},{38,6},{39,7},{40,8},{41... | collective-permute-start | bytes 393224 | tf_op jit(solution)/shard_map/ppermute | solution.py:430
  44.8 1.3 %collective-permute-start.3 = (bf16[2,128,256]{2,1,0:T(8,128)(2,1)S(1)}, bf16[2,128,256]{2,1,0:T(8,128)(2,1)S(1)}, u32[]{:S(2)}, u32[]{:S(2)}) collective-permute-start(bf16[2,128,256]{2,1,0:T(8,128)(2,1)S(1)} %get-tuple-element.52), channel_id=1, source_target_pairs={{32,1},{33,2},{34,3},{35,4},{36,5},{37,6},{38,7},{39,8},{40,9},{41... | collective-permute-start | bytes 393224 | tf_op jit(solution)/shard_map/ppermute | solution.py:430
  46.1 4.1 %all-to-all-done = f32[32,1,128]{2,1,0:T(1,128)S(1)} async-done(((f32[32,1,128]{2,1,0:T(1,128)}), f32[32,1,128]{2,1,0:T(1,128)S(1)}, u32[]{:S(2)}, u32[]{:S(2)}) %all-to-all-start) | async-done | bytes 16416 | tf_op jit(solution)/shard_map/all_to_all | solution.py:450
  50.2 0.6 add_up.1
  50.8 6.7 %all-to-all-start.1 = ((f32[16,1,128]{2,1,0:T(1,128)}), f32[16,1,128]{2,1,0:T(1,128)S(1)}, u32[]{:S(2)}, u32[]{:S(2)}) async-start(f32[16,1,128]{2,1,0:T(1,128)} %bitcast.11), calls=%async_computation.1 | async-start | bytes 16384 | tf_op jit(solution)/shard_map/all_to_all | solution.py:453
  57.6 0.0 collective-permute-done.5.hi
  57.6 0.0 collective-permute-done.4.mid
  57.6 0.0 collective-permute-done.3.lo
  57.6 4.7 %late_grads.1 = (bf16[256,2048]{1,0:T(8,128)(2,1)}, bf16[256,256]{1,0:T(8,128)(2,1)}, bf16[256,256]{1,0:T(8,128)(2,1)}) custom-call(s32[1,1,1]{2,1,0:T(1,128)S(6)} %copy.16.length, bf16[128,512]{1,0:T(8,128)(2,1)S(1)} %get-tuple-element.38.q_last, bf16[128,512]{1,0:T(8,128)(2,1)S(1)} %get-tuple-element.39.d_last, ...), custom_call_target="tpu_custom_call", output_to_operand_aliasing={{0}: (14, {})} | custom-call | flops 1000 | bytes 1000 | tf_op jit(solution)/shard_map/late_grads/pallas_call | solution.py:310
  62.4 1.6 %all-to-all-done.1 = f32[16,1,128]{2,1,0:T(1,128)S(1)} async-done(((f32[16,1,128]{2,1,0:T(1,128)}), f32[16,1,128]{2,1,0:T(1,128)S(1)}, u32[]{:S(2)}, u32[]{:S(2)}) %all-to-all-start.1) | async-done | bytes 8224 | tf_op jit(solution)/shard_map/all_to_all | solution.py:453
  64.0 0.5 reduce_sum.9
Async XLA Ops:
  2.6 15.9 %collective-permute-start.2 = (bf16[2,128,256]{2,1,0:T(8,128)(2,1)S(1)}, bf16[2,128,256]{2,1,0:T(8,128)(2,1)S(1)}, u32[]{:S(2)}, u32[]{:S(2)}) collective-permute-start(bf16[2,128,256]{2,1,0:T(8,128)(2,1)S(1)} %get-tuple-element.44), channel_id=1, source_target_pairs={{1,32},{2,33},{3,34},{4,35},{5,36},{6,37},{7,38},{8,39},{9,40},{10... | collective-permute-start | bytes 393224 | tf_op jit(solution)/shard_map/ppermute | solution.py:430
  7.1 11.4 %collective-permute-start.1 = (bf16[2,128,256]{2,1,0:T(8,128)(2,1)S(1)}, bf16[2,128,256]{2,1,0:T(8,128)(2,1)S(1)}, u32[]{:S(2)}, u32[]{:S(2)}) collective-permute-start(bf16[2,128,256]{2,1,0:T(8,128)(2,1)S(1)} %get-tuple-element.44), channel_id=1, source_target_pairs={{0,32},{1,33},{2,34},{3,35},{4,36},{5,37},{6,38},{7,39},{8,40},{9,... | collective-permute-start | bytes 393224 | tf_op jit(solution)/shard_map/ppermute | solution.py:430
  10.2 8.3 %collective-permute-start = (bf16[2,128,256]{2,1,0:T(8,128)(2,1)S(1)}, bf16[2,128,256]{2,1,0:T(8,128)(2,1)S(1)}, u32[]{:S(2)}, u32[]{:S(2)}) collective-permute-start(bf16[2,128,256]{2,1,0:T(8,128)(2,1)S(1)} %get-tuple-element.44), channel_id=1, source_target_pairs={{0,33},{1,34},{2,35},{3,36},{4,37},{5,38},{6,39},{7,40},{8,41},{9,... | collective-permute-start | bytes 393224 | tf_op jit(solution)/shard_map/ppermute | solution.py:430
  23.1 27.1 %all-to-all-start = ((f32[32,1,128]{2,1,0:T(1,128)}), f32[32,1,128]{2,1,0:T(1,128)S(1)}, u32[]{:S(2)}, u32[]{:S(2)}) async-start(f32[32,1,128]{2,1,0:T(1,128)} %bitcast.8), calls=%async_computation | async-start | bytes 32768 | tf_op jit(solution)/shard_map/all_to_all | solution.py:450
  42.2 15.4 %collective-permute-start.5 = (bf16[2,128,256]{2,1,0:T(8,128)(2,1)S(1)}, bf16[2,128,256]{2,1,0:T(8,128)(2,1)S(1)}, u32[]{:S(2)}, u32[]{:S(2)}) collective-permute-start(bf16[2,128,256]{2,1,0:T(8,128)(2,1)S(1)} %get-tuple-element.52), channel_id=1, source_target_pairs={{33,0},{34,1},{35,2},{36,3},{37,4},{38,5},{39,6},{40,7},{41,8},{42... | collective-permute-start | bytes 393224 | tf_op jit(solution)/shard_map/ppermute | solution.py:430
  43.5 14.1 %collective-permute-start.4 = (bf16[2,128,256]{2,1,0:T(8,128)(2,1)S(1)}, bf16[2,128,256]{2,1,0:T(8,128)(2,1)S(1)}, u32[]{:S(2)}, u32[]{:S(2)}) collective-permute-start(bf16[2,128,256]{2,1,0:T(8,128)(2,1)S(1)} %get-tuple-element.52), channel_id=1, source_target_pairs={{32,0},{33,1},{34,2},{35,3},{36,4},{37,5},{38,6},{39,7},{40,8},{41... | collective-permute-start | bytes 393224 | tf_op jit(solution)/shard_map/ppermute | solution.py:430
  44.8 12.8 %collective-permute-start.3 = (bf16[2,128,256]{2,1,0:T(8,128)(2,1)S(1)}, bf16[2,128,256]{2,1,0:T(8,128)(2,1)S(1)}, u32[]{:S(2)}, u32[]{:S(2)}) collective-permute-start(bf16[2,128,256]{2,1,0:T(8,128)(2,1)S(1)} %get-tuple-element.52), channel_id=1, source_target_pairs={{32,1},{33,2},{34,3},{35,4},{36,5},{37,6},{38,7},{39,8},{40,9},{41... | collective-permute-start | bytes 393224 | tf_op jit(solution)/shard_map/ppermute | solution.py:430
  50.8 13.2 %all-to-all-start.1 = ((f32[16,1,128]{2,1,0:T(1,128)}), f32[16,1,128]{2,1,0:T(1,128)S(1)}, u32[]{:S(2)}, u32[]{:S(2)}) async-start(f32[16,1,128]{2,1,0:T(1,128)} %bitcast.11), calls=%async_computation.1 | async-start | bytes 16384 | tf_op jit(solution)/shard_map/all_to_all | solution.py:453

commit v5 on v4

--- a/solution.py
+++ b/solution.py
@@ -61,7 +61,7 @@
                 s_up = s_up + bias
             s = jnp.where(seen_upper, s_up, s2[WIN:, lanes])
             dp = jnp.where(seen_upper, dp2[:WIN, lanes], dp2[WIN:, lanes])
-            l_h, ds_h, sink_h = one_head(s, dp, sinks[first + h], alive)
+            l_h, ds_h, sink_h = one_head(s, dp, sinks[pl.ds(first + h, 1), :], alive)
             cols = slice(h * WIN, (h + 1) * WIN)
             low[sub, :, cols] = l_h
             ds[sub, :, cols] = ds_h
@@ -112,9 +112,11 @@
     return copies
 
 
-def load_kernel(length, k_in, v_in, q_in, d_in, k_ref, v_ref, tail_ref, q_first, d_first, sems, first_sems):
+def load_kernel(length, sinks_in, k_in, v_in, q_in, d_in, k_ref, v_ref, tail_ref, q_first, d_first, sinks_ref, sinks, sems, first_sems, sink_sem):
     copies = [pltpu.make_async_copy(src, dst, sems.at[n]) for n, (src, dst) in enumerate(((k_in, k_ref), (v_in, v_ref)))]
     start_all(copies)
+    sinks_copy = pltpu.make_async_copy(sinks_in, sinks, sink_sem)
+    sinks_copy.start()
     firsts = columns_of(0, WIN, (q_in, d_in), (q_first, d_first), first_sems)
     c = lax.broadcasted_iota(jnp.int32, (WIN, 2 * WIN), 0)
     j = lax.broadcasted_iota(jnp.int32, (WIN, 2 * WIN), 1)
@@ -122,13 +124,14 @@
     for copy, ref, part in zip(copies, (k_ref, v_ref), range(2)):
         copy.wait()
         tail_ref[part] = mm(pick, ref[...], NN).astype(BF16)
+    sinks_copy.wait()
+    for h in range(HQ):
+        sinks_ref[pl.ds(h, 1), :] = jnp.full((1, WIN), sinks[h], F32)
     for copy in firsts:
         copy.wait()
 
 
-def late_kernel(length, sinks_in, k_ref, v_ref, q_first, d_first, q_in, d_in, q_early, d_early, q_last, d_last, low_out, ds_out, low_last, ds_last, sink_ref, q_ref, d_ref, low, ds, sinks, sems, early_sems, out_sems, sink_sem):
-    sinks_copy = pltpu.make_async_copy(sinks_in, sinks, sink_sem)
-    sinks_copy.start()
+def late_kernel(length, sinks, k_ref, v_ref, q_first, d_first, q_in, d_in, q_early, d_early, q_last, d_last, low_out, ds_out, low_last, ds_last, sink_ref, q_ref, d_ref, low, ds, sems, early_sems, out_sems):
     came = {g: columns_of(g, WIN, (q_in, d_in), (q_ref, d_ref), sems) for g in range(1, LAST)}
     cols = slice(LAST * GCOLS, HK * GCOLS)
     came[LAST] = [
@@ -143,7 +146,6 @@
     seen_upper = upper()
     alive = lax.broadcasted_iota(jnp.int32, (1, WIN), 1) < length[0, 0, 0] - WIN
     written = []
-    sinks_copy.wait()
     for g in range(HK):
         cols = slice(g * GCOLS, (g + 1) * GCOLS)
         kv = slice(g * HD, (g + 1) * HD)
@@ -164,25 +166,22 @@
         copy.wait()
 
 
-def early_kernel(parent, branch, level, sinks_in, q_ref, d_ref, k_ref, v_ref, lo, mid, hi, late_sink, low_out, ds_out, low_last, ds_last, keys_ref, sink_ref, sink_rows, low, ds, sinks, out_sems, sink_sem):
-    sinks_copy = pltpu.make_async_copy(sinks_in, sinks, sink_sem)
-    sinks_copy.start()
+def early_kernel(parent, branch, level, sinks, q_ref, d_ref, k_ref, v_ref, lo, mid, hi, late_sink, low_out, ds_out, low_last, ds_last, keys_ref, sink_ref, sink_rows, low, ds, out_sems):
     slot = parent[0, 0, 0] - branch[0] + 1
     bias = jnp.where(level[0] > 0, 0.0, LOW)
     seen_upper = upper()
     sink_rows[HQ:, :] = jnp.zeros((WIN - HQ, WIN), F32)
     written = []
     tail = jnp.where(slot == 0, lo[...], jnp.where(slot == 1, mid[...], hi[...]))
-    sinks_copy.wait()
     for g in range(HK):
         cols = slice(g * GCOLS, (g + 1) * GCOLS)
         kv = slice(g * HD, (g + 1) * HD)
         keys = jnp.concatenate([tail[0, :, kv], k_ref[:WIN, kv]], axis=0) * (HD**-0.5)
         values = jnp.concatenate([tail[1, :, kv], v_ref[:WIN, kv]], axis=0)
         keys_ref[:, kv] = keys
-        to = (g, low, ds) if g < LAST else (0, low_last, ds_last)
+        to = (g, low, ds) if g < FAR else (g - FAR, low_last, ds_last)
         forward_group(to[0], keys, values, q_ref[:, cols], d_ref[:, cols], seen_upper, sinks, g * GROUP, bias, None, to[1], to[2], sink_rows, g * GROUP)
-        if g < LAST:
+        if g < FAR:
             written += carried(g, (low, ds), (low_out, ds_out), out_sems)
     sink_rows[:HQ, :] = sink_rows[:HQ, :] + late_sink[...]
     total = -jnp.sum(sink_rows[...].T, axis=0, keepdims=True)
@@ -202,19 +201,19 @@
 
 
 def early_grads_kernel(parent, branch, q_ref, d_ref, keys_ref, low_last, ds_last, low_in, ds_in, dq_out, own_ref, tail_ref, dq_ref, low, ds, sems, in_sems):
-    came = [carried(g, (low_in, ds_in), (low, ds), in_sems) for g in range(LAST)]
+    came = [carried(g, (low_in, ds_in), (low, ds), in_sems) for g in range(FAR)]
     mask = upper_mask()
     flag = (parent[0, 0, 0] - branch[0] + 2).astype(F32)
     row = lax.broadcasted_iota(jnp.int32, (WIN, HD), 0)
     rows = slice(0, WIN)
     copies = []
-    for g in (LAST,) + tuple(range(LAST)):
+    for g in tuple(range(FAR, HK)) + tuple(range(FAR)):
         cols = slice(g * GCOLS, (g + 1) * GCOLS)
         kv = slice(g * HD, (g + 1) * HD)
-        if g < LAST:
+        if g < FAR:
             for copy in came[g]:
                 copy.wait()
-        low_g, ds_g = (low[g], ds[g]) if g < LAST else (low_last[0], ds_last[0])
+        low_g, ds_g = (low[g], ds[g]) if g < FAR else (low_last[g - FAR], ds_last[g - FAR])
         dq_ref[:, cols], dk, dv = one_side(keys_ref[:, kv], q_ref[:, cols], d_ref[:, cols], low_g, ds_g, mask)
         copies.append(pltpu.make_async_copy(dq_ref.at[:, cols], dq_out.at[rows, cols], sems.at[g]))
         copies[-1].start()
@@ -282,6 +281,9 @@
 LAST = HK - 1
 PACKED = (LAST, WIN, GROUP * WIN)
 PACKED_LAST = (1, WIN, GROUP * WIN)
+FAR = 3
+PACKED_FAR = (FAR, WIN, GROUP * WIN)
+PACKED_NEAR = (HK - FAR, WIN, GROUP * WIN)
 
 
 def shaped(shape, dtype):
@@ -320,21 +322,22 @@
     )(*operands)
 
 
-def load(length, k, v, q, d):
+def load(length, sinks, k, v, q, d):
     return call(
         load_kernel,
         "load",
-        [SMEM] + [HBM] * 4,
+        [SMEM] + [HBM] * 5,
         [
             (VMEM, (2 * WIN, KV), BF16),
             (VMEM, (2 * WIN, KV), BF16),
             (VMEM, (2, WIN, KV), BF16),
             (VMEM, (WIN, GCOLS), BF16),
             (VMEM, (WIN, GCOLS), BF16),
+            (VMEM, (HQ, WIN), F32),
         ],
-        [DMA((2,)), DMA((2,))],
+        [pltpu.SMEM((HQ,), F32), DMA((2,)), DMA((2,)), DMA],
         cost(1, 400_000),
-        length, k, v, q, d,
+        length, sinks, k, v, q, d,
     )
 
 
@@ -342,7 +345,7 @@
     return call(
         late_kernel,
         "late_rows",
-        [SMEM, HBM] + [VMEM] * 4 + [HBM] * 2,
+        [SMEM] + [VMEM] * 5 + [HBM] * 2,
         [
             (VMEM, (WIN, COLS), BF16),
             (VMEM, (WIN, COLS), BF16),
@@ -356,7 +359,7 @@
         ],
         [pltpu.VMEM((WIN, COLS), BF16)] * 2
         + [pltpu.VMEM(PACKED, BF16)] * 2
-        + [pltpu.SMEM((HQ,), F32), DMA((2 * HK,)), DMA((2,)), DMA((2 * HK,)), DMA],
+        + [DMA((2 * HK,)), DMA((2,)), DMA((2 * HK,))],
         cost(4, 2_500_000),
         length, sinks, k, v, q_first, d_first, q, d,
     )
@@ -366,22 +369,20 @@
     return call(
         early_kernel,
         "early_rows",
-        [SMEM] * 3 + [HBM] + [VMEM] * 8,
+        [SMEM] * 3 + [VMEM] * 9,
         [
-            (HBM, PACKED, BF16),
-            (HBM, PACKED, BF16),
-            (VMEM, PACKED_LAST, BF16),
-            (VMEM, PACKED_LAST, BF16),
+            (HBM, PACKED_FAR, BF16),
+            (HBM, PACKED_FAR, BF16),
+            (VMEM, PACKED_NEAR, BF16),
+            (VMEM, PACKED_NEAR, BF16),
             (VMEM, (2 * WIN, KV), BF16),
             (RESULT, (copies, WIN), F32),
         ],
         [
             pltpu.VMEM((WIN, WIN), F32),
-            pltpu.VMEM(PACKED, BF16),
-            pltpu.VMEM(PACKED, BF16),
-            pltpu.SMEM((HQ,), F32),
-            DMA((2 * HK,)),
-            DMA,
+            pltpu.VMEM(PACKED_FAR, BF16),
+            pltpu.VMEM(PACKED_FAR, BF16),
+            DMA((2 * FAR,)),
         ],
         cost(4, 5_000_000),
         parent, branch, level, sinks, q, d, k, v, lo, mid, hi, late_sink,
@@ -394,7 +395,7 @@
         "early_grads",
         [SMEM] * 2 + [VMEM] * 5 + [HBM] * 2,
         [(HBM, (2 * WIN, COLS), BF16), (VMEM, (2, WIN, KV), F32), (VMEM, (2, WIN, KV), BF16)],
-        [pltpu.VMEM((WIN, COLS), BF16), pltpu.VMEM(PACKED, BF16), pltpu.VMEM(PACKED, BF16), DMA((HK,)), DMA((2 * HK,))],
+        [pltpu.VMEM((WIN, COLS), BF16), pltpu.VMEM(PACKED_FAR, BF16), pltpu.VMEM(PACKED_FAR, BF16), DMA((HK,)), DMA((2 * FAR,))],
         SMALL,
         parent, branch, q, d, keys, low_last, ds_last, low, ds,
     )
@@ -440,12 +441,12 @@
     plane = lax.axis_size("dp") * lax.axis_size("ctx")
     experts = lax.axis_size("expert")
 
-    k, v, tail, q_first, d_first = load(segment_length, k, v, q, d)
-    tail, parent = lax.optimization_barrier((tail, parent_branch))
+    k, v, tail, q_first, d_first, sink_rows = load(segment_length, sink_logits, k, v, q, d)
     length = segment_length
     mid, lo, hi = (sent(tail, 1, by) for by in (0, 1, -1))
-    q_e, d_e, q_l3, d_l3, low_l, ds_l, low_l3, ds_l3, late_sink = late_rows(length, sink_logits, k, v, q_first, d_first, q, d)
-    low_e, ds_e, low_e3, ds_e3, keys, sinks = early_rows(parent, branch, level, sink_logits, q_e, d_e, k, v, lo, mid, hi, late_sink, experts)
+    q_e, d_e, q_l3, d_l3, low_l, ds_l, low_l3, ds_l3, late_sink = late_rows(length, sink_rows, k, v, q_first, d_first, q, d)
+    late_sink, parent = lax.optimization_barrier((late_sink, parent_branch))
+    low_e, ds_e, low_e3, ds_e3, keys, sinks = early_rows(parent, branch, level, sink_rows, q_e, d_e, k, v, lo, mid, hi, late_sink, experts)
 
     column = lax.all_to_all(sinks, "expert", 0, 0, tiled=True)
     dq, early_own, tail = early_grads(parent, branch, q_e, d_e, keys, low_e3, ds_e3, low_e, ds_e)

time: 65 us -> 63.9 us (0.983)
  Pallas kernels: 18.8 us -> 17.8 us
    pallas_call x6, Pallas kernels: 18.8 us -> 17.8 us  [call(): pl.pallas_call(kernel, in_specs=ins, out_specs=tuple((spec for spec, _, _...]
where the time goes in v5:
time: 63.9 us; the launch traced here: 63.5 us
  starting transfers between devices  37.3 us (58%)
  Pallas kernels  17.8 us (28%)
  waiting for transfers between devices  5.79 us (9%)
  between operations  2.08 us (3%)
    pallas_call x6, Pallas kernels, call(): pl.pallas_call(kernel, in_specs=ins, out_specs=tuple((spec for spec, _, _...  17.8 us
    all_to_all x1, starting transfers between devices, shards(): column = lax.all_to_all(sinks, 'expert', 0, 0, tiled=True)  15.4 us
    ppermute x6, starting transfers between devices, sent(): return lax.ppermute(rows, ('ctx', 'expert'), pairs)  15.2 us
    all_to_all x1, starting transfers between devices, shards(): lax.all_to_all(add_up(column, plane), ('dp', 'ctx'), 0, 0, tiled=True)  6.73 us
    all_to_all x1, waiting for transfers between devices, shards(): column = lax.all_to_all(sinks, 'expert', 0, 0, tiled=True)  4.14 us
    all_to_all x1, waiting for transfers between devices, shards(): lax.all_to_all(add_up(column, plane), ('dp', 'ctx'), 0, 0, tiled=True)  1.63 us
  transfers between devices with their start and end apart: 8, of which 2 were waited for; matrix products, arithmetic and copies ran while one was open for 0% of the time, Pallas kernels for 20%

profile of v5, /device:TPU:1, one launch (start us, length us, event | category | flops | bytes accessed | tf_op | source)
XLA Modules:
  0.0 63.5 jit_solution(11405228158529782400)
XLA Ops:
  1.3 1.3 %load.1 = (bf16[256,256]{1,0:T(8,128)(2,1)S(1)}, bf16[256,256]{1,0:T(8,128)(2,1)S(1)}, bf16[2,128,256]{2,1,0:T(8,128)(2,1)S(1)}, bf16[128,512]{1,0:T(8,128)(2,1)...) custom-call(s32[1,1,1]{2,1,0:T(1,128)S(6)} %copy.16.length, f32[32]{0:T(128)} %sinks_in.1, ...), custom_call_target="tpu_custom_call" | custom-call | flops 134217728 | bytes 400000 | tf_op jit(solution)/shard_map/load/pallas_call | solution.py:312
  2.6 4.5 %collective-permute-start.2 = (bf16[2,128,256]{2,1,0:T(8,128)(2,1)S(1)}, bf16[2,128,256]{2,1,0:T(8,128)(2,1)S(1)}, u32[]{:S(2)}, u32[]{:S(2)}) collective-permute-start(bf16[2,128,256]{2,1,0:T(8,128)(2,1)S(1)} %get-tuple-element.46), channel_id=1, source_target_pairs={{1,32},{2,33},{3,34},{4,35},{5,36},{6,37},{7,38},{8,39},{9,40},{10... | collective-permute-start | bytes 393224 | tf_op jit(solution)/shard_map/ppermute | solution.py:431
  7.1 3.1 %collective-permute-start.1 = (bf16[2,128,256]{2,1,0:T(8,128)(2,1)S(1)}, bf16[2,128,256]{2,1,0:T(8,128)(2,1)S(1)}, u32[]{:S(2)}, u32[]{:S(2)}) collective-permute-start(bf16[2,128,256]{2,1,0:T(8,128)(2,1)S(1)} %get-tuple-element.46), channel_id=1, source_target_pairs={{0,32},{1,33},{2,34},{3,35},{4,36},{5,37},{6,38},{7,39},{8,40},{9,... | collective-permute-start | bytes 393224 | tf_op jit(solution)/shard_map/ppermute | solution.py:431
  10.3 3.7 %collective-permute-start = (bf16[2,128,256]{2,1,0:T(8,128)(2,1)S(1)}, bf16[2,128,256]{2,1,0:T(8,128)(2,1)S(1)}, u32[]{:S(2)}, u32[]{:S(2)}) collective-permute-start(bf16[2,128,256]{2,1,0:T(8,128)(2,1)S(1)} %get-tuple-element.46), channel_id=1, source_target_pairs={{0,33},{1,34},{2,35},{3,36},{4,37},{5,38},{6,39},{7,40},{8,41},{9,... | collective-permute-start | bytes 393224 | tf_op jit(solution)/shard_map/ppermute | solution.py:431
  14.7 3.5 %late_rows.1 = (bf16[128,2048]{1,0:T(8,128)(2,1)S(1)}, bf16[128,2048]{1,0:T(8,128)(2,1)S(1)}, bf16[128,512]{1,0:T(8,128)(2,1)S(1)}, bf16[128,512]{1,0:T(8,128)(2...) custom-call(s32[1,1,1]{2,1,0:T(1,128)S(6)} %copy.16.length, ...), custom_call_target="tpu_custom_call" | custom-call | flops 536870912 | bytes 2500000 | tf_op jit(solution)/shard_map/late_rows/pallas_call | solution.py:312
  18.2 0.0 collective-permute-done.2.hi
  18.2 0.0 collective-permute-done.1.mid
  18.2 0.0 collective-permute-done.lo
  18.2 3.9 %early_rows.1 = (bf16[3,128,1024]{2,1,0:T(8,128)(2,1)}, bf16[3,128,1024]{2,1,0:T(8,128)(2,1)}, bf16[1,128,1024]{2,1,0:T(8,128)(2,1)S(1)}, bf16[1,128,1024]{2,1,0...) custom-call(s32[1,1,1]{2,1,0:T(1,128)S(6)} %copy.15.parent, s32[1]{0:T(128)} %bitcast.4.branch, ...), custom_call_target="tpu_custom_call" | custom-call | flops 536870912 | bytes 5000000 | tf_op jit(solution)/shard_map/early_rows/pallas_call | solution.py:312
  22.1 15.4 %all-to-all-start = ((f32[32,1,128]{2,1,0:T(1,128)}), f32[32,1,128]{2,1,0:T(1,128)S(1)}, u32[]{:S(2)}, u32[]{:S(2)}) async-start(f32[32,1,128]{2,1,0:T(1,128)} %bitcast.8), calls=%async_computation | async-start | bytes 32768 | tf_op jit(solution)/shard_map/all_to_all | solution.py:451
  37.5 3.7 %early_grads.1 = (bf16[256,2048]{1,0:T(8,128)(2,1)}, f32[2,128,256]{2,1,0:T(8,128)S(1)}, bf16[2,128,256]{2,1,0:T(8,128)(2,1)S(1)}) custom-call(s32[1,1,1]{2,1,0:T(1,128)S(6)} %copy.15.parent, s32[1]{0:T(128)} %bitcast.4.branch, bf16[128,2048]{1,0:T(8,128)(2,1)S(1)} %get-tuple-element.44.q_ref, bf16[128,2048]{1,0:T(8,128)(2,1)S(1)} %get-tuple-element.45.d_ref, ...), custom_call_target="tpu_custom_call" | custom-call | flops 1000 | bytes 1000 | tf_op jit(solution)/shard_map/early_grads/pallas_call | solution.py:312
  41.2 1.3 %collective-permute-start.5 = (bf16[2,128,256]{2,1,0:T(8,128)(2,1)S(1)}, bf16[2,128,256]{2,1,0:T(8,128)(2,1)S(1)}, u32[]{:S(2)}, u32[]{:S(2)}) collective-permute-start(bf16[2,128,256]{2,1,0:T(8,128)(2,1)S(1)} %get-tuple-element.54), channel_id=1, source_target_pairs={{33,0},{34,1},{35,2},{36,3},{37,4},{38,5},{39,6},{40,7},{41,8},{42... | collective-permute-start | bytes 393224 | tf_op jit(solution)/shard_map/ppermute | solution.py:431
  42.5 1.3 %collective-permute-start.4 = (bf16[2,128,256]{2,1,0:T(8,128)(2,1)S(1)}, bf16[2,128,256]{2,1,0:T(8,128)(2,1)S(1)}, u32[]{:S(2)}, u32[]{:S(2)}) collective-permute-start(bf16[2,128,256]{2,1,0:T(8,128)(2,1)S(1)} %get-tuple-element.54), channel_id=1, source_target_pairs={{32,0},{33,1},{34,2},{35,3},{36,4},{37,5},{38,6},{39,7},{40,8},{41... | collective-permute-start | bytes 393224 | tf_op jit(solution)/shard_map/ppermute | solution.py:431
  43.8 1.3 %collective-permute-start.3 = (bf16[2,128,256]{2,1,0:T(8,128)(2,1)S(1)}, bf16[2,128,256]{2,1,0:T(8,128)(2,1)S(1)}, u32[]{:S(2)}, u32[]{:S(2)}) collective-permute-start(bf16[2,128,256]{2,1,0:T(8,128)(2,1)S(1)} %get-tuple-element.54), channel_id=1, source_target_pairs={{32,1},{33,2},{34,3},{35,4},{36,5},{37,6},{38,7},{39,8},{40,9},{41... | collective-permute-start | bytes 393224 | tf_op jit(solution)/shard_map/ppermute | solution.py:431
  45.1 4.1 %all-to-all-done = f32[32,1,128]{2,1,0:T(1,128)S(1)} async-done(((f32[32,1,128]{2,1,0:T(1,128)}), f32[32,1,128]{2,1,0:T(1,128)S(1)}, u32[]{:S(2)}, u32[]{:S(2)}) %all-to-all-start) | async-done | bytes 16416 | tf_op jit(solution)/shard_map/all_to_all | solution.py:451
  49.2 0.6 add_up.1
  49.8 6.7 %all-to-all-start.1 = ((f32[16,1,128]{2,1,0:T(1,128)}), f32[16,1,128]{2,1,0:T(1,128)S(1)}, u32[]{:S(2)}, u32[]{:S(2)}) async-start(f32[16,1,128]{2,1,0:T(1,128)} %bitcast.11), calls=%async_computation.1 | async-start | bytes 16384 | tf_op jit(solution)/shard_map/all_to_all | solution.py:454
  56.6 0.0 collective-permute-done.5.hi
  56.6 0.0 collective-permute-done.4.mid
  56.6 0.0 collective-permute-done.3.lo
  56.6 4.7 %late_grads.1 = (bf16[256,2048]{1,0:T(8,128)(2,1)}, bf16[256,256]{1,0:T(8,128)(2,1)}, bf16[256,256]{1,0:T(8,128)(2,1)}) custom-call(s32[1,1,1]{2,1,0:T(1,128)S(6)} %copy.16.length, bf16[128,512]{1,0:T(8,128)(2,1)S(1)} %get-tuple-element.40.q_last, bf16[128,512]{1,0:T(8,128)(2,1)S(1)} %get-tuple-element.41.d_last, ...), custom_call_target="tpu_custom_call", output_to_operand_aliasing={{0}: (14, {})} | custom-call | flops 1000 | bytes 1000 | tf_op jit(solution)/shard_map/late_grads/pallas_call | solution.py:312
  61.3 1.6 %all-to-all-done.1 = f32[16,1,128]{2,1,0:T(1,128)S(1)} async-done(((f32[16,1,128]{2,1,0:T(1,128)}), f32[16,1,128]{2,1,0:T(1,128)S(1)}, u32[]{:S(2)}, u32[]{:S(2)}) %all-to-all-start.1) | async-done | bytes 8224 | tf_op jit(solution)/shard_map/all_to_all | solution.py:454
  63.0 0.5 reduce_sum.9
Async XLA Ops:
  2.6 15.5 %collective-permute-start.2 = (bf16[2,128,256]{2,1,0:T(8,128)(2,1)S(1)}, bf16[2,128,256]{2,1,0:T(8,128)(2,1)S(1)}, u32[]{:S(2)}, u32[]{:S(2)}) collective-permute-start(bf16[2,128,256]{2,1,0:T(8,128)(2,1)S(1)} %get-tuple-element.46), channel_id=1, source_target_pairs={{1,32},{2,33},{3,34},{4,35},{5,36},{6,37},{7,38},{8,39},{9,40},{10... | collective-permute-start | bytes 393224 | tf_op jit(solution)/shard_map/ppermute | solution.py:431
  7.1 11.0 %collective-permute-start.1 = (bf16[2,128,256]{2,1,0:T(8,128)(2,1)S(1)}, bf16[2,128,256]{2,1,0:T(8,128)(2,1)S(1)}, u32[]{:S(2)}, u32[]{:S(2)}) collective-permute-start(bf16[2,128,256]{2,1,0:T(8,128)(2,1)S(1)} %get-tuple-element.46), channel_id=1, source_target_pairs={{0,32},{1,33},{2,34},{3,35},{4,36},{5,37},{6,38},{7,39},{8,40},{9,... | collective-permute-start | bytes 393224 | tf_op jit(solution)/shard_map/ppermute | solution.py:431
  10.3 7.9 %collective-permute-start = (bf16[2,128,256]{2,1,0:T(8,128)(2,1)S(1)}, bf16[2,128,256]{2,1,0:T(8,128)(2,1)S(1)}, u32[]{:S(2)}, u32[]{:S(2)}) collective-permute-start(bf16[2,128,256]{2,1,0:T(8,128)(2,1)S(1)} %get-tuple-element.46), channel_id=1, source_target_pairs={{0,33},{1,34},{2,35},{3,36},{4,37},{5,38},{6,39},{7,40},{8,41},{9,... | collective-permute-start | bytes 393224 | tf_op jit(solution)/shard_map/ppermute | solution.py:431
  22.1 27.1 %all-to-all-start = ((f32[32,1,128]{2,1,0:T(1,128)}), f32[32,1,128]{2,1,0:T(1,128)S(1)}, u32[]{:S(2)}, u32[]{:S(2)}) async-start(f32[32,1,128]{2,1,0:T(1,128)} %bitcast.8), calls=%async_computation | async-start | bytes 32768 | tf_op jit(solution)/shard_map/all_to_all | solution.py:451
  41.2 15.4 %collective-permute-start.5 = (bf16[2,128,256]{2,1,0:T(8,128)(2,1)S(1)}, bf16[2,128,256]{2,1,0:T(8,128)(2,1)S(1)}, u32[]{:S(2)}, u32[]{:S(2)}) collective-permute-start(bf16[2,128,256]{2,1,0:T(8,128)(2,1)S(1)} %get-tuple-element.54), channel_id=1, source_target_pairs={{33,0},{34,1},{35,2},{36,3},{37,4},{38,5},{39,6},{40,7},{41,8},{42... | collective-permute-start | bytes 393224 | tf_op jit(solution)/shard_map/ppermute | solution.py:431
  42.5 14.1 %collective-permute-start.4 = (bf16[2,128,256]{2,1,0:T(8,128)(2,1)S(1)}, bf16[2,128,256]{2,1,0:T(8,128)(2,1)S(1)}, u32[]{:S(2)}, u32[]{:S(2)}) collective-permute-start(bf16[2,128,256]{2,1,0:T(8,128)(2,1)S(1)} %get-tuple-element.54), channel_id=1, source_target_pairs={{32,0},{33,1},{34,2},{35,3},{36,4},{37,5},{38,6},{39,7},{40,8},{41... | collective-permute-start | bytes 393224 | tf_op jit(solution)/shard_map/ppermute | solution.py:431
  43.8 12.8 %collective-permute-start.3 = (bf16[2,128,256]{2,1,0:T(8,128)(2,1)S(1)}, bf16[2,128,256]{2,1,0:T(8,128)(2,1)S(1)}, u32[]{:S(2)}, u32[]{:S(2)}) collective-permute-start(bf16[2,128,256]{2,1,0:T(8,128)(2,1)S(1)} %get-tuple-element.54), channel_id=1, source_target_pairs={{32,1},{33,2},{34,3},{35,4},{36,5},{37,6},{38,7},{39,8},{40,9},{41... | collective-permute-start | bytes 393224 | tf_op jit(solution)/shard_map/ppermute | solution.py:431
  49.8 13.1 %all-to-all-start.1 = ((f32[16,1,128]{2,1,0:T(1,128)}), f32[16,1,128]{2,1,0:T(1,128)S(1)}, u32[]{:S(2)}, u32[]{:S(2)}) async-start(f32[16,1,128]{2,1,0:T(1,128)} %bitcast.11), calls=%async_computation.1 | async-start | bytes 16384 | tf_op jit(solution)/shard_map/all_to_all | solution.py:454

commit v6 on v5

--- a/solution.py
+++ b/solution.py
@@ -190,14 +190,15 @@
         copy.wait()
 
 
-def one_side(keys, q, d, low, ds, mask):
+def one_side(keys, q, d, low, ds, mask, send):
     ds_up = ds * mask
     low_up = low * mask
     ds_all = jnp.concatenate([ds_up, ds - ds_up], axis=0)
     low_all = jnp.concatenate([low_up, low - low_up], axis=0)
+    send(query_side(keys, ds_all))
     dk = mm(ds_all, stacked(q), NN) * (HD**-0.5)
     dv = mm(low_all, stacked(d), NN)
-    return query_side(keys, ds_all), dk, dv
+    return dk, dv
 
 
 def early_grads_kernel(parent, branch, q_ref, d_ref, keys_ref, low_last, ds_last, low_in, ds_in, dq_out, own_ref, tail_ref, dq_ref, low, ds, sems, in_sems):
@@ -214,9 +215,13 @@
             for copy in came[g]:
                 copy.wait()
         low_g, ds_g = (low[g], ds[g]) if g < FAR else (low_last[g - FAR], ds_last[g - FAR])
-        dq_ref[:, cols], dk, dv = one_side(keys_ref[:, kv], q_ref[:, cols], d_ref[:, cols], low_g, ds_g, mask)
-        copies.append(pltpu.make_async_copy(dq_ref.at[:, cols], dq_out.at[rows, cols], sems.at[g]))
-        copies[-1].start()
+
+        def send(dq, g=g, cols=cols):
+            dq_ref[:, cols] = dq
+            copies.append(pltpu.make_async_copy(dq_ref.at[:, cols], dq_out.at[rows, cols], sems.at[g]))
+            copies[-1].start()
+
+        dk, dv = one_side(keys_ref[:, kv], q_ref[:, cols], d_ref[:, cols], low_g, ds_g, mask, send)
         tail_ref[0, :, kv] = jnp.where(row == 0, flag, dk[:WIN]).astype(BF16)
         tail_ref[1, :, kv] = dv[:WIN].astype(BF16)
         own_ref[0, :, kv] = dk[WIN:]
@@ -255,9 +260,13 @@
             q_g, d_g, low_g, ds_g = q_ref[:, cols], d_ref[:, cols], low[g], ds[g]
         else:
             q_g, d_g, low_g, ds_g = q_last[...], d_last[...], low_last[0], ds_last[0]
-        dq_ref[:, cols], dk, dv = one_side(k_ref[:, kv] * (HD**-0.5), q_g, d_g, low_g, ds_g, mask)
-        copies.append(pltpu.make_async_copy(dq_ref.at[:, cols], dq_out.at[rows, cols], sems.at[g]))
-        copies[-1].start()
+
+        def send(dq, g=g, cols=cols):
+            dq_ref[:, cols] = dq
+            copies.append(pltpu.make_async_copy(dq_ref.at[:, cols], dq_out.at[rows, cols], sems.at[g]))
+            copies[-1].start()
+
+        dk, dv = one_side(k_ref[:, kv] * (HD**-0.5), q_g, d_g, low_g, ds_g, mask, send)
         for part, (late, out) in enumerate(((dk, dk_ref), (dv, dv_ref))):
             total = late + sums[part][:, kv]
             out[:WIN, kv] = (total[:WIN] + own[part, :, kv]).astype(BF16)

time: 63.9 us -> 64.1 us (level)
  no operation moved by 1% of the time
where the time goes in v6:
time: 64.1 us; the launch traced here: 63.7 us
  starting transfers between devices  37.5 us (59%)
  Pallas kernels  18 us (28%)
  waiting for transfers between devices  5.53 us (9%)
  between operations  2.08 us (3%)
    pallas_call x6, Pallas kernels, call(): pl.pallas_call(kernel, in_specs=ins, out_specs=tuple((spec for spec, _, _...  18 us
    all_to_all x1, starting transfers between devices, shards(): column = lax.all_to_all(sinks, 'expert', 0, 0, tiled=True)  15.4 us
    ppermute x6, starting transfers between devices, sent(): return lax.ppermute(rows, ('ctx', 'expert'), pairs)  15.2 us
    all_to_all x1, starting transfers between devices, shards(): lax.all_to_all(add_up(column, plane), ('dp', 'ctx'), 0, 0, tiled=True)  6.91 us
    all_to_all x1, waiting for transfers between devices, shards(): column = lax.all_to_all(sinks, 'expert', 0, 0, tiled=True)  3.97 us
    all_to_all x1, waiting for transfers between devices, shards(): lax.all_to_all(add_up(column, plane), ('dp', 'ctx'), 0, 0, tiled=True)  1.55 us
  transfers between devices with their start and end apart: 8, of which 2 were waited for; matrix products, arithmetic and copies ran while one was open for 0% of the time, Pallas kernels for 20%

profile of v6, /device:TPU:1, one launch (start us, length us, event | category | flops | bytes accessed | tf_op | source)
XLA Modules:
  0.0 63.7 jit_solution(11331097231237213248)
XLA Ops:
  1.3 1.3 %load.1 = (bf16[256,256]{1,0:T(8,128)(2,1)S(1)}, bf16[256,256]{1,0:T(8,128)(2,1)S(1)}, bf16[2,128,256]{2,1,0:T(8,128)(2,1)S(1)}, bf16[128,512]{1,0:T(8,128)(2,1)...) custom-call(s32[1,1,1]{2,1,0:T(1,128)S(6)} %copy.16.length, f32[32]{0:T(128)} %sinks_in.1, ...), custom_call_target="tpu_custom_call" | custom-call | flops 134217728 | bytes 400000 | tf_op jit(solution)/shard_map/load/pallas_call | solution.py:321
  2.6 4.5 %collective-permute-start.2 = (bf16[2,128,256]{2,1,0:T(8,128)(2,1)S(1)}, bf16[2,128,256]{2,1,0:T(8,128)(2,1)S(1)}, u32[]{:S(2)}, u32[]{:S(2)}) collective-permute-start(bf16[2,128,256]{2,1,0:T(8,128)(2,1)S(1)} %get-tuple-element.46), channel_id=1, source_target_pairs={{1,32},{2,33},{3,34},{4,35},{5,36},{6,37},{7,38},{8,39},{9,40},{10... | collective-permute-start | bytes 393224 | tf_op jit(solution)/shard_map/ppermute | solution.py:440
  7.1 3.1 %collective-permute-start.1 = (bf16[2,128,256]{2,1,0:T(8,128)(2,1)S(1)}, bf16[2,128,256]{2,1,0:T(8,128)(2,1)S(1)}, u32[]{:S(2)}, u32[]{:S(2)}) collective-permute-start(bf16[2,128,256]{2,1,0:T(8,128)(2,1)S(1)} %get-tuple-element.46), channel_id=1, source_target_pairs={{0,32},{1,33},{2,34},{3,35},{4,36},{5,37},{6,38},{7,39},{8,40},{9,... | collective-permute-start | bytes 393224 | tf_op jit(solution)/shard_map/ppermute | solution.py:440
  10.3 3.7 %collective-permute-start = (bf16[2,128,256]{2,1,0:T(8,128)(2,1)S(1)}, bf16[2,128,256]{2,1,0:T(8,128)(2,1)S(1)}, u32[]{:S(2)}, u32[]{:S(2)}) collective-permute-start(bf16[2,128,256]{2,1,0:T(8,128)(2,1)S(1)} %get-tuple-element.46), channel_id=1, source_target_pairs={{0,33},{1,34},{2,35},{3,36},{4,37},{5,38},{6,39},{7,40},{8,41},{9,... | collective-permute-start | bytes 393224 | tf_op jit(solution)/shard_map/ppermute | solution.py:440
  14.7 3.5 %late_rows.1 = (bf16[128,2048]{1,0:T(8,128)(2,1)S(1)}, bf16[128,2048]{1,0:T(8,128)(2,1)S(1)}, bf16[128,512]{1,0:T(8,128)(2,1)S(1)}, bf16[128,512]{1,0:T(8,128)(2...) custom-call(s32[1,1,1]{2,1,0:T(1,128)S(6)} %copy.16.length, ...), custom_call_target="tpu_custom_call" | custom-call | flops 536870912 | bytes 2500000 | tf_op jit(solution)/shard_map/late_rows/pallas_call | solution.py:321
  18.2 0.0 collective-permute-done.2.hi
  18.2 0.0 collective-permute-done.1.mid
  18.2 0.0 collective-permute-done.lo
  18.2 3.9 %early_rows.1 = (bf16[3,128,1024]{2,1,0:T(8,128)(2,1)}, bf16[3,128,1024]{2,1,0:T(8,128)(2,1)}, bf16[1,128,1024]{2,1,0:T(8,128)(2,1)S(1)}, bf16[1,128,1024]{2,1,0...) custom-call(s32[1,1,1]{2,1,0:T(1,128)S(6)} %copy.15.parent, s32[1]{0:T(128)} %bitcast.4.branch, ...), custom_call_target="tpu_custom_call" | custom-call | flops 536870912 | bytes 5000000 | tf_op jit(solution)/shard_map/early_rows/pallas_call | solution.py:321
  22.1 15.4 %all-to-all-start = ((f32[32,1,128]{2,1,0:T(1,128)}), f32[32,1,128]{2,1,0:T(1,128)S(1)}, u32[]{:S(2)}, u32[]{:S(2)}) async-start(f32[32,1,128]{2,1,0:T(1,128)} %bitcast.8), calls=%async_computation | async-start | bytes 32768 | tf_op jit(solution)/shard_map/all_to_all | solution.py:460
  37.5 3.8 %early_grads.1 = (bf16[256,2048]{1,0:T(8,128)(2,1)}, f32[2,128,256]{2,1,0:T(8,128)S(1)}, bf16[2,128,256]{2,1,0:T(8,128)(2,1)S(1)}) custom-call(s32[1,1,1]{2,1,0:T(1,128)S(6)} %copy.15.parent, s32[1]{0:T(128)} %bitcast.4.branch, bf16[128,2048]{1,0:T(8,128)(2,1)S(1)} %get-tuple-element.44.q_ref, bf16[128,2048]{1,0:T(8,128)(2,1)S(1)} %get-tuple-element.45.d_ref, ...), custom_call_target="tpu_custom_call" | custom-call | flops 1000 | bytes 1000 | tf_op jit(solution)/shard_map/early_grads/pallas_call | solution.py:321
  41.4 1.3 %collective-permute-start.5 = (bf16[2,128,256]{2,1,0:T(8,128)(2,1)S(1)}, bf16[2,128,256]{2,1,0:T(8,128)(2,1)S(1)}, u32[]{:S(2)}, u32[]{:S(2)}) collective-permute-start(bf16[2,128,256]{2,1,0:T(8,128)(2,1)S(1)} %get-tuple-element.54), channel_id=1, source_target_pairs={{33,0},{34,1},{35,2},{36,3},{37,4},{38,5},{39,6},{40,7},{41,8},{42... | collective-permute-start | bytes 393224 | tf_op jit(solution)/shard_map/ppermute | solution.py:440
  42.7 1.3 %collective-permute-start.4 = (bf16[2,128,256]{2,1,0:T(8,128)(2,1)S(1)}, bf16[2,128,256]{2,1,0:T(8,128)(2,1)S(1)}, u32[]{:S(2)}, u32[]{:S(2)}) collective-permute-start(bf16[2,128,256]{2,1,0:T(8,128)(2,1)S(1)} %get-tuple-element.54), channel_id=1, source_target_pairs={{32,0},{33,1},{34,2},{35,3},{36,4},{37,5},{38,6},{39,7},{40,8},{41... | collective-permute-start | bytes 393224 | tf_op jit(solution)/shard_map/ppermute | solution.py:440
  44.0 1.3 %collective-permute-start.3 = (bf16[2,128,256]{2,1,0:T(8,128)(2,1)S(1)}, bf16[2,128,256]{2,1,0:T(8,128)(2,1)S(1)}, u32[]{:S(2)}, u32[]{:S(2)}) collective-permute-start(bf16[2,128,256]{2,1,0:T(8,128)(2,1)S(1)} %get-tuple-element.54), channel_id=1, source_target_pairs={{32,1},{33,2},{34,3},{35,4},{36,5},{37,6},{38,7},{39,8},{40,9},{41... | collective-permute-start | bytes 393224 | tf_op jit(solution)/shard_map/ppermute | solution.py:440
  45.3 4.0 %all-to-all-done = f32[32,1,128]{2,1,0:T(1,128)S(1)} async-done(((f32[32,1,128]{2,1,0:T(1,128)}), f32[32,1,128]{2,1,0:T(1,128)S(1)}, u32[]{:S(2)}, u32[]{:S(2)}) %all-to-all-start) | async-done | bytes 16416 | tf_op jit(solution)/shard_map/all_to_all | solution.py:460
  49.2 0.6 add_up.1
  49.8 6.9 %all-to-all-start.1 = ((f32[16,1,128]{2,1,0:T(1,128)}), f32[16,1,128]{2,1,0:T(1,128)S(1)}, u32[]{:S(2)}, u32[]{:S(2)}) async-start(f32[16,1,128]{2,1,0:T(1,128)} %bitcast.11), calls=%async_computation.1 | async-start | bytes 16384 | tf_op jit(solution)/shard_map/all_to_all | solution.py:463
  56.7 0.0 collective-permute-done.5.hi
  56.8 0.0 collective-permute-done.4.mid
  56.8 0.0 collective-permute-done.3.lo
  56.8 4.8 %late_grads.1 = (bf16[256,2048]{1,0:T(8,128)(2,1)}, bf16[256,256]{1,0:T(8,128)(2,1)}, bf16[256,256]{1,0:T(8,128)(2,1)}) custom-call(s32[1,1,1]{2,1,0:T(1,128)S(6)} %copy.16.length, bf16[128,512]{1,0:T(8,128)(2,1)S(1)} %get-tuple-element.40.q_last, bf16[128,512]{1,0:T(8,128)(2,1)S(1)} %get-tuple-element.41.d_last, ...), custom_call_target="tpu_custom_call", output_to_operand_aliasing={{0}: (14, {})} | custom-call | flops 1000 | bytes 1000 | tf_op jit(solution)/shard_map/late_grads/pallas_call | solution.py:321
  61.6 1.6 %all-to-all-done.1 = f32[16,1,128]{2,1,0:T(1,128)S(1)} async-done(((f32[16,1,128]{2,1,0:T(1,128)}), f32[16,1,128]{2,1,0:T(1,128)S(1)}, u32[]{:S(2)}, u32[]{:S(2)}) %all-to-all-start.1) | async-done | bytes 8224 | tf_op jit(solution)/shard_map/all_to_all | solution.py:463
  63.1 0.5 reduce_sum.9
Async XLA Ops:
  2.6 15.5 %collective-permute-start.2 = (bf16[2,128,256]{2,1,0:T(8,128)(2,1)S(1)}, bf16[2,128,256]{2,1,0:T(8,128)(2,1)S(1)}, u32[]{:S(2)}, u32[]{:S(2)}) collective-permute-start(bf16[2,128,256]{2,1,0:T(8,128)(2,1)S(1)} %get-tuple-element.46), channel_id=1, source_target_pairs={{1,32},{2,33},{3,34},{4,35},{5,36},{6,37},{7,38},{8,39},{9,40},{10... | collective-permute-start | bytes 393224 | tf_op jit(solution)/shard_map/ppermute | solution.py:440
  7.1 11.0 %collective-permute-start.1 = (bf16[2,128,256]{2,1,0:T(8,128)(2,1)S(1)}, bf16[2,128,256]{2,1,0:T(8,128)(2,1)S(1)}, u32[]{:S(2)}, u32[]{:S(2)}) collective-permute-start(bf16[2,128,256]{2,1,0:T(8,128)(2,1)S(1)} %get-tuple-element.46), channel_id=1, source_target_pairs={{0,32},{1,33},{2,34},{3,35},{4,36},{5,37},{6,38},{7,39},{8,40},{9,... | collective-permute-start | bytes 393224 | tf_op jit(solution)/shard_map/ppermute | solution.py:440
  10.3 7.9 %collective-permute-start = (bf16[2,128,256]{2,1,0:T(8,128)(2,1)S(1)}, bf16[2,128,256]{2,1,0:T(8,128)(2,1)S(1)}, u32[]{:S(2)}, u32[]{:S(2)}) collective-permute-start(bf16[2,128,256]{2,1,0:T(8,128)(2,1)S(1)} %get-tuple-element.46), channel_id=1, source_target_pairs={{0,33},{1,34},{2,35},{3,36},{4,37},{5,38},{6,39},{7,40},{8,41},{9,... | collective-permute-start | bytes 393224 | tf_op jit(solution)/shard_map/ppermute | solution.py:440
  22.1 27.1 %all-to-all-start = ((f32[32,1,128]{2,1,0:T(1,128)}), f32[32,1,128]{2,1,0:T(1,128)S(1)}, u32[]{:S(2)}, u32[]{:S(2)}) async-start(f32[32,1,128]{2,1,0:T(1,128)} %bitcast.8), calls=%async_computation | async-start | bytes 32768 | tf_op jit(solution)/shard_map/all_to_all | solution.py:460
  41.4 15.4 %collective-permute-start.5 = (bf16[2,128,256]{2,1,0:T(8,128)(2,1)S(1)}, bf16[2,128,256]{2,1,0:T(8,128)(2,1)S(1)}, u32[]{:S(2)}, u32[]{:S(2)}) collective-permute-start(bf16[2,128,256]{2,1,0:T(8,128)(2,1)S(1)} %get-tuple-element.54), channel_id=1, source_target_pairs={{33,0},{34,1},{35,2},{36,3},{37,4},{38,5},{39,6},{40,7},{41,8},{42... | collective-permute-start | bytes 393224 | tf_op jit(solution)/shard_map/ppermute | solution.py:440
  42.7 14.1 %collective-permute-start.4 = (bf16[2,128,256]{2,1,0:T(8,128)(2,1)S(1)}, bf16[2,128,256]{2,1,0:T(8,128)(2,1)S(1)}, u32[]{:S(2)}, u32[]{:S(2)}) collective-permute-start(bf16[2,128,256]{2,1,0:T(8,128)(2,1)S(1)} %get-tuple-element.54), channel_id=1, source_target_pairs={{32,0},{33,1},{34,2},{35,3},{36,4},{37,5},{38,6},{39,7},{40,8},{41... | collective-permute-start | bytes 393224 | tf_op jit(solution)/shard_map/ppermute | solution.py:440
  44.0 12.8 %collective-permute-start.3 = (bf16[2,128,256]{2,1,0:T(8,128)(2,1)S(1)}, bf16[2,128,256]{2,1,0:T(8,128)(2,1)S(1)}, u32[]{:S(2)}, u32[]{:S(2)}) collective-permute-start(bf16[2,128,256]{2,1,0:T(8,128)(2,1)S(1)} %get-tuple-element.54), channel_id=1, source_target_pairs={{32,1},{33,2},{34,3},{35,4},{36,5},{37,6},{38,7},{39,8},{40,9},{41... | collective-permute-start | bytes 393224 | tf_op jit(solution)/shard_map/ppermute | solution.py:440
  49.8 13.3 %all-to-all-start.1 = ((f32[16,1,128]{2,1,0:T(1,128)}), f32[16,1,128]{2,1,0:T(1,128)S(1)}, u32[]{:S(2)}, u32[]{:S(2)}) async-start(f32[16,1,128]{2,1,0:T(1,128)} %bitcast.11), calls=%async_computation.1 | async-start | bytes 16384 | tf_op jit(solution)/shard_map/all_to_all | solution.py:463
